TPU v7x, 512 devices: a whole 4x4x16 slice. The times are simulated.
512 devices in a mesh: group: 4 (over y), expert: 32 (over x_hi, z), tensor: 4 (over x_lo, core).
Axes of the slice: x: 4 (x_hi: 2, x_lo: 2; x = x_hi * 2 + x_lo), y: 4, z: 16, core: 2. Of those that a mesh axis runs over, the one named last changes fastest.
Arguments:
- weights: bfloat16 [32, 3584, 1024], P(None, ('group', 'expert'), 'tensor'), may hold values from -0.09375 to 0.09375
- gradients: bfloat16 [32, 3584, 1024], P(None, ('group', 'expert'), 'tensor'), may hold values from -6 to 6
- moment_one: float32 [32, 3584, 1024], P(None, ('group', 'expert'), 'tensor'), may hold values from -4 to 4
- moment_two: float32 [32, 3584, 1024], P(None, ('group', 'expert'), 'tensor'), may hold values from 0.1 to 4
- hidden_in: bfloat16 [4, 512, 3584], P(None, ('group', 'expert', 'tensor')), may hold values from -6 to 6
- query_latent: bfloat16 [4, 512, 16384], P(None, ('group', 'expert', 'tensor')), may hold values from -16 to 16
- query_rope: bfloat16 [4, 512, 2048], P(None, ('group', 'expert', 'tensor')), may hold values from -6 to 6
- cache_latent: bfloat16 [512, 256, 512], P(('group', 'expert', 'tensor')), may hold values from -8 to 8
- cache_rope: bfloat16 [512, 64, 256], P(('group', 'expert', 'tensor')), may hold values from -6 to 6
- new_latent: bfloat16 [4, 512, 512], P(None, ('group', 'expert', 'tensor')), may hold values from -6 to 6
- new_rope: bfloat16 [4, 512, 64], P(None, ('group', 'expert', 'tensor')), may hold values from -6 to 6
- lengths: int32 [512], P(('group', 'expert', 'tensor')), may hold values from 64 to 256, as said below
- expert_ids: int32 [4, 512, 8], P(None, ('group', 'expert')), may hold values from 0 to 31, all different within a row; in each aligned block of 4 rows (0 to 3, 4 to 7, ..., all dimensions but the last counted through in order) at most 2 rows name the same one
- router: bfloat16 [512, 32], replicated, may hold values from -0.5 to 0.5
Outputs:
- moment_one_new: float32 [32, 3584, 1024], P(None, ('group', 'expert'), 'tensor')
- moment_two_new: float32 [32, 3584, 1024], P(None, ('group', 'expert'), 'tensor')
- attention_out: bfloat16 [4, 512, 16384], P(None, ('group', 'expert', 'tensor'))
- expert_out: bfloat16 [4, 512, 1024], P(None, ('group', 'expert'), 'tensor')
Inputs may be any that keep to these rules, and one draw needn't show every extreme that they name: `lengths`: each row holds between 64 and 256 filled slots; the first row holds 256. `expert_ids`: within a step, in each aligned block of 4 rows, no expert is chosen by more than 2 rows.
All inputs are finite; a program needn't handle non-finite values.
Results may differ from a plain program's by a relative error of at most 0.0059.
Values may be sent and summed in bfloat16 or wider, within the bound.
No kernel may reach another device: no remote copies, remote signals or barrier semaphores. Data moves between devices by JAX's collectives and lax.ppermute only.
A program may use at most 64 MiB of HBM per device.

v0:
```python
import jax
import jax.numpy as jnp
from jax import lax
from jax.sharding import PartitionSpec as P

EXPERTS = 32
HEADS = 32
LAT = 512
ROPE = 64


BETA_ONE = 0.9
BETA_TWO = 0.95
LEARN_RATE = 0.005
WEIGHT_DECAY = 0.1
ADAM_EPS = 1e-08
BIAS_ONE = 1.0 - 0.9**10
BIAS_TWO = 1.0 - 0.95**10
QK_SCALE = 192.0 ** (-0.5)
ROUTE_SCALE = 2.827
NEGATIVE = -1e30


def adamw(weights, gradients, moment_one, moment_two):
    grad_wide = gradients.astype(jnp.float32)
    first_new = BETA_ONE * moment_one + (1.0 - BETA_ONE) * grad_wide
    second_new = BETA_TWO * moment_two + (1.0 - BETA_TWO) * grad_wide * grad_wide
    old_weight = weights.astype(jnp.float32)
    ratio = first_new / BIAS_ONE / (jnp.sqrt(second_new / BIAS_TWO) + ADAM_EPS)
    updated = (old_weight - LEARN_RATE * (ratio + WEIGHT_DECAY * old_weight)).astype(jnp.bfloat16)
    return (first_new, second_new, updated)


def attend(query_latent, query_rope, cache_latent, cache_rope, new_latent, new_rope, lengths):
    step_count, row_count = (query_latent.shape[0], query_latent.shape[1])
    slot_total = cache_latent.shape[1]
    query_lat = query_latent.reshape(step_count, row_count, HEADS, LAT)
    query_pos = query_rope.reshape(step_count, row_count, HEADS, ROPE)
    old_scores = (
        jnp.einsum("srhc,rlc->srhl", query_lat, cache_latent, preferred_element_type=jnp.float32)
        + jnp.einsum("srhp,rpl->srhl", query_pos, cache_rope, preferred_element_type=jnp.float32)
    ) * QK_SCALE
    new_scores = (
        jnp.einsum("srhc,trc->srht", query_lat, new_latent, preferred_element_type=jnp.float32)
        + jnp.einsum("srhp,trp->srht", query_pos, new_rope, preferred_element_type=jnp.float32)
    ) * QK_SCALE
    valid_old = jnp.arange(slot_total, dtype=jnp.int32)[None, :] < lengths[:, None]
    valid_new = jnp.arange(step_count)[None, :] <= jnp.arange(step_count)[:, None]
    old_scores = jnp.where(valid_old[None, :, None, :], old_scores, NEGATIVE)
    new_scores = jnp.where(valid_new[:, None, None, :], new_scores, NEGATIVE)
    peak_score = jnp.maximum(
        jnp.max(old_scores, -1, keepdims=True), jnp.max(new_scores, -1, keepdims=True)
    )
    old_mass = jnp.exp(old_scores - peak_score)
    new_mass = jnp.exp(new_scores - peak_score)
    total_mass = jnp.sum(old_mass, -1, keepdims=True) + jnp.sum(new_mass, -1, keepdims=True)
    old_prob = (old_mass / total_mass).astype(jnp.bfloat16)
    new_prob = (new_mass / total_mass).astype(jnp.bfloat16)
    mixture = jnp.einsum(
        "srhl,rlc->srhc", old_prob, cache_latent, preferred_element_type=jnp.float32
    ) + jnp.einsum("srht,trc->srhc", new_prob, new_latent, preferred_element_type=jnp.float32)
    summary = jnp.mean(mixture, 2)
    summary = summary * lax.rsqrt(jnp.mean(summary * summary, -1, keepdims=True) + 1e-05)
    attention_out = mixture.reshape(step_count, row_count, HEADS * LAT).astype(jnp.bfloat16)
    return (attention_out, summary.astype(jnp.bfloat16))


def move_weights(updated, expert_count, local_experts):
    slab_rows, columns = (updated.shape[1], updated.shape[2])
    collected = lax.all_gather(updated[:, None], "group", axis=1, tiled=True)
    group_count = collected.shape[1]
    shaped = collected.reshape(expert_count, local_experts, group_count, 1, slab_rows, columns)
    sorted_slab = lax.all_to_all(shaped, "expert", split_axis=0, concat_axis=3, tiled=True)
    sectioned = sorted_slab.reshape(local_experts, group_count * expert_count * slab_rows, columns)
    return sectioned


def local(
    weights,
    gradients,
    moment_one,
    moment_two,
    hidden_in,
    query_latent,
    query_rope,
    cache_latent,
    cache_rope,
    new_latent,
    new_rope,
    lengths,
    expert_ids,
    router,
):
    first_new, second_new, updated = adamw(weights, gradients, moment_one, moment_two)
    expert_count = lax.axis_size("expert")
    local_experts = updated.shape[0] // expert_count
    columns = updated.shape[2]
    attention_out, summary = attend(
        query_latent, query_rope, cache_latent, cache_rope, new_latent, new_rope, lengths
    )
    sectioned = move_weights(updated, expert_count, local_experts)
    rows_all, summary_all = (
        lax.all_gather(hidden_in, "tensor", axis=1, tiled=True),
        lax.all_gather(summary, "tensor", axis=1, tiled=True),
    )
    step_count, block_rows = (rows_all.shape[0], rows_all.shape[1])
    width = rows_all.shape[2]
    top_count = expert_ids.shape[2]
    slot_count = 2 * block_rows * top_count // EXPERTS
    logits = jnp.einsum("sbc,ce->sbe", summary_all, router, preferred_element_type=jnp.float32)
    gate_prob = jax.nn.sigmoid(logits)
    picked = (expert_ids[..., None] == jnp.arange(EXPERTS, dtype=jnp.int32)).astype(jnp.float32)
    chosen = jnp.sum(picked * gate_prob[:, :, None, :], -1)
    route_weight = (ROUTE_SCALE * chosen / jnp.sum(chosen, -1, keepdims=True)).astype(jnp.bfloat16)
    per_expert = jnp.sum(picked, 2)
    expert_weight = jnp.sum(picked * route_weight.astype(jnp.float32)[..., None], 2)
    earlier = jnp.cumsum(per_expert, 1) - per_expert
    slot_hit = (earlier[..., None] == jnp.arange(slot_count, dtype=jnp.float32)).astype(
        jnp.float32
    ) * per_expert[..., None]
    outgoing = jnp.einsum(
        "sbec,sbd->escd",
        slot_hit.astype(jnp.bfloat16),
        rows_all,
        preferred_element_type=jnp.float32,
    ).astype(jnp.bfloat16)
    outgoing = outgoing.reshape(expert_count, local_experts, step_count, slot_count, width)
    arrived = lax.all_to_all(outgoing, "expert", split_axis=0, concat_axis=0, tiled=True)
    pre_act = jnp.einsum("xjscd,jdf->xjscf", arrived, sectioned, preferred_element_type=jnp.float32)
    active = jax.nn.silu(pre_act).astype(jnp.bfloat16)
    returned = lax.all_to_all(active, "expert", split_axis=0, concat_axis=0, tiled=True)
    returned = returned.reshape(EXPERTS, step_count, slot_count, columns)
    combine = (slot_hit * expert_weight[..., None]).astype(jnp.bfloat16)
    expert_out = jnp.einsum(
        "sbec,escf->sbf", combine, returned, preferred_element_type=jnp.float32
    ).astype(jnp.bfloat16)
    return (first_new, second_new, attention_out, expert_out)


def solution(mesh):
    return jax.shard_map(
        local,
        mesh=mesh,
        in_specs=(
            P(None, ("group", "expert"), "tensor"),
            P(None, ("group", "expert"), "tensor"),
            P(None, ("group", "expert"), "tensor"),
            P(None, ("group", "expert"), "tensor"),
            P(None, ("group", "expert", "tensor"), None),
            P(None, ("group", "expert", "tensor"), None),
            P(None, ("group", "expert", "tensor"), None),
            P(("group", "expert", "tensor"), None, None),
            P(("group", "expert", "tensor"), None, None),
            P(None, ("group", "expert", "tensor"), None),
            P(None, ("group", "expert", "tensor"), None),
            P(("group", "expert", "tensor")),
            P(None, ("group", "expert"), None),
            P(),
        ),
        out_specs=(
            P(None, ("group", "expert"), "tensor"),
            P(None, ("group", "expert"), "tensor"),
            P(None, ("group", "expert", "tensor"), None),
            P(None, ("group", "expert"), "tensor"),
        ),
        check_vma=False,
    )
```

profile of v0, /device:TPU:2, one launch (start us, length us, event | category | flops | bytes accessed | tf_op | source)
XLA Modules:
  0.0 289.4 jit_solution(83562535180176250)
XLA Ops:
  7.2 3.8 %fusion.25 = (bf16[32,28,256]{2,0,1:T(8,128)(2,1)}, f32[32,28,256]{2,0,1:T(8,128)}, f32[32,28,256]{2,0,1:T(8,128)}) fusion(bf16[32,28,256]{2,0,1:T(8,128)(2,1)} %param.14, bf16[32,28,256]{2,0,1:T(8,128)(2,1)} %param.15, f32[32,28,256]{2,0,1:T(8,128)} %param.17, f32[32,28,256]{2,0,1:T(8,128)} %param.16), kind=kLoop, calls=%fused_computation.31 | loop fusion | flops 4128768 | bytes 5046272 | tf_op jit(solution)/shard_map/convert_element_type | solution.py:30
  11.0 41.0 %all-gather.3.cloned.1.call-done = bf16[32,112,256]{2,0,1:T(8,128)(2,1)} async-done(((bf16[32,28,256]{2,0,1:T(8,128)(2,1)}), bf16[32,112,256]{2,0,1:T(8,128)(2,1)}) %all-gather.3.cloned.1.call-update) | async-done | bytes 1835024 | tf_op jit(solution)/shard_map/all_gather | solution.py:70
  52.0 4.1 %copy.31 = bf16[32,1,4,1,28,256]{5,2,4,3,1,0:T(4,128)(2,1)} copy(bf16[32,1,4,1,28,256]{5,0,4,2,3,1:T(8,128)(2,1)} %bitcast.121) | data formatting | bytes 3670016 | tf_op jit(solution)/shard_map/reshape | solution.py:72
  56.2 14.2 %all-to-all-start = ((bf16[32,1,4,1,28,256]{5,2,4,3,1,0:T(4,128)(2,1)}), bf16[32,1,4,1,28,256]{5,2,4,3,1,0:T(4,128)(2,1)S(1)}, u32[]{:S(2)}, u32[]{:S(2)}) async-start(bf16[32,1,4,1,28,256]{5,2,4,3,1,0:T(4,128)(2,1)} %copy.31), calls=%async_computation | async-start | bytes 3670016 | tf_op jit(solution)/shard_map/all_to_all | solution.py:73
  71.1 0.1 reshape.215
  71.3 0.2 fusion.33
  71.5 0.2 fusion.73
  71.7 0.1 fusion.45
  71.8 0.3 fusion.72
  72.2 0.2 fusion.38
  72.4 0.2 fusion.61
  72.6 0.3 fusion.71
  72.9 0.1 multiply_reduce_fusion
  73.1 5.2 %all_gather.9 = bf16[4,4,512]{2,0,1:T(4,128)(2,1)S(1)} all-gather(bf16[4,1,512]{2,0,1:T(4,128)(2,1)S(1)} %fusion.50), channel_id=1, replica_groups=mesh['group'=4,'expert'=32,'tensor'=4] {'tensor'}, dimensions={1}, use_global_device_ids=true | all-gather | bytes 20480 | tf_op jit(solution)/shard_map/all_gather | solution.py:104
  78.3 0.1 fusion.20
  78.4 0.2 select_reduce_fusion
  78.7 0.1 select_reduce_fusion.2
  78.9 5.4 %all_gather.11 = bf16[4,4,3584]{2,0,1:T(4,128)(2,1)S(1)} all-gather(bf16[4,1,3584]{2,0,1:T(4,128)(2,1)S(1)} %copy-done.5), channel_id=1, replica_groups=mesh['group'=4,'expert'=32,'tensor'=4] {'tensor'}, dimensions={1}, use_global_device_ids=true | all-gather | bytes 143360 | tf_op jit(solution)/shard_map/all_gather | solution.py:103
  84.3 0.7 fusion
  85.0 3.1 %copy.34 = bf16[32,1,4,2,3584]{4,3,2,1,0:T(2,128)(2,1)} copy(bf16[32,1,4,2,3584]{4,0,3,2,1:T(8,128)(2,1)S(1)} %fusion) | data formatting | bytes 3670016 | tf_op jit(solution)/shard_map/reshape | solution.py:127
  88.2 66.5 %all-to-all-done = bf16[32,1,4,1,28,256]{5,2,4,3,1,0:T(4,128)(2,1)S(1)} async-done(((bf16[32,1,4,1,28,256]{5,2,4,3,1,0:T(4,128)(2,1)}), bf16[32,1,4,1,28,256]{5,2,4,3,1,0:T(4,128)(2,1)S(1)}, u32[]{:S(2)}, u32[]{:S(2)}) %all-to-all-start) | async-done | bytes 1835040 | tf_op jit(solution)/shard_map/all_to_all | solution.py:73
  154.6 1.3 copy-done.1
  155.9 10.0 %all-to-all-start.1 = ((bf16[32,1,4,2,3584]{4,3,2,1,0:T(2,128)(2,1)}), bf16[32,1,4,2,3584]{4,3,2,1,0:T(2,128)(2,1)}, u32[]{:S(2)}, u32[]{:S(2)}) async-start(bf16[32,1,4,2,3584]{4,3,2,1,0:T(2,128)(2,1)} %copy.34), calls=%async_computation.1 | async-start | bytes 3670016 | tf_op jit(solution)/shard_map/all_to_all | solution.py:128
  165.9 1.9 copy.32
  167.8 1.4 reshape.233
  169.2 80.8 %all-to-all-done.1 = bf16[32,1,4,2,3584]{4,3,2,1,0:T(2,128)(2,1)} async-done(((bf16[32,1,4,2,3584]{4,3,2,1,0:T(2,128)(2,1)}), bf16[32,1,4,2,3584]{4,3,2,1,0:T(2,128)(2,1)}, u32[]{:S(2)}, u32[]{:S(2)}) %all-to-all-start.1) | async-done | bytes 1835040 | tf_op jit(solution)/shard_map/all_to_all | solution.py:128
  250.0 2.8 multiply_convert_fusion
  252.8 0.8 copy.36
  253.6 9.8 %all-to-all-start.2 = ((bf16[32,1,4,2,256]{4,3,2,1,0:T(2,128)(2,1)}), bf16[32,1,4,2,256]{4,3,2,1,0:T(2,128)(2,1)S(1)}, u32[]{:S(2)}, u32[]{:S(2)}) async-start(bf16[32,1,4,2,256]{4,3,2,1,0:T(2,128)(2,1)} %copy.36), calls=%async_computation.2 | async-start | bytes 262144 | tf_op jit(solution)/shard_map/all_to_all | solution.py:131
  263.3 0.7 convert_element_type.80
  264.1 17.7 %all-to-all-done.2 = bf16[32,1,4,2,256]{4,3,2,1,0:T(2,128)(2,1)S(1)} async-done(((bf16[32,1,4,2,256]{4,3,2,1,0:T(2,128)(2,1)}), bf16[32,1,4,2,256]{4,3,2,1,0:T(2,128)(2,1)S(1)}, u32[]{:S(2)}, u32[]{:S(2)}) %all-to-all-start.2) | async-done | bytes 131104 | tf_op jit(solution)/shard_map/all_to_all | solution.py:131
  281.8 0.8 fusion.15
  (31 shorter events, 0.4 us)
Async XLA Ops:
  7.2 64.7 %copy-start = (bf16[1,256,512]{2,1,0:T(8,128)(2,1)S(1)}, bf16[1,256,512]{2,1,0:T(8,128)(2,1)}, u32[]{:S(2)}) copy-start(bf16[1,256,512]{2,1,0:T(8,128)(2,1)} %param.21) | copy-start | bytes 786436
  7.2 44.9 %all-gather.3.cloned.1.call-start = ((), (), s32[]{:S(2)}) async-start(), calls=%async_computation.3 | async-start | bytes 2293760 | tf_op jit(solution)/shard_map/all_gather | solution.py:70
  56.2 15.0 %copy-start.7 = (bf16[4,1,2048]{2,0,1:T(4,128)(2,1)S(1)}, bf16[4,1,2048]{2,0,1:T(4,128)(2,1)}, u32[]{:S(2)}) copy-start(bf16[4,1,2048]{2,0,1:T(4,128)(2,1)} %param.20) | copy-start | bytes 49156
  56.2 15.1 %copy-start.2 = (bf16[4,1,16384]{2,0,1:T(4,128)(2,1)S(1)}, bf16[4,1,16384]{2,0,1:T(4,128)(2,1)}, u32[]{:S(2)}) copy-start(bf16[4,1,16384]{2,0,1:T(4,128)(2,1)} %param.19) | copy-start | bytes 393220
  56.2 15.1 %copy-start.6 = (bf16[4,1,512]{2,0,1:T(4,128)(2,1)S(1)}, bf16[4,1,512]{2,0,1:T(4,128)(2,1)}, u32[]{:S(2)}) copy-start(bf16[4,1,512]{2,0,1:T(4,128)(2,1)} %param.23) | copy-start | bytes 12292
  56.2 15.3 %copy-start.9 = (bf16[4,1,64]{2,0,1:T(4,128)(2,1)S(1)}, bf16[4,1,64]{2,0,1:T(4,128)(2,1)}, u32[]{:S(2)}) copy-start(bf16[4,1,64]{2,0,1:T(4,128)(2,1)} %param.24) | copy-start | bytes 1540
  56.2 15.5 %copy-start.4 = (bf16[1,64,256]{2,1,0:T(8,128)(2,1)S(1)}, bf16[1,64,256]{2,1,0:T(8,128)(2,1)}, u32[]{:S(2)}) copy-start(bf16[1,64,256]{2,1,0:T(8,128)(2,1)} %param.22) | copy-start | bytes 98308
  56.2 98.4 %all-to-all-start = ((bf16[32,1,4,1,28,256]{5,2,4,3,1,0:T(4,128)(2,1)}), bf16[32,1,4,1,28,256]{5,2,4,3,1,0:T(4,128)(2,1)S(1)}, u32[]{:S(2)}, u32[]{:S(2)}) async-start(bf16[32,1,4,1,28,256]{5,2,4,3,1,0:T(4,128)(2,1)} %copy.31), calls=%async_computation | async-start | bytes 3670016 | tf_op jit(solution)/shard_map/all_to_all | solution.py:73
  70.4 7.8 %copy-start.8 = (bf16[512,32]{0,1:T(8,128)(2,1)S(1)}, bf16[512,32]{0,1:T(8,128)(2,1)}, u32[]{:S(2)}) copy-start(bf16[512,32]{0,1:T(8,128)(2,1)} %param.27) | copy-start | bytes 98308
  70.5 8.0 %copy-start.3 = (s32[4,4,8]{2,1,0:T(4,128)S(1)}, s32[4,4,8]{2,1,0:T(4,128)}, u32[]{:S(2)}) copy-start(s32[4,4,8]{2,1,0:T(4,128)} %param.26) | copy-start | bytes 1540
  70.5 8.4 %copy-start.5 = (bf16[4,1,3584]{2,0,1:T(4,128)(2,1)S(1)}, bf16[4,1,3584]{2,0,1:T(4,128)(2,1)}, u32[]{:S(2)}) copy-start(bf16[4,1,3584]{2,0,1:T(4,128)(2,1)} %param.18) | copy-start | bytes 86020
  154.6 1.3 copy-start.1
  155.9 94.1 %all-to-all-start.1 = ((bf16[32,1,4,2,3584]{4,3,2,1,0:T(2,128)(2,1)}), bf16[32,1,4,2,3584]{4,3,2,1,0:T(2,128)(2,1)}, u32[]{:S(2)}, u32[]{:S(2)}) async-start(bf16[32,1,4,2,3584]{4,3,2,1,0:T(2,128)(2,1)} %copy.34), calls=%async_computation.1 | async-start | bytes 3670016 | tf_op jit(solution)/shard_map/all_to_all | solution.py:128
  253.6 28.2 %all-to-all-start.2 = ((bf16[32,1,4,2,256]{4,3,2,1,0:T(2,128)(2,1)}), bf16[32,1,4,2,256]{4,3,2,1,0:T(2,128)(2,1)S(1)}, u32[]{:S(2)}, u32[]{:S(2)}) async-start(bf16[32,1,4,2,256]{4,3,2,1,0:T(2,128)(2,1)} %copy.36), calls=%async_computation.2 | async-start | bytes 262144 | tf_op jit(solution)/shard_map/all_to_all | solution.py:131
Sparse Core Ops, SparseCore 0:
  11.2 40.8 all-gather.2
where the time goes:
time: 290 us; the launch traced here: 289 us
  waiting for transfers between devices  206 us (71%)
  starting transfers between devices  34.1 us (12%)
  between operations  14.9 us (5%)
  local copies, waits for them, and re-layouts  13.5 us (5%)
  blocking collectives  10.6 us (4%)
  matrix products  5.76 us (2%)
  other arithmetic  4.68 us (2%)
    all_to_all x1, waiting for transfers between devices, local(): lax.all_to_all(outgoing, 'expert', split_axis=0, concat_axis=0, tiled=True)  80.8 us
    all_to_all x1, waiting for transfers between devices, move_weights(): lax.all_to_all(shaped, 'expert', split_axis=0, concat_axis=3, tiled=True)  66.5 us
    all_gather x1, waiting for transfers between devices, move_weights(): collected = lax.all_gather(updated[:, None], 'group', axis=1, tiled=True)  41 us
    all_to_all x1, waiting for transfers between devices, local(): lax.all_to_all(active, 'expert', split_axis=0, concat_axis=0, tiled=True)  17.7 us
    all_to_all x1, starting transfers between devices, move_weights(): lax.all_to_all(shaped, 'expert', split_axis=0, concat_axis=3, tiled=True)  14.2 us
    all_to_all x1, starting transfers between devices, local(): lax.all_to_all(outgoing, 'expert', split_axis=0, concat_axis=0, tiled=True)  10 us
    all_to_all x1, starting transfers between devices, local(): lax.all_to_all(active, 'expert', split_axis=0, concat_axis=0, tiled=True)  9.77 us
  transfers between devices with their start and end apart: 4, of which 4 were waited for; matrix products, arithmetic and copies ran while one was open for 4% of the time, Pallas kernels for 0%

commit v1 on v0

--- a/solution.py
+++ b/solution.py
@@ -65,14 +65,9 @@
     return (attention_out, summary.astype(jnp.bfloat16))
 
 
-def move_weights(updated, expert_count, local_experts):
-    slab_rows, columns = (updated.shape[1], updated.shape[2])
-    collected = lax.all_gather(updated[:, None], "group", axis=1, tiled=True)
-    group_count = collected.shape[1]
-    shaped = collected.reshape(expert_count, local_experts, group_count, 1, slab_rows, columns)
-    sorted_slab = lax.all_to_all(shaped, "expert", split_axis=0, concat_axis=3, tiled=True)
-    sectioned = sorted_slab.reshape(local_experts, group_count * expert_count * slab_rows, columns)
-    return sectioned
+def flip(value, axis, distance):
+    size = lax.axis_size(axis)
+    return lax.ppermute(value, axis, [(i, i ^ distance) for i in range(size)])
 
 
 def local(
@@ -92,45 +87,63 @@
     router,
 ):
     first_new, second_new, updated = adamw(weights, gradients, moment_one, moment_two)
-    expert_count = lax.axis_size("expert")
-    local_experts = updated.shape[0] // expert_count
-    columns = updated.shape[2]
+    expert_count, slab, columns = updated.shape
     attention_out, summary = attend(
         query_latent, query_rope, cache_latent, cache_rope, new_latent, new_rope, lengths
     )
-    sectioned = move_weights(updated, expert_count, local_experts)
-    rows_all, summary_all = (
-        lax.all_gather(hidden_in, "tensor", axis=1, tiled=True),
-        lax.all_gather(summary, "tensor", axis=1, tiled=True),
-    )
-    step_count, block_rows = (rows_all.shape[0], rows_all.shape[1])
-    width = rows_all.shape[2]
-    top_count = expert_ids.shape[2]
-    slot_count = 2 * block_rows * top_count // EXPERTS
-    logits = jnp.einsum("sbc,ce->sbe", summary_all, router, preferred_element_type=jnp.float32)
-    gate_prob = jax.nn.sigmoid(logits)
+    step_count, _, width = hidden_in.shape
+    quarter = width // 4
+    group, tensor = lax.axis_index("group"), lax.axis_index("tensor")
+    rows_all = lax.all_gather(hidden_in, "tensor", axis=1, tiled=True)
+    block_rows = rows_all.shape[1]
+    slot_count = 2
+    places = step_count * slot_count
+
     picked = (expert_ids[..., None] == jnp.arange(EXPERTS, dtype=jnp.int32)).astype(jnp.float32)
-    chosen = jnp.sum(picked * gate_prob[:, :, None, :], -1)
-    route_weight = (ROUTE_SCALE * chosen / jnp.sum(chosen, -1, keepdims=True)).astype(jnp.bfloat16)
     per_expert = jnp.sum(picked, 2)
-    expert_weight = jnp.sum(picked * route_weight.astype(jnp.float32)[..., None], 2)
     earlier = jnp.cumsum(per_expert, 1) - per_expert
     slot_hit = (earlier[..., None] == jnp.arange(slot_count, dtype=jnp.float32)).astype(
         jnp.float32
     ) * per_expert[..., None]
+    my_part = lax.dynamic_slice_in_dim(rows_all, tensor * quarter, quarter, 2)
     outgoing = jnp.einsum(
         "sbec,sbd->escd",
         slot_hit.astype(jnp.bfloat16),
-        rows_all,
+        my_part,
         preferred_element_type=jnp.float32,
     ).astype(jnp.bfloat16)
-    outgoing = outgoing.reshape(expert_count, local_experts, step_count, slot_count, width)
-    arrived = lax.all_to_all(outgoing, "expert", split_axis=0, concat_axis=0, tiled=True)
-    pre_act = jnp.einsum("xjscd,jdf->xjscf", arrived, sectioned, preferred_element_type=jnp.float32)
+    outgoing = outgoing.reshape(expert_count, places * quarter // 128, 128)
+    slabs = jnp.swapaxes(updated.reshape(expert_count, slab, 2, 128), 1, 2)
+    slabs = slabs.reshape(expert_count, 2 * slab, 128)
+    payload = jnp.concatenate([slabs, outgoing], 1)
+    arrived = lax.all_to_all(payload, "expert", split_axis=0, concat_axis=0, tiled=True)
+    held = jnp.swapaxes(arrived[:, : 2 * slab].reshape(expert_count, 2, slab, 128), 1, 2)
+    held = held.reshape(expert_count * slab, columns)
+    rows_in = arrived[:, 2 * slab :].reshape(expert_count * places, quarter)
+
+    held_other = [flip(held, "group", k) for k in (1, 3, 2)]
+    rows_far = flip(rows_in, "tensor", 2)
+    rows_core = flip(rows_in, "tensor", 1)
+    rows_diag = flip(rows_far, "tensor", 1)
+
+    summary_all = lax.all_gather(summary, "tensor", axis=1, tiled=True)
+    logits = jnp.einsum("sbc,ce->sbe", summary_all, router, preferred_element_type=jnp.float32)
+    gate_prob = jax.nn.sigmoid(logits)
+    chosen = jnp.sum(picked * gate_prob[:, :, None, :], -1)
+    route_weight = (ROUTE_SCALE * chosen / jnp.sum(chosen, -1, keepdims=True)).astype(jnp.bfloat16)
+    expert_weight = jnp.sum(picked * route_weight.astype(jnp.float32)[..., None], 2)
+    combine = (slot_hit * expert_weight[..., None]).astype(jnp.bfloat16)
+
+    rows_stack = jnp.stack([rows_in, rows_core, rows_far, rows_diag])
+    turn = jnp.bitwise_xor(group, tensor)
+    pre_act = jnp.zeros((expert_count * places, columns), jnp.float32)
+    for k, piece in zip((0, 1, 3, 2), [held] + held_other):
+        part = lax.dynamic_index_in_dim(rows_stack, jnp.bitwise_xor(turn, k), 0, keepdims=False)
+        pre_act = pre_act + jnp.dot(part, piece, preferred_element_type=jnp.float32)
     active = jax.nn.silu(pre_act).astype(jnp.bfloat16)
+    active = active.reshape(expert_count, places, columns)
     returned = lax.all_to_all(active, "expert", split_axis=0, concat_axis=0, tiled=True)
     returned = returned.reshape(EXPERTS, step_count, slot_count, columns)
-    combine = (slot_hit * expert_weight[..., None]).astype(jnp.bfloat16)
     expert_out = jnp.einsum(
         "sbec,escf->sbf", combine, returned, preferred_element_type=jnp.float32
     ).astype(jnp.bfloat16)

time: 290 us -> 169 us (0.58)
  waiting for transfers between devices: 206 us -> 44 us
  blocking collectives: 10.6 us -> 75.5 us
  between operations: 14.9 us -> 1.69 us
  local copies, waits for them, and re-layouts: 13.5 us -> 5.32 us
  starting transfers between devices: 34.1 us -> 26.6 us
  matrix products: 5.76 us -> 11.1 us
    all_to_all x2 -> x0, waiting for transfers between devices: 147 us -> none  [the longest x1 80.8 us: local(): lax.all_to_all(outgoing, 'expert', split_axis=0, concat_axis=0, tiled=True)]
    all_to_all x0 -> x1, blocking collectives: none -> 60.6 us  [local(): lax.all_to_all(payload, 'expert', split_axis=0, concat_axis=0, tiled=True)]
    all_gather x1 -> x0, waiting for transfers between devices: 41 us -> none  [move_weights(): collected = lax.all_gather(updated[:, None], 'group', axis=1, tiled=True)]
    ppermute x0 -> x6, waiting for transfers between devices: none -> 27.1 us  [flip(): return lax.ppermute(value, axis, [(i, i ^ distance) for i in range(size)])]
    all_to_all x2 -> x0, starting transfers between devices: 24.3 us -> none  [the longest x1 14.2 us: move_weights(): lax.all_to_all(shaped, 'expert', split_axis=0, concat_axis=3, tiled=True)]
    ppermute x0 -> x6, starting transfers between devices: none -> 17.6 us  [flip(): return lax.ppermute(value, axis, [(i, i ^ distance) for i in range(size)])]
    reshape x2 -> x4, local copies, waits for them, and re-layouts: 7.28 us -> 1.72 us  [the longest x1 1.25 us: local(): rows_in = arrived[:, 2 * slab:].reshape(expert_count * places, quarter)]
    all_gather x2, blocking collectives: 10.6 us -> 14.8 us  [the longest x1 9.15 us: local(): summary_all = lax.all_gather(summary, 'tensor', axis=1, tiled=True)]
  transfers between devices with their start and end apart: 4 -> 7, of which waited for: 4 -> 5; matrix products, arithmetic and copies ran while one was open for 4% -> 3% of each run, Pallas kernels for 0% -> 0%
where the time goes in v1:
time: 169 us; the launch traced here: 168 us
  blocking collectives  75.5 us (45%)
  waiting for transfers between devices  44 us (26%)
  starting transfers between devices  26.6 us (16%)
  matrix products  11.1 us (7%)
  local copies, waits for them, and re-layouts  5.32 us (3%)
  other arithmetic  4.31 us (3%)
  between operations  1.69 us (1%)
    all_to_all x1, blocking collectives, local(): lax.all_to_all(payload, 'expert', split_axis=0, concat_axis=0, tiled=True)  60.6 us
    ppermute x6, waiting for transfers between devices, flip(): return lax.ppermute(value, axis, [(i, i ^ distance) for i in range(size)])  27.1 us
    ppermute x6, starting transfers between devices, flip(): return lax.ppermute(value, axis, [(i, i ^ distance) for i in range(size)])  17.6 us
    all_to_all x1, waiting for transfers between devices, local(): lax.all_to_all(active, 'expert', split_axis=0, concat_axis=0, tiled=True)  16.8 us
    all_gather x1, blocking collectives, local(): summary_all = lax.all_gather(summary, 'tensor', axis=1, tiled=True)  9.15 us
    all_to_all x1, starting transfers between devices, local(): lax.all_to_all(active, 'expert', split_axis=0, concat_axis=0, tiled=True)  9.02 us
    all_gather x1, blocking collectives, local(): rows_all = lax.all_gather(hidden_in, 'tensor', axis=1, tiled=True)  5.7 us
    dot_general x4, matrix products, local(): pre_act = pre_act + jnp.dot(part, piece, preferred_element_type=jnp.float32)  3.92 us
  transfers between devices with their start and end apart: 7, of which 5 were waited for; matrix products, arithmetic and copies ran while one was open for 3% of the time, Pallas kernels for 0%

profile of v1, /device:TPU:2, one launch (start us, length us, event | category | flops | bytes accessed | tf_op | source)
XLA Modules:
  0.0 168.5 jit_solution(1236199951929803785)
XLA Ops:
  0.7 0.8 reshape.220
  2.2 0.9 fusion.49
  3.1 1.1 fusion.40
  4.2 1.2 fusion.81
  5.5 0.9 fusion.82
  6.5 0.9 fusion.65
  7.5 0.9 fusion.80
  8.6 9.2 %all_gather.6 = bf16[4,4,512]{2,0,1:T(4,128)(2,1)S(1)} all-gather(bf16[4,1,512]{2,0,1:T(4,128)(2,1)S(1)} %fusion.54), channel_id=1, replica_groups=mesh['group'=4,'expert'=32,'tensor'=4] {'tensor'}, dimensions={1}, use_global_device_ids=true | all-gather | bytes 20480 | tf_op jit(solution)/shard_map/all_gather | solution.py:129
  18.4 5.7 %all_gather.7 = bf16[4,4,3584]{2,0,1:T(4,128)(2,1)S(1)} all-gather(bf16[4,1,3584]{2,0,1:T(4,128)(2,1)S(1)} %copy-done.6), channel_id=1, replica_groups=mesh['group'=4,'expert'=32,'tensor'=4] {'tensor'}, dimensions={1}, use_global_device_ids=true | all-gather | bytes 143360 | tf_op jit(solution)/shard_map/all_gather | solution.py:97
  25.2 3.1 %fusion.17 = (bf16[32,28,256]{2,0,1:T(8,128)(2,1)S(1)}, f32[32,28,256]{2,0,1:T(8,128)}, f32[32,28,256]{2,0,1:T(8,128)}) fusion(bf16[32,28,256]{2,0,1:T(8,128)(2,1)S(1)} %copy-done.3, bf16[32,28,256]{2,0,1:T(8,128)(2,1)} %param.15, f32[32,28,256]{2,0,1:T(8,128)S(1)} %copy-done.1, f32[32,28,256]{2,0,1:T(8,128)S(1)} %copy-done.2), kind=kLoop, calls=%fused_computation.29 | loop fusion | flops 4128768 | bytes 5046272 | tf_op jit(solution)/shard_map/convert_element_type | solution.py:30
  28.5 0.4 copy.47
  28.9 60.6 %all_to_all.10 = bf16[32,112,128]{2,1,0:T(8,128)(2,1)S(1)} all-to-all(bf16[32,112,128]{2,1,0:T(8,128)(2,1)S(1)} %copy.47), channel_id=1, replica_groups=mesh['group'=4,'expert'=32,'tensor'=4] {'expert'}, dimensions={0} | all-to-all | bytes 1835008 | tf_op jit(solution)/shard_map/all_to_all | solution.py:119
  89.6 1.3 reshape.228
  90.9 3.3 %collective-permute-start.1 = (bf16[256,896]{1,0:T(8,128)(2,1)}, bf16[256,896]{1,0:T(8,128)(2,1)S(1)}, u32[]{:S(2)}, u32[]{:S(2)}) collective-permute-start(bf16[256,896]{1,0:T(8,128)(2,1)} %reshape.228), channel_id=1, source_target_pairs={{0,2},{1,3},{2,0},{3,1},{4,6},{5,7},{6,4},{7,5},{8,10},{9,11},{10,... | collective-permute-start | bytes 1376264 | tf_op jit(solution)/shard_map/ppermute | solution.py:70
  94.2 1.9 %collective-permute-start = (bf16[256,896]{1,0:T(8,128)(2,1)}, bf16[256,896]{1,0:T(8,128)(2,1)S(1)}, u32[]{:S(2)}, u32[]{:S(2)}) collective-permute-start(bf16[256,896]{1,0:T(8,128)(2,1)} %reshape.228), channel_id=1, source_target_pairs={{0,1},{1,0},{2,3},{3,2},{4,5},{5,4},{6,7},{7,6},{8,9},{9,8},{10,11... | collective-permute-start | bytes 1376264 | tf_op jit(solution)/shard_map/ppermute | solution.py:70
  96.1 7.3 %collective-permute-done.1 = bf16[256,896]{1,0:T(8,128)(2,1)S(1)} collective-permute-done((bf16[256,896]{1,0:T(8,128)(2,1)}, bf16[256,896]{1,0:T(8,128)(2,1)S(1)}, u32[]{:S(2)}, u32[]{:S(2)}) %collective-permute-start.1) | collective-permute-done | bytes 458784 | tf_op jit(solution)/shard_map/ppermute | solution.py:70
  103.4 1.9 %collective-permute-start.2 = (bf16[256,896]{1,0:T(8,128)(2,1)S(1)}, bf16[256,896]{1,0:T(8,128)(2,1)S(1)}, u32[]{:S(2)}, u32[]{:S(2)}) collective-permute-start(bf16[256,896]{1,0:T(8,128)(2,1)S(1)} %collective-permute-done.1), channel_id=1, source_target_pairs={{0,1},{1,0},{2,3},{3,2},{4,5},{5,4},{6,7},{7,6},{8,9},{9,8},{10,11... | collective-permute-start | bytes 1376264 | tf_op jit(solution)/shard_map/ppermute | solution.py:70
  105.4 0.5 copy.49
  106.0 3.5 %collective-permute-start.3 = (bf16[896,256]{1,0:T(8,128)(2,1)S(1)}, bf16[896,256]{1,0:T(8,128)(2,1)}, u32[]{:S(2)}, u32[]{:S(2)}) collective-permute-start(bf16[896,256]{1,0:T(8,128)(2,1)S(1)} %bitcast.145), channel_id=1, source_target_pairs={{0,128},{128,0},{256,384},{384,256},{1,129},{129,1},{257,385},{385... | collective-permute-start | bytes 1376264 | tf_op jit(solution)/shard_map/ppermute | solution.py:70
  109.5 4.8 %collective-permute-start.5 = (bf16[896,256]{1,0:T(8,128)(2,1)S(1)}, bf16[896,256]{1,0:T(8,128)(2,1)}, u32[]{:S(2)}, u32[]{:S(2)}) collective-permute-start(bf16[896,256]{1,0:T(8,128)(2,1)S(1)} %bitcast.146), channel_id=1, source_target_pairs={{0,256},{128,384},{256,0},{384,128},{1,257},{129,385},{257,1},{385... | collective-permute-start | bytes 1376264 | tf_op jit(solution)/shard_map/ppermute | solution.py:70
  114.3 0.5 stack_reshape.3
  114.8 2.1 %collective-permute-start.4 = (bf16[896,256]{1,0:T(8,128)(2,1)S(1)}, bf16[896,256]{1,0:T(8,128)(2,1)S(1)}, u32[]{:S(2)}, u32[]{:S(2)}) collective-permute-start(bf16[896,256]{1,0:T(8,128)(2,1)S(1)} %bitcast.147), channel_id=1, source_target_pairs={{0,384},{128,256},{256,128},{384,0},{1,385},{129,257},{257,129},{3... | collective-permute-start | bytes 1376264 | tf_op jit(solution)/shard_map/ppermute | solution.py:70
  117.2 4.1 %collective-permute-done.3 = bf16[896,256]{1,0:T(8,128)(2,1)} collective-permute-done((bf16[896,256]{1,0:T(8,128)(2,1)S(1)}, bf16[896,256]{1,0:T(8,128)(2,1)}, u32[]{:S(2)}, u32[]{:S(2)}) %collective-permute-start.3) | collective-permute-done | bytes 458784 | tf_op jit(solution)/shard_map/ppermute | solution.py:70
  121.3 1.3 fusion.22
  122.6 10.7 %collective-permute-done.5 = bf16[896,256]{1,0:T(8,128)(2,1)} collective-permute-done((bf16[896,256]{1,0:T(8,128)(2,1)S(1)}, bf16[896,256]{1,0:T(8,128)(2,1)}, u32[]{:S(2)}, u32[]{:S(2)}) %collective-permute-start.5) | collective-permute-done | bytes 458784 | tf_op jit(solution)/shard_map/ppermute | solution.py:70
  133.3 1.3 fusion.19
  134.9 5.1 %collective-permute-done.4 = bf16[896,256]{1,0:T(8,128)(2,1)S(1)} collective-permute-done((bf16[896,256]{1,0:T(8,128)(2,1)S(1)}, bf16[896,256]{1,0:T(8,128)(2,1)S(1)}, u32[]{:S(2)}, u32[]{:S(2)}) %collective-permute-start.4) | collective-permute-done | bytes 458784 | tf_op jit(solution)/shard_map/ppermute | solution.py:70
  140.1 1.0 fusion.37
  141.1 9.0 %all-to-all-start.1 = ((bf16[32,8,256]{2,1,0:T(8,128)(2,1)}), bf16[32,8,256]{2,1,0:T(8,128)(2,1)S(1)}, u32[]{:S(2)}, u32[]{:S(2)}) async-start(bf16[32,8,256]{2,1,0:T(8,128)(2,1)} %fusion.37), calls=%async_computation.1 | async-start | bytes 262144 | tf_op jit(solution)/shard_map/all_to_all | solution.py:145
  150.1 0.7 convert_element_type.80
  150.8 16.8 %all-to-all-done.1 = bf16[32,8,256]{2,1,0:T(8,128)(2,1)S(1)} async-done(((bf16[32,8,256]{2,1,0:T(8,128)(2,1)}), bf16[32,8,256]{2,1,0:T(8,128)(2,1)S(1)}, u32[]{:S(2)}, u32[]{:S(2)}) %all-to-all-start.1) | async-done | bytes 131104 | tf_op jit(solution)/shard_map/all_to_all | solution.py:145
  167.7 0.8 fusion.7
  (47 shorter events, 3.2 us)
Async XLA Ops:
  0.6 3.6 %copy-start = (bf16[1,256,512]{2,1,0:T(8,128)(2,1)S(1)}, bf16[1,256,512]{2,1,0:T(8,128)(2,1)}, u32[]{:S(2)}) copy-start(bf16[1,256,512]{2,1,0:T(8,128)(2,1)} %param.21) | copy-start | bytes 786436
  0.6 17.1 %copy-start.7 = (bf16[512,32]{0,1:T(8,128)(2,1)S(1)}, bf16[512,32]{0,1:T(8,128)(2,1)}, u32[]{:S(2)}) copy-start(bf16[512,32]{0,1:T(8,128)(2,1)} %param.27) | copy-start | bytes 98308
  0.7 17.2 %copy-start.5 = (s32[4,4,8]{2,1,0:T(4,128)S(1)}, s32[4,4,8]{2,1,0:T(4,128)}, u32[]{:S(2)}) copy-start(s32[4,4,8]{2,1,0:T(4,128)} %param.26) | copy-start | bytes 1540
  0.7 17.7 %copy-start.6 = (bf16[4,1,3584]{2,0,1:T(4,128)(2,1)S(1)}, bf16[4,1,3584]{2,0,1:T(4,128)(2,1)}, u32[]{:S(2)}) copy-start(bf16[4,1,3584]{2,0,1:T(4,128)(2,1)} %param.18) | copy-start | bytes 86020
  17.7 7.4 %copy-start.1 = (f32[32,28,256]{2,0,1:T(8,128)S(1)}, f32[32,28,256]{2,0,1:T(8,128)}, u32[]{:S(2)}) copy-start(f32[32,28,256]{2,0,1:T(8,128)} %param.17) | copy-start | bytes 2752516
  17.7 7.4 %copy-start.2 = (f32[32,28,256]{2,0,1:T(8,128)S(1)}, f32[32,28,256]{2,0,1:T(8,128)}, u32[]{:S(2)}) copy-start(f32[32,28,256]{2,0,1:T(8,128)} %param.16) | copy-start | bytes 2752516
  17.7 7.4 %copy-start.3 = (bf16[32,28,256]{2,0,1:T(8,128)(2,1)S(1)}, bf16[32,28,256]{2,0,1:T(8,128)(2,1)}, u32[]{:S(2)}) copy-start(bf16[32,28,256]{2,0,1:T(8,128)(2,1)} %param.14) | copy-start | bytes 1376260
  90.9 12.6 %collective-permute-start.1 = (bf16[256,896]{1,0:T(8,128)(2,1)}, bf16[256,896]{1,0:T(8,128)(2,1)S(1)}, u32[]{:S(2)}, u32[]{:S(2)}) collective-permute-start(bf16[256,896]{1,0:T(8,128)(2,1)} %reshape.228), channel_id=1, source_target_pairs={{0,2},{1,3},{2,0},{3,1},{4,6},{5,7},{6,4},{7,5},{8,10},{9,11},{10,... | collective-permute-start | bytes 1376264 | tf_op jit(solution)/shard_map/ppermute | solution.py:70
  94.2 22.7 %collective-permute-start = (bf16[256,896]{1,0:T(8,128)(2,1)}, bf16[256,896]{1,0:T(8,128)(2,1)S(1)}, u32[]{:S(2)}, u32[]{:S(2)}) collective-permute-start(bf16[256,896]{1,0:T(8,128)(2,1)} %reshape.228), channel_id=1, source_target_pairs={{0,1},{1,0},{2,3},{3,2},{4,5},{5,4},{6,7},{7,6},{8,9},{9,8},{10,11... | collective-permute-start | bytes 1376264 | tf_op jit(solution)/shard_map/ppermute | solution.py:70
  103.4 13.5 %collective-permute-start.2 = (bf16[256,896]{1,0:T(8,128)(2,1)S(1)}, bf16[256,896]{1,0:T(8,128)(2,1)S(1)}, u32[]{:S(2)}, u32[]{:S(2)}) collective-permute-start(bf16[256,896]{1,0:T(8,128)(2,1)S(1)} %collective-permute-done.1), channel_id=1, source_target_pairs={{0,1},{1,0},{2,3},{3,2},{4,5},{5,4},{6,7},{7,6},{8,9},{9,8},{10,11... | collective-permute-start | bytes 1376264 | tf_op jit(solution)/shard_map/ppermute | solution.py:70
  106.0 15.3 %collective-permute-start.3 = (bf16[896,256]{1,0:T(8,128)(2,1)S(1)}, bf16[896,256]{1,0:T(8,128)(2,1)}, u32[]{:S(2)}, u32[]{:S(2)}) collective-permute-start(bf16[896,256]{1,0:T(8,128)(2,1)S(1)} %bitcast.145), channel_id=1, source_target_pairs={{0,128},{128,0},{256,384},{384,256},{1,129},{129,1},{257,385},{385... | collective-permute-start | bytes 1376264 | tf_op jit(solution)/shard_map/ppermute | solution.py:70
  109.5 23.8 %collective-permute-start.5 = (bf16[896,256]{1,0:T(8,128)(2,1)S(1)}, bf16[896,256]{1,0:T(8,128)(2,1)}, u32[]{:S(2)}, u32[]{:S(2)}) collective-permute-start(bf16[896,256]{1,0:T(8,128)(2,1)S(1)} %bitcast.146), channel_id=1, source_target_pairs={{0,256},{128,384},{256,0},{384,128},{1,257},{129,385},{257,1},{385... | collective-permute-start | bytes 1376264 | tf_op jit(solution)/shard_map/ppermute | solution.py:70
  114.8 25.3 %collective-permute-start.4 = (bf16[896,256]{1,0:T(8,128)(2,1)S(1)}, bf16[896,256]{1,0:T(8,128)(2,1)S(1)}, u32[]{:S(2)}, u32[]{:S(2)}) collective-permute-start(bf16[896,256]{1,0:T(8,128)(2,1)S(1)} %bitcast.147), channel_id=1, source_target_pairs={{0,384},{128,256},{256,128},{384,0},{1,385},{129,257},{257,129},{3... | collective-permute-start | bytes 1376264 | tf_op jit(solution)/shard_map/ppermute | solution.py:70
  134.6 15.5 %copy-start.4 = (bf16[4,1,32,512]{3,2,0,1:T(8,128)(2,1)S(1)}, bf16[4,1,32,512]{3,2,0,1:T(8,128)(2,1)}, u32[]{:S(2)}) copy-start(bf16[4,1,32,512]{3,2,0,1:T(8,128)(2,1)} %get-tuple-element.14) | copy-start | bytes 393220
  141.1 26.6 %all-to-all-start.1 = ((bf16[32,8,256]{2,1,0:T(8,128)(2,1)}), bf16[32,8,256]{2,1,0:T(8,128)(2,1)S(1)}, u32[]{:S(2)}, u32[]{:S(2)}) async-start(bf16[32,8,256]{2,1,0:T(8,128)(2,1)} %fusion.37), calls=%async_computation.1 | async-start | bytes 262144 | tf_op jit(solution)/shard_map/all_to_all | solution.py:145

commit v2 on v1

--- a/solution.py
+++ b/solution.py
@@ -88,12 +88,9 @@
 ):
     first_new, second_new, updated = adamw(weights, gradients, moment_one, moment_two)
     expert_count, slab, columns = updated.shape
-    attention_out, summary = attend(
-        query_latent, query_rope, cache_latent, cache_rope, new_latent, new_rope, lengths
-    )
     step_count, _, width = hidden_in.shape
     quarter = width // 4
-    group, tensor = lax.axis_index("group"), lax.axis_index("tensor")
+    tensor = lax.axis_index("tensor")
     rows_all = lax.all_gather(hidden_in, "tensor", axis=1, tiled=True)
     block_rows = rows_all.shape[1]
     slot_count = 2
@@ -116,12 +113,19 @@
     slabs = jnp.swapaxes(updated.reshape(expert_count, slab, 2, 128), 1, 2)
     slabs = slabs.reshape(expert_count, 2 * slab, 128)
     payload = jnp.concatenate([slabs, outgoing], 1)
+    payload, query_latent, query_rope, new_latent, new_rope = lax.optimization_barrier(
+        (payload, query_latent, query_rope, new_latent, new_rope)
+    )
+    attention_out, summary = attend(
+        query_latent, query_rope, cache_latent, cache_rope, new_latent, new_rope, lengths
+    )
     arrived = lax.all_to_all(payload, "expert", split_axis=0, concat_axis=0, tiled=True)
     held = jnp.swapaxes(arrived[:, : 2 * slab].reshape(expert_count, 2, slab, 128), 1, 2)
     held = held.reshape(expert_count * slab, columns)
     rows_in = arrived[:, 2 * slab :].reshape(expert_count * places, quarter)
 
-    held_other = [flip(held, "group", k) for k in (1, 3, 2)]
+    copies = jnp.broadcast_to(held[None], (lax.axis_size("group"),) + held.shape)
+    whole = lax.all_to_all(copies, "group", split_axis=0, concat_axis=0, tiled=True)
     rows_far = flip(rows_in, "tensor", 2)
     rows_core = flip(rows_in, "tensor", 1)
     rows_diag = flip(rows_far, "tensor", 1)
@@ -134,11 +138,9 @@
     expert_weight = jnp.sum(picked * route_weight.astype(jnp.float32)[..., None], 2)
     combine = (slot_hit * expert_weight[..., None]).astype(jnp.bfloat16)
 
-    rows_stack = jnp.stack([rows_in, rows_core, rows_far, rows_diag])
-    turn = jnp.bitwise_xor(group, tensor)
     pre_act = jnp.zeros((expert_count * places, columns), jnp.float32)
-    for k, piece in zip((0, 1, 3, 2), [held] + held_other):
-        part = lax.dynamic_index_in_dim(rows_stack, jnp.bitwise_xor(turn, k), 0, keepdims=False)
+    for k, part in enumerate((rows_in, rows_core, rows_far, rows_diag)):
+        piece = lax.dynamic_index_in_dim(whole, jnp.bitwise_xor(tensor, k), 0, keepdims=False)
         pre_act = pre_act + jnp.dot(part, piece, preferred_element_type=jnp.float32)
     active = jax.nn.silu(pre_act).astype(jnp.bfloat16)
     active = active.reshape(expert_count, places, columns)

time: 169 us -> 138 us (0.82)
  blocking collectives: 75.5 us -> 17.3 us
  waiting for transfers between devices: 44 us -> 67.6 us
  starting transfers between devices: 26.6 us -> 34.1 us
  matrix products: 11.1 us -> 6.49 us
    all_to_all x1 -> x0, blocking collectives: 60.6 us -> none  [local(): lax.all_to_all(payload, 'expert', split_axis=0, concat_axis=0, tiled=True)]
    all_to_all x0 -> x2, waiting for transfers between devices: none -> 51.6 us  [the longest x1 46.5 us: local(): lax.all_to_all(payload, 'expert', split_axis=0, concat_axis=0, tiled=True)]
    ppermute x6 -> x3, waiting for transfers between devices: 27.1 us -> 0.01 us  [flip(): return lax.ppermute(value, axis, [(i, i ^ distance) for i in range(size)])]
    all_to_all x0 -> x2, starting transfers between devices: none -> 17.7 us  [the longest x1 13.1 us: local(): lax.all_to_all(payload, 'expert', split_axis=0, concat_axis=0, tiled=True)]
    ppermute x6 -> x3, starting transfers between devices: 17.6 us -> 7.46 us  [flip(): return lax.ppermute(value, axis, [(i, i ^ distance) for i in range(size)])]
    all_gather x1, blocking collectives: 5.7 us -> 9.71 us  [local(): rows_all = lax.all_gather(hidden_in, 'tensor', axis=1, tiled=True)]
  transfers between devices with their start and end apart: 7 -> 6, of which waited for: 5 -> 3; matrix products, arithmetic and copies ran while one was open for 3% -> 4% of each run, Pallas kernels for 0% -> 0%
where the time goes in v2:
time: 138 us
  waiting for transfers between devices  67.6 us (49%)
  starting transfers between devices  34.1 us (25%)
  blocking collectives  17.3 us (13%)
  matrix products  6.49 us (5%)
  local copies, waits for them, and re-layouts  5.65 us (4%)
  other arithmetic  4.8 us (3%)
  between operations  1.71 us (1%)
    all_to_all x1, waiting for transfers between devices, local(): lax.all_to_all(payload, 'expert', split_axis=0, concat_axis=0, tiled=True)  46.5 us
    all_to_all x1, waiting for transfers between devices, local(): lax.all_to_all(active, 'expert', split_axis=0, concat_axis=0, tiled=True)  16 us
    all_to_all x1, starting transfers between devices, local(): lax.all_to_all(payload, 'expert', split_axis=0, concat_axis=0, tiled=True)  13.1 us
    all_gather x1, blocking collectives, local(): rows_all = lax.all_gather(hidden_in, 'tensor', axis=1, tiled=True)  9.71 us
    all_to_all x1, starting transfers between devices, local(): lax.all_to_all(active, 'expert', split_axis=0, concat_axis=0, tiled=True)  9.01 us
    all_gather x1, blocking collectives, local(): summary_all = lax.all_gather(summary, 'tensor', axis=1, tiled=True)  7.57 us
    ppermute x3, starting transfers between devices, flip(): return lax.ppermute(value, axis, [(i, i ^ distance) for i in range(size)])  7.46 us
    all_to_all x1, waiting for transfers between devices, local(): lax.all_to_all(copies, 'group', split_axis=0, concat_axis=0, tiled=True)  5.07 us
  transfers between devices with their start and end apart: 6, of which 3 were waited for; matrix products, arithmetic and copies ran while one was open for 4% of the time, Pallas kernels for 0%

profile of v2, /device:TPU:2, one launch (start us, length us, event | category | flops | bytes accessed | tf_op | source)
XLA Modules:
  0.0 137.7 jit_solution(9995079380089139221)
XLA Ops:
  0.7 9.7 %all_gather.6 = bf16[4,4,3584]{2,0,1:T(4,128)(2,1)S(1)} all-gather(bf16[4,1,3584]{2,0,1:T(4,128)(2,1)} %param.18), channel_id=1, replica_groups=mesh['group'=4,'expert'=32,'tensor'=4] {'tensor'}, dimensions={1}, use_global_device_ids=true | all-gather | bytes 143360 | tf_op jit(solution)/shard_map/all_gather | solution.py:94
  10.4 0.8 convert_reduce_fusion
  11.3 0.3 fusion
  11.6 0.4 copy.43
  12.0 0.3 reshape.219
  12.4 3.1 %fusion.16 = (bf16[32,28,256]{2,0,1:T(8,128)(2,1)S(1)}, f32[32,28,256]{2,0,1:T(8,128)}, f32[32,28,256]{2,0,1:T(8,128)}) fusion(bf16[32,28,256]{2,0,1:T(8,128)(2,1)S(1)} %copy-done.4, bf16[32,28,256]{2,0,1:T(8,128)(2,1)} %param.15, f32[32,28,256]{2,0,1:T(8,128)S(1)} %copy-done.1, f32[32,28,256]{2,0,1:T(8,128)S(1)} %copy-done.2), kind=kLoop, calls=%fused_computation.30 | loop fusion | flops 4128768 | bytes 5046272 | tf_op jit(solution)/shard_map/convert_element_type | solution.py:30
  15.7 1.3 copy.46
  17.0 13.1 %all-to-all-start = ((bf16[32,112,128]{2,1,0:T(8,128)(2,1)}), bf16[32,112,128]{2,1,0:T(8,128)(2,1)S(1)}, u32[]{:S(2)}, u32[]{:S(2)}) async-start(bf16[32,112,128]{2,1,0:T(8,128)(2,1)} %copy.46), calls=%async_computation | async-start | bytes 1835008 | tf_op jit(solution)/shard_map/all_to_all | solution.py:122
  30.9 0.2 fusion.34
  31.3 0.3 fusion.74
  31.6 46.5 %all-to-all-done = bf16[32,112,128]{2,1,0:T(8,128)(2,1)S(1)} async-done(((bf16[32,112,128]{2,1,0:T(8,128)(2,1)}), bf16[32,112,128]{2,1,0:T(8,128)(2,1)S(1)}, u32[]{:S(2)}, u32[]{:S(2)}) %all-to-all-start) | async-done | bytes 917536 | tf_op jit(solution)/shard_map/all_to_all | solution.py:122
  78.2 0.5 copy.48
  78.8 1.4 broadcast_in_dim.33
  80.2 4.6 %all-to-all-start.1 = ((bf16[4,896,256]{2,1,0:T(8,128)(2,1)}), bf16[4,896,256]{2,1,0:T(8,128)(2,1)S(1)}, u32[]{:S(2)}, u32[]{:S(2)}) async-start(bf16[4,896,256]{2,1,0:T(8,128)(2,1)} %broadcast_in_dim.33), calls=%async_computation.1 | async-start | bytes 3670016 | tf_op jit(solution)/shard_map/all_to_all | solution.py:128
  84.8 0.2 fusion.75
  85.2 0.2 convolution_bitcast_fusion
  85.4 0.3 fusion.73
  85.7 0.5 reshape.228
  86.1 3.3 %collective-permute-start.1 = (bf16[256,896]{1,0:T(8,128)(2,1)S(1)}, bf16[256,896]{1,0:T(8,128)(2,1)S(1)}, u32[]{:S(2)}, u32[]{:S(2)}) collective-permute-start(bf16[256,896]{1,0:T(8,128)(2,1)S(1)} %reshape.228), channel_id=1, source_target_pairs={{0,2},{1,3},{2,0},{3,1},{4,6},{5,7},{6,4},{7,5},{8,10},{9,11},{10,... | collective-permute-start | bytes 1376264 | tf_op jit(solution)/shard_map/ppermute | solution.py:70
  89.6 1.9 %collective-permute-start = (bf16[256,896]{1,0:T(8,128)(2,1)S(1)}, bf16[256,896]{1,0:T(8,128)(2,1)}, u32[]{:S(2)}, u32[]{:S(2)}) collective-permute-start(bf16[256,896]{1,0:T(8,128)(2,1)S(1)} %reshape.228), channel_id=1, source_target_pairs={{0,1},{1,0},{2,3},{3,2},{4,5},{5,4},{6,7},{7,6},{8,9},{9,8},{10,11... | collective-permute-start | bytes 1376264 | tf_op jit(solution)/shard_map/ppermute | solution.py:70
  91.6 7.6 %all_gather.7 = bf16[4,4,512]{2,0,1:T(4,128)(2,1)S(1)} all-gather(bf16[4,1,512]{2,0,1:T(4,128)(2,1)S(1)} %fusion.48), channel_id=1, replica_groups=mesh['group'=4,'expert'=32,'tensor'=4] {'tensor'}, dimensions={1}, use_global_device_ids=true | all-gather | bytes 20480 | tf_op jit(solution)/shard_map/all_gather | solution.py:133
  99.2 2.2 %collective-permute-start.2 = (bf16[256,896]{1,0:T(8,128)(2,1)S(1)}, bf16[256,896]{1,0:T(8,128)(2,1)}, u32[]{:S(2)}, u32[]{:S(2)}) collective-permute-start(bf16[256,896]{1,0:T(8,128)(2,1)S(1)} %collective-permute-done.1), channel_id=1, source_target_pairs={{0,1},{1,0},{2,3},{3,2},{4,5},{5,4},{6,7},{7,6},{8,9},{9,8},{10,11... | collective-permute-start | bytes 1376264 | tf_op jit(solution)/shard_map/ppermute | solution.py:70
  101.4 5.1 %all-to-all-done.1 = bf16[4,896,256]{2,1,0:T(8,128)(2,1)S(1)} async-done(((bf16[4,896,256]{2,1,0:T(8,128)(2,1)}), bf16[4,896,256]{2,1,0:T(8,128)(2,1)S(1)}, u32[]{:S(2)}, u32[]{:S(2)}) %all-to-all-start.1) | async-done | bytes 1835040 | tf_op jit(solution)/shard_map/all_to_all | solution.py:128
  106.5 0.3 fusion.21
  106.8 1.3 convolution_add_fusion.2
  108.2 0.3 convolution_add_fusion.1
  108.5 2.0 %fusion.31 = bf16[32,8,256]{2,1,0:T(8,128)(2,1)} fusion(f32[256,256]{1,0:T(8,128)S(1)} %convolution_add_fusion.1, bf16[256,896]{1,0:T(8,128)(2,1)} %collective-permute-done.2, bf16[4,896,256]{2,1,0:T(8,128)(2,1)S(1)} %all-to-all-done.1, s32[]{:T(128)S(6)} %select_n.34), kind=kOutput, calls=%fused_computation.46 | convolution fusion | flops 117833728 | bytes 1310724 | tf_op jit(solution)/shard_map/dot_general | solution.py:144
  110.5 9.0 %all-to-all-start.2 = ((bf16[32,8,256]{2,1,0:T(8,128)(2,1)}), bf16[32,8,256]{2,1,0:T(8,128)(2,1)S(1)}, u32[]{:S(2)}, u32[]{:S(2)}) async-start(bf16[32,8,256]{2,1,0:T(8,128)(2,1)} %fusion.31), calls=%async_computation.2 | async-start | bytes 262144 | tf_op jit(solution)/shard_map/all_to_all | solution.py:147
  119.6 0.7 convert_element_type.86
  120.4 0.2 select_reduce_fusion
  120.8 16.0 %all-to-all-done.2 = bf16[32,8,256]{2,1,0:T(8,128)(2,1)S(1)} async-done(((bf16[32,8,256]{2,1,0:T(8,128)(2,1)}), bf16[32,8,256]{2,1,0:T(8,128)(2,1)S(1)}, u32[]{:S(2)}, u32[]{:S(2)}) %all-to-all-start.2) | async-done | bytes 131104 | tf_op jit(solution)/shard_map/all_to_all | solution.py:147
  136.9 0.8 fusion.6
  (50 shorter events, 1.7 us)
Async XLA Ops:
  0.6 30.6 %copy-start = (bf16[1,256,512]{2,1,0:T(8,128)(2,1)S(1)}, bf16[1,256,512]{2,1,0:T(8,128)(2,1)}, u32[]{:S(2)}) copy-start(bf16[1,256,512]{2,1,0:T(8,128)(2,1)} %param.21) | copy-start | bytes 786436
  0.6 11.7 %copy-start.4 = (bf16[32,28,256]{2,0,1:T(8,128)(2,1)S(1)}, bf16[32,28,256]{2,0,1:T(8,128)(2,1)}, u32[]{:S(2)}) copy-start(bf16[32,28,256]{2,0,1:T(8,128)(2,1)} %param.14) | copy-start | bytes 1376260
  0.7 11.7 %copy-start.1 = (f32[32,28,256]{2,0,1:T(8,128)S(1)}, f32[32,28,256]{2,0,1:T(8,128)}, u32[]{:S(2)}) copy-start(f32[32,28,256]{2,0,1:T(8,128)} %param.17) | copy-start | bytes 2752516
  0.7 11.7 %copy-start.2 = (f32[32,28,256]{2,0,1:T(8,128)S(1)}, f32[32,28,256]{2,0,1:T(8,128)}, u32[]{:S(2)}) copy-start(f32[32,28,256]{2,0,1:T(8,128)} %param.16) | copy-start | bytes 2752516
  15.7 14.4 %copy-start.8 = (bf16[4,1,2048]{2,0,1:T(4,128)(2,1)S(1)}, bf16[4,1,2048]{2,0,1:T(4,128)(2,1)}, u32[]{:S(2)}) copy-start(bf16[4,1,2048]{2,0,1:T(4,128)(2,1)} %param.20) | copy-start | bytes 49156
  15.7 15.2 %copy-start.3 = (bf16[4,1,16384]{2,0,1:T(4,128)(2,1)S(1)}, bf16[4,1,16384]{2,0,1:T(4,128)(2,1)}, u32[]{:S(2)}) copy-start(bf16[4,1,16384]{2,0,1:T(4,128)(2,1)} %param.19) | copy-start | bytes 393220
  15.7 15.2 %copy-start.7 = (bf16[4,1,512]{2,0,1:T(4,128)(2,1)S(1)}, bf16[4,1,512]{2,0,1:T(4,128)(2,1)}, u32[]{:S(2)}) copy-start(bf16[4,1,512]{2,0,1:T(4,128)(2,1)} %param.23) | copy-start | bytes 12292
  15.7 15.4 %copy-start.6 = (bf16[1,64,256]{2,1,0:T(8,128)(2,1)S(1)}, bf16[1,64,256]{2,1,0:T(8,128)(2,1)}, u32[]{:S(2)}) copy-start(bf16[1,64,256]{2,1,0:T(8,128)(2,1)} %param.22) | copy-start | bytes 98308
  17.0 61.0 %all-to-all-start = ((bf16[32,112,128]{2,1,0:T(8,128)(2,1)}), bf16[32,112,128]{2,1,0:T(8,128)(2,1)S(1)}, u32[]{:S(2)}, u32[]{:S(2)}) async-start(bf16[32,112,128]{2,1,0:T(8,128)(2,1)} %copy.46), calls=%async_computation | async-start | bytes 1835008 | tf_op jit(solution)/shard_map/all_to_all | solution.py:122
  80.2 4.6 %copy-start.10 = (bf16[4,1,64]{2,0,1:T(4,128)(2,1)S(1)}, bf16[4,1,64]{2,0,1:T(4,128)(2,1)}, u32[]{:S(2)}) copy-start(bf16[4,1,64]{2,0,1:T(4,128)(2,1)} %param.24) | copy-start | bytes 1540
  80.2 26.3 %all-to-all-start.1 = ((bf16[4,896,256]{2,1,0:T(8,128)(2,1)}), bf16[4,896,256]{2,1,0:T(8,128)(2,1)S(1)}, u32[]{:S(2)}, u32[]{:S(2)}) async-start(bf16[4,896,256]{2,1,0:T(8,128)(2,1)} %broadcast_in_dim.33), calls=%async_computation.1 | async-start | bytes 3670016 | tf_op jit(solution)/shard_map/all_to_all | solution.py:128
  86.1 13.1 %collective-permute-start.1 = (bf16[256,896]{1,0:T(8,128)(2,1)S(1)}, bf16[256,896]{1,0:T(8,128)(2,1)S(1)}, u32[]{:S(2)}, u32[]{:S(2)}) collective-permute-start(bf16[256,896]{1,0:T(8,128)(2,1)S(1)} %reshape.228), channel_id=1, source_target_pairs={{0,2},{1,3},{2,0},{3,1},{4,6},{5,7},{6,4},{7,5},{8,10},{9,11},{10,... | collective-permute-start | bytes 1376264 | tf_op jit(solution)/shard_map/ppermute | solution.py:70
  89.6 17.2 %collective-permute-start = (bf16[256,896]{1,0:T(8,128)(2,1)S(1)}, bf16[256,896]{1,0:T(8,128)(2,1)}, u32[]{:S(2)}, u32[]{:S(2)}) collective-permute-start(bf16[256,896]{1,0:T(8,128)(2,1)S(1)} %reshape.228), channel_id=1, source_target_pairs={{0,1},{1,0},{2,3},{3,2},{4,5},{5,4},{6,7},{7,6},{8,9},{9,8},{10,11... | collective-permute-start | bytes 1376264 | tf_op jit(solution)/shard_map/ppermute | solution.py:70
  99.2 9.3 %collective-permute-start.2 = (bf16[256,896]{1,0:T(8,128)(2,1)S(1)}, bf16[256,896]{1,0:T(8,128)(2,1)}, u32[]{:S(2)}, u32[]{:S(2)}) collective-permute-start(bf16[256,896]{1,0:T(8,128)(2,1)S(1)} %collective-permute-done.1), channel_id=1, source_target_pairs={{0,1},{1,0},{2,3},{3,2},{4,5},{5,4},{6,7},{7,6},{8,9},{9,8},{10,11... | collective-permute-start | bytes 1376264 | tf_op jit(solution)/shard_map/ppermute | solution.py:70
  108.1 11.4 %copy-start.9 = (bf16[512,32]{0,1:T(8,128)(2,1)S(1)}, bf16[512,32]{0,1:T(8,128)(2,1)}, u32[]{:S(2)}) copy-start(bf16[512,32]{0,1:T(8,128)(2,1)} %param.27) | copy-start | bytes 98308
  108.1 12.2 %copy-start.5 = (s32[4,4,8]{2,1,0:T(4,128)S(1)}, s32[4,4,8]{2,1,0:T(4,128)}, u32[]{:S(2)}) copy-start(s32[4,4,8]{2,1,0:T(4,128)} %param.26) | copy-start | bytes 1540
  110.5 26.4 %all-to-all-start.2 = ((bf16[32,8,256]{2,1,0:T(8,128)(2,1)}), bf16[32,8,256]{2,1,0:T(8,128)(2,1)S(1)}, u32[]{:S(2)}, u32[]{:S(2)}) async-start(bf16[32,8,256]{2,1,0:T(8,128)(2,1)} %fusion.31), calls=%async_computation.2 | async-start | bytes 262144 | tf_op jit(solution)/shard_map/all_to_all | solution.py:147

commit v3 on v2

--- a/solution.py
+++ b/solution.py
@@ -7,6 +7,7 @@
 HEADS = 32
 LAT = 512
 ROPE = 64
+RING = 16
 
 
 BETA_ONE = 0.9
@@ -65,6 +66,13 @@
     return (attention_out, summary.astype(jnp.bfloat16))
 
 
+def shift(value, distance):
+    pairs = [
+        (x * RING + (z + distance) % RING, x * RING + z) for x in range(2) for z in range(RING)
+    ]
+    return lax.ppermute(value, "expert", pairs)
+
+
 def flip(value, axis, distance):
     size = lax.axis_size(axis)
     return lax.ppermute(value, axis, [(i, i ^ distance) for i in range(size)])
@@ -86,53 +94,83 @@
     expert_ids,
     router,
 ):
+    step_count, _, width = hidden_in.shape
+    quarter = width // 4
+    top_count = expert_ids.shape[2]
+    expert, tensor = lax.axis_index("expert"), lax.axis_index("tensor")
+    side, ring = expert // RING, expert % RING
+    slot_count = 2
+    places = step_count * slot_count
+
+    own_ids = lax.dynamic_index_in_dim(expert_ids, tensor, 1, keepdims=False)
+    own_ids = jnp.pad(own_ids.astype(jnp.bfloat16), ((0, 0), (0, 128 - top_count)))
+    parts = jnp.swapaxes(hidden_in.reshape(step_count, 4, quarter), 0, 1)
+    parts = jnp.concatenate([parts, jnp.broadcast_to(own_ids, (4,) + own_ids.shape)], -1)
+    parts = jnp.broadcast_to(parts[None], (4,) + parts.shape).reshape((16,) + parts.shape[1:])
+    parts, query_latent, query_rope, new_latent, new_rope = lax.optimization_barrier(
+        (parts, query_latent, query_rope, new_latent, new_rope)
+    )
+    far_groups = [
+        [(x * RING + 4 * b + r) * 4 + t for b in range(4) for t in range(4)]
+        for x in range(2)
+        for r in range(4)
+    ]
+    near = lax.all_to_all(
+        parts,
+        ("expert", "tensor"),
+        split_axis=0,
+        concat_axis=0,
+        tiled=True,
+        axis_index_groups=far_groups,
+    )
+
     first_new, second_new, updated = adamw(weights, gradients, moment_one, moment_two)
     expert_count, slab, columns = updated.shape
-    step_count, _, width = hidden_in.shape
-    quarter = width // 4
-    tensor = lax.axis_index("tensor")
-    rows_all = lax.all_gather(hidden_in, "tensor", axis=1, tiled=True)
-    block_rows = rows_all.shape[1]
-    slot_count = 2
-    places = step_count * slot_count
-
+    attention_out, summary = attend(
+        query_latent, query_rope, cache_latent, cache_rope, new_latent, new_rope, lengths
+    )
+
+    near, updated = lax.optimization_barrier((near, updated))
+    held = lax.all_to_all(updated, "expert", split_axis=0, concat_axis=0, tiled=True)
+    held = held.reshape(expert_count * slab, columns)
+
+    both = jnp.stack([near, flip(near, "expert", RING)])
+    pieces = [both] + [shift(both, j) for j in (1, 2, -1)]
+    pieces = jnp.stack(pieces).reshape((8, 4, 4, step_count, quarter + 128))
+    order = [
+        lax.rem(r + 4 - lax.rem(ring, 4), 4) * 2 + jnp.bitwise_xor(x, side)
+        for x in range(2)
+        for r in range(4)
+    ]
+    rows_all = jnp.stack([lax.dynamic_index_in_dim(pieces, i, 0, keepdims=False) for i in order])
+    rows_all = rows_all.reshape(2, 4, 4, 4, step_count, quarter + 128)
+    ids = rows_all[..., quarter : quarter + top_count]
+    wanted = jnp.sum((ids == expert.astype(jnp.bfloat16)).astype(jnp.float32), -1)
+    before = jnp.cumsum(wanted, 3) - wanted
+    chosen_rows = []
+    for c in range(slot_count):
+        take = wanted * (before == c).astype(jnp.float32)
+        chosen_rows.append(
+            jnp.sum(take[..., None] * rows_all[..., :quarter].astype(jnp.float32), 3)
+        )
+    rows_in = jnp.stack(chosen_rows, 3).astype(jnp.bfloat16)
+    rows_in = jnp.transpose(rows_in, (0, 2, 1, 3, 4, 5)).reshape(expert_count * places, quarter)
+
+    copies = jnp.broadcast_to(held[None], (lax.axis_size("group"),) + held.shape)
+    whole = lax.all_to_all(copies, "group", split_axis=0, concat_axis=0, tiled=True)
+    rows_far = flip(rows_in, "tensor", 2)
+    rows_core = flip(rows_in, "tensor", 1)
+    rows_diag = flip(rows_far, "tensor", 1)
+
+    summary_all = lax.all_gather(summary, "tensor", axis=1, tiled=True)
+    logits = jnp.einsum("sbc,ce->sbe", summary_all, router, preferred_element_type=jnp.float32)
+    gate_prob = jax.nn.sigmoid(logits)
     picked = (expert_ids[..., None] == jnp.arange(EXPERTS, dtype=jnp.int32)).astype(jnp.float32)
     per_expert = jnp.sum(picked, 2)
     earlier = jnp.cumsum(per_expert, 1) - per_expert
     slot_hit = (earlier[..., None] == jnp.arange(slot_count, dtype=jnp.float32)).astype(
         jnp.float32
     ) * per_expert[..., None]
-    my_part = lax.dynamic_slice_in_dim(rows_all, tensor * quarter, quarter, 2)
-    outgoing = jnp.einsum(
-        "sbec,sbd->escd",
-        slot_hit.astype(jnp.bfloat16),
-        my_part,
-        preferred_element_type=jnp.float32,
-    ).astype(jnp.bfloat16)
-    outgoing = outgoing.reshape(expert_count, places * quarter // 128, 128)
-    slabs = jnp.swapaxes(updated.reshape(expert_count, slab, 2, 128), 1, 2)
-    slabs = slabs.reshape(expert_count, 2 * slab, 128)
-    payload = jnp.concatenate([slabs, outgoing], 1)
-    payload, query_latent, query_rope, new_latent, new_rope = lax.optimization_barrier(
-        (payload, query_latent, query_rope, new_latent, new_rope)
-    )
-    attention_out, summary = attend(
-        query_latent, query_rope, cache_latent, cache_rope, new_latent, new_rope, lengths
-    )
-    arrived = lax.all_to_all(payload, "expert", split_axis=0, concat_axis=0, tiled=True)
-    held = jnp.swapaxes(arrived[:, : 2 * slab].reshape(expert_count, 2, slab, 128), 1, 2)
-    held = held.reshape(expert_count * slab, columns)
-    rows_in = arrived[:, 2 * slab :].reshape(expert_count * places, quarter)
-
-    copies = jnp.broadcast_to(held[None], (lax.axis_size("group"),) + held.shape)
-    whole = lax.all_to_all(copies, "group", split_axis=0, concat_axis=0, tiled=True)
-    rows_far = flip(rows_in, "tensor", 2)
-    rows_core = flip(rows_in, "tensor", 1)
-    rows_diag = flip(rows_far, "tensor", 1)
-
-    summary_all = lax.all_gather(summary, "tensor", axis=1, tiled=True)
-    logits = jnp.einsum("sbc,ce->sbe", summary_all, router, preferred_element_type=jnp.float32)
-    gate_prob = jax.nn.sigmoid(logits)
     chosen = jnp.sum(picked * gate_prob[:, :, None, :], -1)
     route_weight = (ROUTE_SCALE * chosen / jnp.sum(chosen, -1, keepdims=True)).astype(jnp.bfloat16)
     expert_weight = jnp.sum(picked * route_weight.astype(jnp.float32)[..., None], 2)
@@ -145,9 +183,9 @@
     active = jax.nn.silu(pre_act).astype(jnp.bfloat16)
     active = active.reshape(expert_count, places, columns)
     returned = lax.all_to_all(active, "expert", split_axis=0, concat_axis=0, tiled=True)
-    returned = returned.reshape(EXPERTS, step_count, slot_count, columns)
+    returned = returned.reshape(EXPERTS, slot_count, step_count, columns)
     expert_out = jnp.einsum(
-        "sbec,escf->sbf", combine, returned, preferred_element_type=jnp.float32
+        "sbec,ecsf->sbf", combine, returned, preferred_element_type=jnp.float32
     ).astype(jnp.bfloat16)
     return (first_new, second_new, attention_out, expert_out)
 

time: 138 us -> 159 us (1.15)
  the two profiles are of different devices: /device:TPU:2 before, /device:TPU:8 now
where the time goes in v3:
time: 159 us; the launch traced here: 158 us
  starting transfers between devices  68.4 us (43%)
  waiting for transfers between devices  45.6 us (29%)
  other arithmetic  12.8 us (8%)
  local copies, waits for them, and re-layouts  11.1 us (7%)
  matrix products  9.52 us (6%)
  blocking collectives  8.32 us (5%)
  between operations  1.81 us (1%)
    ppermute x3, waiting for transfers between devices, shift(): return lax.ppermute(value, 'expert', pairs)  28.8 us
    all_to_all x1, starting transfers between devices, local(): lax.all_to_all(parts, ('expert', 'tensor'), split_axis=0, concat_axis=0,...  16.1 us
    all_to_all x1, starting transfers between devices, local(): lax.all_to_all(active, 'expert', split_axis=0, concat_axis=0, tiled=True)  14.5 us
    all_to_all x1, waiting for transfers between devices, local(): lax.all_to_all(active, 'expert', split_axis=0, concat_axis=0, tiled=True)  13.2 us
    ppermute x4, starting transfers between devices, flip(): return lax.ppermute(value, axis, [(i, i ^ distance) for i in range(size)])  12.1 us
    ppermute x3, starting transfers between devices, shift(): return lax.ppermute(value, 'expert', pairs)  11.7 us
    all_to_all x1, starting transfers between devices, local(): lax.all_to_all(updated, 'expert', split_axis=0, concat_axis=0, tiled=True)  9.12 us
    all_gather x1, blocking collectives, local(): summary_all = lax.all_gather(summary, 'tensor', axis=1, tiled=True)  8.32 us
  transfers between devices with their start and end apart: 11, of which 5 were waited for; matrix products, arithmetic and copies ran while one was open for 16% of the time, Pallas kernels for 0%

profile of v3, /device:TPU:8, one launch (start us, length us, event | category | flops | bytes accessed | tf_op | source)
XLA Modules:
  0.0 157.7 jit_solution(12391874267698134403)
XLA Ops:
  0.7 0.8 fusion.64
  3.0 16.1 %all-to-all-start = ((bf16[16,4,1024]{2,1,0:T(4,128)(2,1)}), bf16[16,4,1024]{2,1,0:T(4,128)(2,1)S(1)}, u32[]{:S(2)}, u32[]{:S(2)}) async-start(bf16[16,4,1024]{2,1,0:T(4,128)(2,1)} %bitcast.2), calls=%async_computation | async-start | bytes 262144 | tf_op jit(solution)/shard_map/all_to_all | solution.py:118
  20.7 0.9 fusion.45
  21.6 1.1 fusion.35
  22.7 1.2 fusion.71
  23.9 0.9 fusion.72
  24.8 4.7 %fusion.17 = (bf16[32,28,256]{2,1,0:T(8,128)(2,1)}, f32[32,28,256]{2,1,0:T(8,128)}, f32[32,28,256]{2,1,0:T(8,128)}) fusion(bf16[32,28,256]{2,0,1:T(8,128)(2,1)S(1)} %copy-done.4, bf16[32,28,256]{2,0,1:T(8,128)(2,1)} %param.15, f32[32,28,256]{2,0,1:T(8,128)S(1)} %copy-done.3, f32[32,28,256]{2,0,1:T(8,128)} %param.16), kind=kLoop, calls=%fused_computation.32 | loop fusion | flops 4128768 | bytes 5046272 | tf_op jit(solution)/shard_map/convert_element_type | solution.py:31
  29.5 3.6 %all-to-all-done = bf16[16,4,1024]{2,1,0:T(4,128)(2,1)S(1)} async-done(((bf16[16,4,1024]{2,1,0:T(4,128)(2,1)}), bf16[16,4,1024]{2,1,0:T(4,128)(2,1)S(1)}, u32[]{:S(2)}, u32[]{:S(2)}) %all-to-all-start) | async-done | bytes 131104 | tf_op jit(solution)/shard_map/all_to_all | solution.py:118
  33.1 4.6 %collective-permute-start = (bf16[16,4,1024]{2,1,0:T(4,128)(2,1)S(1)}, bf16[16,4,1024]{2,1,0:T(4,128)(2,1)S(1)}, u32[]{:S(2)}, u32[]{:S(2)}) collective-permute-start(bf16[16,4,1024]{2,1,0:T(4,128)(2,1)S(1)} %all-to-all-done), channel_id=1, source_target_pairs={{0,64},{4,68},{8,72},{12,76},{16,80},{20,84},{24,88},{28,92},{32,9... | collective-permute-start | bytes 393224 | tf_op jit(solution)/shard_map/ppermute | solution.py:78
  37.7 9.1 %all-to-all-start.1 = ((bf16[32,28,256]{2,1,0:T(8,128)(2,1)}), bf16[32,28,256]{2,1,0:T(8,128)(2,1)S(1)}, u32[]{:S(2)}, u32[]{:S(2)}) async-start(bf16[32,28,256]{2,1,0:T(8,128)(2,1)} %get-tuple-element.17), calls=%async_computation.1 | async-start | bytes 1048576 | tf_op jit(solution)/shard_map/all_to_all | solution.py:134
  47.3 3.7 %collective-permute-start.3 = (bf16[2,16,4,1024]{3,2,1,0:T(4,128)(2,1)S(1)}, bf16[2,16,4,1024]{3,2,1,0:T(4,128)(2,1)S(1)}, u32[]{:S(2)}, u32[]{:S(2)}) collective-permute-start(bf16[2,16,4,1024]{3,2,1,0:T(4,128)(2,1)S(1)} %get-tuple-element.37), channel_id=1, source_target_pairs={{60,0},{0,4},{4,8},{8,12},{12,16},{16,20},{20,24},{24,28},{28,32},... | collective-permute-start | bytes 786440 | tf_op jit(solution)/shard_map/ppermute | solution.py:73
  51.0 4.6 %collective-permute-start.2 = (bf16[2,16,4,1024]{3,2,1,0:T(4,128)(2,1)S(1)}, bf16[2,16,4,1024]{3,2,1,0:T(4,128)(2,1)}, u32[]{:S(2)}, u32[]{:S(2)}) collective-permute-start(bf16[2,16,4,1024]{3,2,1,0:T(4,128)(2,1)S(1)} %get-tuple-element.37), channel_id=1, source_target_pairs={{8,0},{12,4},{16,8},{20,12},{24,16},{28,20},{32,24},{36,28},{40,32... | collective-permute-start | bytes 786440 | tf_op jit(solution)/shard_map/ppermute | solution.py:73
  55.6 3.4 %collective-permute-start.1 = (bf16[2,16,4,1024]{3,2,1,0:T(4,128)(2,1)S(1)}, bf16[2,16,4,1024]{3,2,1,0:T(4,128)(2,1)}, u32[]{:S(2)}, u32[]{:S(2)}) collective-permute-start(bf16[2,16,4,1024]{3,2,1,0:T(4,128)(2,1)S(1)} %get-tuple-element.37), channel_id=1, source_target_pairs={{4,0},{8,4},{12,8},{16,12},{20,16},{24,20},{28,24},{32,28},{36,32}... | collective-permute-start | bytes 786440 | tf_op jit(solution)/shard_map/ppermute | solution.py:73
  59.6 18.6 %collective-permute-done.3 = bf16[2,16,4,1024]{3,2,1,0:T(4,128)(2,1)S(1)} collective-permute-done((bf16[2,16,4,1024]{3,2,1,0:T(4,128)(2,1)S(1)}, bf16[2,16,4,1024]{3,2,1,0:T(4,128)(2,1)S(1)}, u32[]{:S(2)}, u32[]{:S(2)}) %collective-permute-start.3) | collective-permute-done | bytes 262176 | tf_op jit(solution)/shard_map/ppermute | solution.py:73
  78.2 6.4 %collective-permute-done.2 = bf16[2,16,4,1024]{3,2,1,0:T(4,128)(2,1)} collective-permute-done((bf16[2,16,4,1024]{3,2,1,0:T(4,128)(2,1)S(1)}, bf16[2,16,4,1024]{3,2,1,0:T(4,128)(2,1)}, u32[]{:S(2)}, u32[]{:S(2)}) %collective-permute-start.2) | collective-permute-done | bytes 262176 | tf_op jit(solution)/shard_map/ppermute | solution.py:73
  84.6 3.8 %collective-permute-done.1 = bf16[2,16,4,1024]{3,2,1,0:T(4,128)(2,1)} collective-permute-done((bf16[2,16,4,1024]{3,2,1,0:T(4,128)(2,1)S(1)}, bf16[2,16,4,1024]{3,2,1,0:T(4,128)(2,1)}, u32[]{:S(2)}, u32[]{:S(2)}) %collective-permute-start.1) | collective-permute-done | bytes 262176 | tf_op jit(solution)/shard_map/ppermute | solution.py:73
  88.4 2.0 %pad_maximum_fusion = bf16[4,2,16,4,1024]{4,3,2,1,0:T(4,128)(2,1)S(1)} fusion(bf16[1,2,16,4,1024]{4,3,2,1,0:T(4,128)(2,1)S(1)} %bitcast.150, bf16[1,2,16,4,1024]{4,3,2,1,0:T(4,128)(2,1)} %bitcast.28, bf16[1,2,16,4,1024]{4,3,2,1,0:T(4,128)(2,1)} %bitcast.27, bf16[1,2,16,4,1024]{4,3,2,1,0:T(4,128)(2,1)S(1)} %get-tuple-element.36), kind=kLoop, calls=%fused_computation.34 | loop fusion | flops 1572864 | bytes 2097152 | tf_op jit(solution)/shard_map/stack | solution.py:139
  90.9 1.0 copy-done.2
  92.0 1.4 broadcast_in_dim.39
  93.3 4.9 %all-to-all-start.2 = ((bf16[4,896,256]{2,1,0:T(8,128)(2,1)}), bf16[4,896,256]{2,1,0:T(8,128)(2,1)S(1)}, u32[]{:S(2)}, u32[]{:S(2)}) async-start(bf16[4,896,256]{2,1,0:T(8,128)(2,1)} %broadcast_in_dim.39), calls=%async_computation.2 | async-start | bytes 3670016 | tf_op jit(solution)/shard_map/all_to_all | solution.py:160
  98.9 1.1 convert_reduce_fusion
  100.2 2.6 %fusion = (bf16[2,4,4,4,896]{4,3,2,1,0:T(4,128)(2,1)S(1)}, bf16[2,4,4,4,896]{4,3,2,1,0:T(4,128)(2,1)S(1)}) fusion(f32[2,4,4,4,4]{4,3,2,1,0:T(4,128)S(1)} %get-tuple-element.39, bf16[2,4,4,4,4,1024]{5,4,3,2,1,0:T(4,128)(2,1)} %bitcast.144, f32[2,4,4,4,4]{4,3,2,1,0:T(4,128)S(1)} %get-tuple-element.38), kind=kLoop, calls=%fused_computation.2 | loop fusion | flops 2064384 | bytes 1380352 | tf_op jit(solution)/shard_map/reduce_sum | solution.py:154
  103.4 3.4 %collective-permute-start.5 = (bf16[256,896]{1,0:T(8,128)(2,1)S(1)}, bf16[256,896]{1,0:T(8,128)(2,1)}, u32[]{:S(2)}, u32[]{:S(2)}) collective-permute-start(bf16[256,896]{1,0:T(8,128)(2,1)S(1)} %reshape.244), channel_id=1, source_target_pairs={{0,2},{1,3},{2,0},{3,1},{4,6},{5,7},{6,4},{7,5},{8,10},{9,11},{10,... | collective-permute-start | bytes 1376264 | tf_op jit(solution)/shard_map/ppermute | solution.py:78
  107.0 1.9 %collective-permute-start.4 = (bf16[256,896]{1,0:T(8,128)(2,1)S(1)}, bf16[256,896]{1,0:T(8,128)(2,1)S(1)}, u32[]{:S(2)}, u32[]{:S(2)}) collective-permute-start(bf16[256,896]{1,0:T(8,128)(2,1)S(1)} %reshape.244), channel_id=1, source_target_pairs={{0,1},{1,0},{2,3},{3,2},{4,5},{5,4},{6,7},{7,6},{8,9},{9,8},{10,11... | collective-permute-start | bytes 1376264 | tf_op jit(solution)/shard_map/ppermute | solution.py:78
  109.0 8.3 %all_gather.3 = bf16[4,4,512]{2,0,1:T(4,128)(2,1)S(1)} all-gather(bf16[4,1,512]{2,0,1:T(4,128)(2,1)S(1)} %fusion.48), channel_id=1, replica_groups=mesh['group'=4,'expert'=32,'tensor'=4] {'tensor'}, dimensions={1}, use_global_device_ids=true | all-gather | bytes 20480 | tf_op jit(solution)/shard_map/all_gather | solution.py:165
  117.3 2.2 %collective-permute-start.6 = (bf16[256,896]{1,0:T(8,128)(2,1)}, bf16[256,896]{1,0:T(8,128)(2,1)}, u32[]{:S(2)}, u32[]{:S(2)}) collective-permute-start(bf16[256,896]{1,0:T(8,128)(2,1)} %collective-permute-done.5), channel_id=1, source_target_pairs={{0,1},{1,0},{2,3},{3,2},{4,5},{5,4},{6,7},{7,6},{8,9},{9,8},{10,11... | collective-permute-start | bytes 1376264 | tf_op jit(solution)/shard_map/ppermute | solution.py:78
  120.2 1.3 convolution_add_fusion.1
  121.5 2.1 %fusion.32 = bf16[32,8,256]{2,1,0:T(8,128)(2,1)} fusion(f32[256,256]{1,0:T(8,128)S(1)} %convolution_add_fusion.1, bf16[256,896]{1,0:T(8,128)(2,1)} %collective-permute-done.6, bf16[4,896,256]{2,1,0:T(8,128)(2,1)S(1)} %all-to-all-done.2, s32[]{:T(128)S(6)} %select_n.78), kind=kOutput, calls=%fused_computation.51 | convolution fusion | flops 117833728 | bytes 1310724 | tf_op jit(solution)/shard_map/dot_general | solution.py:182
  123.6 14.5 %all-to-all-start.3 = ((bf16[32,8,256]{2,1,0:T(8,128)(2,1)}), bf16[32,8,256]{2,1,0:T(8,128)(2,1)S(1)}, u32[]{:S(2)}, u32[]{:S(2)}) async-start(bf16[32,8,256]{2,1,0:T(8,128)(2,1)} %fusion.32), calls=%async_computation.3 | async-start | bytes 262144 | tf_op jit(solution)/shard_map/all_to_all | solution.py:185
  138.3 2.7 %copy.42 = f32[32,28,256]{2,0,1:T(8,128)} copy(f32[32,28,256]{2,1,0:T(8,128)} %get-tuple-element.33) | data formatting | bytes 1835008
  141.0 1.5 copy.43
  143.6 13.2 %all-to-all-done.3 = bf16[32,8,256]{2,1,0:T(8,128)(2,1)S(1)} async-done(((bf16[32,8,256]{2,1,0:T(8,128)(2,1)}), bf16[32,8,256]{2,1,0:T(8,128)(2,1)S(1)}, u32[]{:S(2)}, u32[]{:S(2)}) %all-to-all-start.3) | async-done | bytes 131104 | tf_op jit(solution)/shard_map/all_to_all | solution.py:185
  (66 shorter events, 8.3 us)
Async XLA Ops:
  0.6 22.0 %copy-start = (bf16[1,256,512]{2,1,0:T(8,128)(2,1)S(1)}, bf16[1,256,512]{2,1,0:T(8,128)(2,1)}, u32[]{:S(2)}) copy-start(bf16[1,256,512]{2,1,0:T(8,128)(2,1)} %param.21) | copy-start | bytes 786436
  0.6 24.1 %copy-start.4 = (bf16[32,28,256]{2,0,1:T(8,128)(2,1)S(1)}, bf16[32,28,256]{2,0,1:T(8,128)(2,1)}, u32[]{:S(2)}) copy-start(bf16[32,28,256]{2,0,1:T(8,128)(2,1)} %param.14) | copy-start | bytes 1376260
  0.7 24.1 %copy-start.3 = (f32[32,28,256]{2,0,1:T(8,128)S(1)}, f32[32,28,256]{2,0,1:T(8,128)}, u32[]{:S(2)}) copy-start(f32[32,28,256]{2,0,1:T(8,128)} %param.17) | copy-start | bytes 2752516
  3.0 30.1 %all-to-all-start = ((bf16[16,4,1024]{2,1,0:T(4,128)(2,1)}), bf16[16,4,1024]{2,1,0:T(4,128)(2,1)S(1)}, u32[]{:S(2)}, u32[]{:S(2)}) async-start(bf16[16,4,1024]{2,1,0:T(4,128)(2,1)} %bitcast.2), calls=%async_computation | async-start | bytes 262144 | tf_op jit(solution)/shard_map/all_to_all | solution.py:118
  29.5 29.8 %copy-start.6 = (bf16[4,1,512]{2,0,1:T(4,128)(2,1)S(1)}, bf16[4,1,512]{2,0,1:T(4,128)(2,1)}, u32[]{:S(2)}) copy-start(bf16[4,1,512]{2,0,1:T(4,128)(2,1)} %param.23) | copy-start | bytes 12292
  33.1 14.0 %collective-permute-start = (bf16[16,4,1024]{2,1,0:T(4,128)(2,1)S(1)}, bf16[16,4,1024]{2,1,0:T(4,128)(2,1)S(1)}, u32[]{:S(2)}, u32[]{:S(2)}) collective-permute-start(bf16[16,4,1024]{2,1,0:T(4,128)(2,1)S(1)} %all-to-all-done), channel_id=1, source_target_pairs={{0,64},{4,68},{8,72},{12,76},{16,80},{20,84},{24,88},{28,92},{32,9... | collective-permute-start | bytes 393224 | tf_op jit(solution)/shard_map/ppermute | solution.py:78
  37.7 54.1 %all-to-all-start.1 = ((bf16[32,28,256]{2,1,0:T(8,128)(2,1)}), bf16[32,28,256]{2,1,0:T(8,128)(2,1)S(1)}, u32[]{:S(2)}, u32[]{:S(2)}) async-start(bf16[32,28,256]{2,1,0:T(8,128)(2,1)} %get-tuple-element.17), calls=%async_computation.1 | async-start | bytes 1048576 | tf_op jit(solution)/shard_map/all_to_all | solution.py:134
  47.3 30.9 %collective-permute-start.3 = (bf16[2,16,4,1024]{3,2,1,0:T(4,128)(2,1)S(1)}, bf16[2,16,4,1024]{3,2,1,0:T(4,128)(2,1)S(1)}, u32[]{:S(2)}, u32[]{:S(2)}) collective-permute-start(bf16[2,16,4,1024]{3,2,1,0:T(4,128)(2,1)S(1)} %get-tuple-element.37), channel_id=1, source_target_pairs={{60,0},{0,4},{4,8},{8,12},{12,16},{16,20},{20,24},{24,28},{28,32},... | collective-permute-start | bytes 786440 | tf_op jit(solution)/shard_map/ppermute | solution.py:73
  51.0 33.6 %collective-permute-start.2 = (bf16[2,16,4,1024]{3,2,1,0:T(4,128)(2,1)S(1)}, bf16[2,16,4,1024]{3,2,1,0:T(4,128)(2,1)}, u32[]{:S(2)}, u32[]{:S(2)}) collective-permute-start(bf16[2,16,4,1024]{3,2,1,0:T(4,128)(2,1)S(1)} %get-tuple-element.37), channel_id=1, source_target_pairs={{8,0},{12,4},{16,8},{20,12},{24,16},{28,20},{32,24},{36,28},{40,32... | collective-permute-start | bytes 786440 | tf_op jit(solution)/shard_map/ppermute | solution.py:73
  55.6 32.8 %collective-permute-start.1 = (bf16[2,16,4,1024]{3,2,1,0:T(4,128)(2,1)S(1)}, bf16[2,16,4,1024]{3,2,1,0:T(4,128)(2,1)}, u32[]{:S(2)}, u32[]{:S(2)}) collective-permute-start(bf16[2,16,4,1024]{3,2,1,0:T(4,128)(2,1)S(1)} %get-tuple-element.37), channel_id=1, source_target_pairs={{4,0},{8,4},{12,8},{16,12},{20,16},{24,20},{28,24},{32,28},{36,32}... | collective-permute-start | bytes 786440 | tf_op jit(solution)/shard_map/ppermute | solution.py:73
  90.9 1.0 copy-start.2
  93.3 26.2 %all-to-all-start.2 = ((bf16[4,896,256]{2,1,0:T(8,128)(2,1)}), bf16[4,896,256]{2,1,0:T(8,128)(2,1)S(1)}, u32[]{:S(2)}, u32[]{:S(2)}) async-start(bf16[4,896,256]{2,1,0:T(8,128)(2,1)} %broadcast_in_dim.39), calls=%async_computation.2 | async-start | bytes 3670016 | tf_op jit(solution)/shard_map/all_to_all | solution.py:160
  103.4 13.9 %collective-permute-start.5 = (bf16[256,896]{1,0:T(8,128)(2,1)S(1)}, bf16[256,896]{1,0:T(8,128)(2,1)}, u32[]{:S(2)}, u32[]{:S(2)}) collective-permute-start(bf16[256,896]{1,0:T(8,128)(2,1)S(1)} %reshape.244), channel_id=1, source_target_pairs={{0,2},{1,3},{2,0},{3,1},{4,6},{5,7},{6,4},{7,5},{8,10},{9,11},{10,... | collective-permute-start | bytes 1376264 | tf_op jit(solution)/shard_map/ppermute | solution.py:78
  107.0 12.9 %collective-permute-start.4 = (bf16[256,896]{1,0:T(8,128)(2,1)S(1)}, bf16[256,896]{1,0:T(8,128)(2,1)S(1)}, u32[]{:S(2)}, u32[]{:S(2)}) collective-permute-start(bf16[256,896]{1,0:T(8,128)(2,1)S(1)} %reshape.244), channel_id=1, source_target_pairs={{0,1},{1,0},{2,3},{3,2},{4,5},{5,4},{6,7},{7,6},{8,9},{9,8},{10,11... | collective-permute-start | bytes 1376264 | tf_op jit(solution)/shard_map/ppermute | solution.py:78
  117.3 4.2 %collective-permute-start.6 = (bf16[256,896]{1,0:T(8,128)(2,1)}, bf16[256,896]{1,0:T(8,128)(2,1)}, u32[]{:S(2)}, u32[]{:S(2)}) collective-permute-start(bf16[256,896]{1,0:T(8,128)(2,1)} %collective-permute-done.5), channel_id=1, source_target_pairs={{0,1},{1,0},{2,3},{3,2},{4,5},{5,4},{6,7},{7,6},{8,9},{9,8},{10,11... | collective-permute-start | bytes 1376264 | tf_op jit(solution)/shard_map/ppermute | solution.py:78
  120.2 17.9 %copy-start.7 = (bf16[512,32]{0,1:T(8,128)(2,1)S(1)}, bf16[512,32]{0,1:T(8,128)(2,1)}, u32[]{:S(2)}) copy-start(bf16[512,32]{0,1:T(8,128)(2,1)} %param.27) | copy-start | bytes 98308
  121.5 19.5 %copy-start.1 = (f32[32,28,256]{2,1,0:T(8,128)S(1)}, f32[32,28,256]{2,1,0:T(8,128)}, u32[]{:S(2)}) copy-start(f32[32,28,256]{2,1,0:T(8,128)} %get-tuple-element.32) | copy-start | bytes 2752516
  123.6 33.2 %all-to-all-start.3 = ((bf16[32,8,256]{2,1,0:T(8,128)(2,1)}), bf16[32,8,256]{2,1,0:T(8,128)(2,1)S(1)}, u32[]{:S(2)}, u32[]{:S(2)}) async-start(bf16[32,8,256]{2,1,0:T(8,128)(2,1)} %fusion.32), calls=%async_computation.3 | async-start | bytes 262144 | tf_op jit(solution)/shard_map/all_to_all | solution.py:185
  138.3 4.9 %copy-start.5 = (s32[4,4,8]{2,1,0:T(4,128)S(1)}, s32[4,4,8]{2,1,0:T(4,128)}, u32[]{:S(2)}) copy-start(s32[4,4,8]{2,1,0:T(4,128)} %param.26) | copy-start | bytes 1540

commit v4 on v2

--- a/solution.py
+++ b/solution.py
@@ -65,11 +65,6 @@
     return (attention_out, summary.astype(jnp.bfloat16))
 
 
-def flip(value, axis, distance):
-    size = lax.axis_size(axis)
-    return lax.ppermute(value, axis, [(i, i ^ distance) for i in range(size)])
-
-
 def local(
     weights,
     gradients,
@@ -90,9 +85,13 @@
     expert_count, slab, columns = updated.shape
     step_count, _, width = hidden_in.shape
     quarter = width // 4
-    tensor = lax.axis_index("tensor")
-    rows_all = lax.all_gather(hidden_in, "tensor", axis=1, tiled=True)
-    block_rows = rows_all.shape[1]
+    my_part = lax.all_to_all(
+        jnp.swapaxes(hidden_in.reshape(step_count, 4, quarter), 0, 1),
+        "tensor",
+        split_axis=0,
+        concat_axis=0,
+        tiled=True,
+    )
     slot_count = 2
     places = step_count * slot_count
 
@@ -102,9 +101,8 @@
     slot_hit = (earlier[..., None] == jnp.arange(slot_count, dtype=jnp.float32)).astype(
         jnp.float32
     ) * per_expert[..., None]
-    my_part = lax.dynamic_slice_in_dim(rows_all, tensor * quarter, quarter, 2)
     outgoing = jnp.einsum(
-        "sbec,sbd->escd",
+        "sbec,bsd->escd",
         slot_hit.astype(jnp.bfloat16),
         my_part,
         preferred_element_type=jnp.float32,
@@ -120,17 +118,18 @@
         query_latent, query_rope, cache_latent, cache_rope, new_latent, new_rope, lengths
     )
     arrived = lax.all_to_all(payload, "expert", split_axis=0, concat_axis=0, tiled=True)
+    summary_all = lax.all_gather(summary, "tensor", axis=1, tiled=True)
+    arrived, summary_all = lax.optimization_barrier((arrived, summary_all))
     held = jnp.swapaxes(arrived[:, : 2 * slab].reshape(expert_count, 2, slab, 128), 1, 2)
     held = held.reshape(expert_count * slab, columns)
     rows_in = arrived[:, 2 * slab :].reshape(expert_count * places, quarter)
 
     copies = jnp.broadcast_to(held[None], (lax.axis_size("group"),) + held.shape)
     whole = lax.all_to_all(copies, "group", split_axis=0, concat_axis=0, tiled=True)
-    rows_far = flip(rows_in, "tensor", 2)
-    rows_core = flip(rows_in, "tensor", 1)
-    rows_diag = flip(rows_far, "tensor", 1)
+    half = rows_in.shape[0] // 2
+    spread = [lax.all_gather(rows_in[i * half : (i + 1) * half], "tensor") for i in range(2)]
+    rows_whole = jnp.concatenate([jnp.swapaxes(x, 0, 1).reshape(half, width) for x in spread], 0)
 
-    summary_all = lax.all_gather(summary, "tensor", axis=1, tiled=True)
     logits = jnp.einsum("sbc,ce->sbe", summary_all, router, preferred_element_type=jnp.float32)
     gate_prob = jax.nn.sigmoid(logits)
     chosen = jnp.sum(picked * gate_prob[:, :, None, :], -1)
@@ -138,10 +137,8 @@
     expert_weight = jnp.sum(picked * route_weight.astype(jnp.float32)[..., None], 2)
     combine = (slot_hit * expert_weight[..., None]).astype(jnp.bfloat16)
 
-    pre_act = jnp.zeros((expert_count * places, columns), jnp.float32)
-    for k, part in enumerate((rows_in, rows_core, rows_far, rows_diag)):
-        piece = lax.dynamic_index_in_dim(whole, jnp.bitwise_xor(tensor, k), 0, keepdims=False)
-        pre_act = pre_act + jnp.dot(part, piece, preferred_element_type=jnp.float32)
+    whole = whole.reshape(width, columns)
+    pre_act = jnp.dot(rows_whole, whole, preferred_element_type=jnp.float32)
     active = jax.nn.silu(pre_act).astype(jnp.bfloat16)
     active = active.reshape(expert_count, places, columns)
     returned = lax.all_to_all(active, "expert", split_axis=0, concat_axis=0, tiled=True)

time: 138 us -> 138 us (level)
  the two profiles are of different devices: /device:TPU:2 before, /device:TPU:8 now
where the time goes in v4:
time: 138 us; the launch traced here: 137 us
  waiting for transfers between devices  58.6 us (42%)
  starting transfers between devices  34.1 us (25%)
  blocking collectives  23.8 us (17%)
  local copies, waits for them, and re-layouts  9.06 us (7%)
  matrix products  5.38 us (4%)
  other arithmetic  4.85 us (4%)
  between operations  1.58 us (1%)
    all_to_all x1, waiting for transfers between devices, local(): lax.all_to_all(payload, 'expert', split_axis=0, concat_axis=0, tiled=True)  40.3 us
    all_gather x2, blocking collectives, local(): lax.all_gather(rows_in[i * half:(i + 1) * half], 'tensor')  18.6 us
    all_to_all x1, waiting for transfers between devices, local(): lax.all_to_all(active, 'expert', split_axis=0, concat_axis=0, tiled=True)  18.3 us
    all_to_all x1, starting transfers between devices, local(): lax.all_to_all(payload, 'expert', split_axis=0, concat_axis=0, tiled=True)  17.9 us
    all_to_all x1, starting transfers between devices, local(): lax.all_to_all(active, 'expert', split_axis=0, concat_axis=0, tiled=True)  7.85 us
    all_gather x1, blocking collectives, local(): summary_all = lax.all_gather(summary, 'tensor', axis=1, tiled=True)  5.18 us
    all_to_all x1, starting transfers between devices, local(): lax.all_to_all(copies, 'group', split_axis=0, concat_axis=0, tiled=True)  4.91 us
    convert_element_type x1, other arithmetic, adamw(): (old_weight - LEARN_RATE * (ratio + WEIGHT_DECAY * old_weight)).astype(jn...  3.78 us
  transfers between devices with their start and end apart: 4, of which 2 were waited for; matrix products, arithmetic and copies ran while one was open for 7% of the time, Pallas kernels for 0%

profile of v4, /device:TPU:8, one launch (start us, length us, event | category | flops | bytes accessed | tf_op | source)
XLA Modules:
  0.0 137.3 jit_solution(1607947686447975000)
XLA Ops:
  0.6 3.4 %all-to-all-start = ((bf16[4,4,896]{2,1,0:T(4,128)(2,1)}), bf16[4,4,896]{2,1,0:T(4,128)(2,1)S(1)}, u32[]{:S(2)}, u32[]{:S(2)}) async-start(bf16[4,4,896]{2,1,0:T(4,128)(2,1)} %bitcast.130), calls=%async_computation | async-start | bytes 57344 | tf_op jit(solution)/shard_map/all_to_all | solution.py:88
  4.1 3.8 %fusion.20 = (bf16[32,28,256]{2,0,1:T(8,128)(2,1)S(1)}, f32[32,28,256]{2,0,1:T(8,128)}, f32[32,28,256]{2,0,1:T(8,128)}) fusion(bf16[32,28,256]{2,0,1:T(8,128)(2,1)} %param.14, bf16[32,28,256]{2,0,1:T(8,128)(2,1)} %param.15, f32[32,28,256]{2,0,1:T(8,128)} %param.17, f32[32,28,256]{2,0,1:T(8,128)} %param.16), kind=kLoop, calls=%fused_computation.31 | loop fusion | flops 4128768 | bytes 5046272 | tf_op jit(solution)/shard_map/convert_element_type | solution.py:30
  8.2 0.3 fusion.4
  8.5 0.4 copy.45
  8.9 0.3 reshape.234
  9.4 1.3 copy.47
  10.7 17.9 %all-to-all-start.1 = ((bf16[32,112,128]{2,1,0:T(8,128)(2,1)}), bf16[32,112,128]{2,1,0:T(8,128)(2,1)S(1)}, u32[]{:S(2)}, u32[]{:S(2)}) async-start(bf16[32,112,128]{2,1,0:T(8,128)(2,1)} %copy.47), calls=%async_computation.1 | async-start | bytes 1835008 | tf_op jit(solution)/shard_map/all_to_all | solution.py:120
  29.5 0.2 fusion.29
  29.7 0.2 fusion.68
  30.0 0.3 fusion.67
  30.4 0.2 fusion.32
  30.6 0.2 convolution_bitcast_fusion
  30.8 0.3 fusion.66
  31.3 5.2 %all_gather.15 = bf16[4,4,512]{2,0,1:T(4,128)(2,1)S(1)} all-gather(bf16[4,1,512]{2,0,1:T(4,128)(2,1)S(1)} %fusion.44), channel_id=1, replica_groups=mesh['group'=4,'expert'=32,'tensor'=4] {'tensor'}, dimensions={1}, use_global_device_ids=true | all-gather | bytes 20480 | tf_op jit(solution)/shard_map/all_gather | solution.py:121
  36.4 40.3 %all-to-all-done.1 = bf16[32,112,128]{2,1,0:T(8,128)(2,1)S(1)} async-done(((bf16[32,112,128]{2,1,0:T(8,128)(2,1)}), bf16[32,112,128]{2,1,0:T(8,128)(2,1)S(1)}, u32[]{:S(2)}, u32[]{:S(2)}) %all-to-all-start.1) | async-done | bytes 917536 | tf_op jit(solution)/shard_map/all_to_all | solution.py:120
  76.7 0.2 copy.51
  77.0 0.5 copy.52
  77.5 1.4 broadcast_in_dim.33
  78.9 4.9 %all-to-all-start.2 = ((bf16[4,896,256]{2,1,0:T(8,128)(2,1)}), bf16[4,896,256]{2,1,0:T(8,128)(2,1)S(1)}, u32[]{:S(2)}, u32[]{:S(2)}) async-start(bf16[4,896,256]{2,1,0:T(8,128)(2,1)} %broadcast_in_dim.33), calls=%async_computation.2 | async-start | bytes 3670016 | tf_op jit(solution)/shard_map/all_to_all | solution.py:128
  83.8 0.7 convert_element_type.86
  84.6 0.9 all_gather.18
  85.5 9.2 %all_gather.19 = bf16[4,128,896]{2,1,0:T(8,128)(2,1)S(1)} all-gather(bf16[1,128,896]{2,1,0:T(8,128)(2,1)} %all_gather.18), channel_id=1, replica_groups=mesh['group'=4,'expert'=32,'tensor'=4] {'tensor'}, dimensions={0}, use_global_device_ids=true | all-gather | bytes 1146880 | tf_op jit(solution)/shard_map/all_gather | solution.py:130
  94.7 1.3 copy.50
  96.0 0.2 all_gather.16
  96.2 9.4 %all_gather.17 = bf16[4,128,896]{2,1,0:T(8,128)(2,1)S(1)} all-gather(bf16[1,128,896]{2,1,0:T(8,128)(2,1)S(1)} %all_gather.16), channel_id=1, replica_groups=mesh['group'=4,'expert'=32,'tensor'=4] {'tensor'}, dimensions={0}, use_global_device_ids=true | all-gather | bytes 1146880 | tf_op jit(solution)/shard_map/all_gather | solution.py:130
  105.7 1.3 copy.49
  107.0 2.8 %fusion.26 = bf16[32,8,256]{2,1,0:T(8,128)(2,1)} fusion(bf16[3584,256]{1,0:T(8,128)(2,1)S(1)} %bitcast.119, bf16[128,3584]{0,1:T(8,128)(2,1)} %bitcast.124, bf16[128,3584]{0,1:T(8,128)(2,1)} %bitcast.125), kind=kOutput, calls=%fused_computation.38 | convolution fusion | flops 473759744 | bytes 3801088 | tf_op jit(solution)/shard_map/dot_general | solution.py:141
  109.8 7.8 %all-to-all-start.3 = ((bf16[32,8,256]{2,1,0:T(8,128)(2,1)}), bf16[32,8,256]{2,1,0:T(8,128)(2,1)S(1)}, u32[]{:S(2)}, u32[]{:S(2)}) async-start(bf16[32,8,256]{2,1,0:T(8,128)(2,1)} %fusion.26), calls=%async_computation.3 | async-start | bytes 262144 | tf_op jit(solution)/shard_map/all_to_all | solution.py:144
  117.6 0.1 fusion.15
  117.8 0.2 select_reduce_fusion
  118.2 18.3 %all-to-all-done.3 = bf16[32,8,256]{2,1,0:T(8,128)(2,1)S(1)} async-done(((bf16[32,8,256]{2,1,0:T(8,128)(2,1)}), bf16[32,8,256]{2,1,0:T(8,128)(2,1)S(1)}, u32[]{:S(2)}, u32[]{:S(2)}) %all-to-all-start.3) | async-done | bytes 131104 | tf_op jit(solution)/shard_map/all_to_all | solution.py:144
  136.5 0.8 fusion.10
  (41 shorter events, 1.4 us)
Async XLA Ops:
  0.6 29.4 %copy-start = (bf16[1,256,512]{2,1,0:T(8,128)(2,1)S(1)}, bf16[1,256,512]{2,1,0:T(8,128)(2,1)}, u32[]{:S(2)}) copy-start(bf16[1,256,512]{2,1,0:T(8,128)(2,1)} %param.21) | copy-start | bytes 786436
  0.6 7.6 %all-to-all-start = ((bf16[4,4,896]{2,1,0:T(4,128)(2,1)}), bf16[4,4,896]{2,1,0:T(4,128)(2,1)S(1)}, u32[]{:S(2)}, u32[]{:S(2)}) async-start(bf16[4,4,896]{2,1,0:T(4,128)(2,1)} %bitcast.130), calls=%async_computation | async-start | bytes 57344 | tf_op jit(solution)/shard_map/all_to_all | solution.py:88
  4.1 3.8 %copy-start.2 = (s32[4,4,8]{2,1,0:T(4,128)S(1)}, s32[4,4,8]{2,1,0:T(4,128)}, u32[]{:S(2)}) copy-start(s32[4,4,8]{2,1,0:T(4,128)} %param.26) | copy-start | bytes 1540
  9.4 20.0 %copy-start.5 = (bf16[4,1,2048]{2,0,1:T(4,128)(2,1)S(1)}, bf16[4,1,2048]{2,0,1:T(4,128)(2,1)}, u32[]{:S(2)}) copy-start(bf16[4,1,2048]{2,0,1:T(4,128)(2,1)} %param.20) | copy-start | bytes 49156
  9.4 20.1 %copy-start.1 = (bf16[4,1,16384]{2,0,1:T(4,128)(2,1)S(1)}, bf16[4,1,16384]{2,0,1:T(4,128)(2,1)}, u32[]{:S(2)}) copy-start(bf16[4,1,16384]{2,0,1:T(4,128)(2,1)} %param.19) | copy-start | bytes 393220
  9.4 20.1 %copy-start.4 = (bf16[4,1,512]{2,0,1:T(4,128)(2,1)S(1)}, bf16[4,1,512]{2,0,1:T(4,128)(2,1)}, u32[]{:S(2)}) copy-start(bf16[4,1,512]{2,0,1:T(4,128)(2,1)} %param.23) | copy-start | bytes 12292
  9.4 20.3 %copy-start.7 = (bf16[4,1,64]{2,0,1:T(4,128)(2,1)S(1)}, bf16[4,1,64]{2,0,1:T(4,128)(2,1)}, u32[]{:S(2)}) copy-start(bf16[4,1,64]{2,0,1:T(4,128)(2,1)} %param.24) | copy-start | bytes 1540
  9.4 20.4 %copy-start.3 = (bf16[1,64,256]{2,1,0:T(8,128)(2,1)S(1)}, bf16[1,64,256]{2,1,0:T(8,128)(2,1)}, u32[]{:S(2)}) copy-start(bf16[1,64,256]{2,1,0:T(8,128)(2,1)} %param.22) | copy-start | bytes 98308
  10.7 66.0 %all-to-all-start.1 = ((bf16[32,112,128]{2,1,0:T(8,128)(2,1)}), bf16[32,112,128]{2,1,0:T(8,128)(2,1)S(1)}, u32[]{:S(2)}, u32[]{:S(2)}) async-start(bf16[32,112,128]{2,1,0:T(8,128)(2,1)} %copy.47), calls=%async_computation.1 | async-start | bytes 1835008 | tf_op jit(solution)/shard_map/all_to_all | solution.py:120
  78.9 28.0 %all-to-all-start.2 = ((bf16[4,896,256]{2,1,0:T(8,128)(2,1)}), bf16[4,896,256]{2,1,0:T(8,128)(2,1)S(1)}, u32[]{:S(2)}, u32[]{:S(2)}) async-start(bf16[4,896,256]{2,1,0:T(8,128)(2,1)} %broadcast_in_dim.33), calls=%async_computation.2 | async-start | bytes 3670016 | tf_op jit(solution)/shard_map/all_to_all | solution.py:128
  107.0 10.7 %copy-start.6 = (bf16[512,32]{0,1:T(8,128)(2,1)S(1)}, bf16[512,32]{0,1:T(8,128)(2,1)}, u32[]{:S(2)}) copy-start(bf16[512,32]{0,1:T(8,128)(2,1)} %param.27) | copy-start | bytes 98308
  109.8 26.7 %all-to-all-start.3 = ((bf16[32,8,256]{2,1,0:T(8,128)(2,1)}), bf16[32,8,256]{2,1,0:T(8,128)(2,1)S(1)}, u32[]{:S(2)}, u32[]{:S(2)}) async-start(bf16[32,8,256]{2,1,0:T(8,128)(2,1)} %fusion.26), calls=%async_computation.3 | async-start | bytes 262144 | tf_op jit(solution)/shard_map/all_to_all | solution.py:144

commit v5 on v4

--- a/solution.py
+++ b/solution.py
@@ -1,6 +1,8 @@
 import jax
 import jax.numpy as jnp
 from jax import lax
+from jax.experimental import pallas as pl
+from jax.experimental.pallas import tpu as pltpu
 from jax.sharding import PartitionSpec as P
 
 EXPERTS = 32
@@ -63,6 +65,53 @@
     summary = summary * lax.rsqrt(jnp.mean(summary * summary, -1, keepdims=True) + 1e-05)
     attention_out = mixture.reshape(step_count, row_count, HEADS * LAT).astype(jnp.bfloat16)
     return (attention_out, summary.astype(jnp.bfloat16))
+
+
+def flip(value, axis, distance):
+    size = lax.axis_size(axis)
+    return lax.ppermute(value, axis, [(i, i ^ distance) for i in range(size)])
+
+
+def expert_kernel(turn_ref, own, core, far, diag, whole, out, total):
+    step = pl.program_id(0)
+    for index, part in enumerate((own, core, far, diag)):
+
+        @pl.when(step == index)
+        def _(index=index, part=part):
+            product = jnp.dot(part[...], whole[0], preferred_element_type=jnp.float32)
+            total[...] = product if index == 0 else total[...] + product
+
+    @pl.when(step == 3)
+    def _():
+        value = total[...]
+        out[...] = (value / (1.0 + jnp.exp(-value))).astype(out.dtype)
+
+
+def expert_rows(parts, whole):
+    rows, quarter = parts[0].shape
+    columns = whole.shape[2]
+    return pl.pallas_call(
+        expert_kernel,
+        out_shape=jax.ShapeDtypeStruct((rows, columns), jnp.bfloat16),
+        grid_spec=pltpu.PrefetchScalarGridSpec(
+            num_scalar_prefetch=1,
+            grid=(4,),
+            in_specs=[pl.BlockSpec((rows, quarter), lambda k, turn: (0, 0))] * 4
+            + [
+                pl.BlockSpec(
+                    (1, quarter, columns), lambda k, turn: (jnp.bitwise_xor(k, turn[0]), 0, 0)
+                )
+            ],
+            out_specs=pl.BlockSpec((rows, columns), lambda k, turn: (0, 0)),
+            scratch_shapes=[pltpu.VMEM((rows, columns), jnp.float32)],
+        ),
+        compiler_params=pltpu.CompilerParams(vmem_limit_bytes=32 * 2**20),
+        cost_estimate=pl.CostEstimate(
+            flops=8 * rows * quarter * columns,
+            bytes_accessed=8 * quarter * (rows + columns),
+            transcendentals=rows * columns,
+        ),
+    )(lax.axis_index("tensor").reshape(1).astype(jnp.int32), *parts, whole)
 
 
 def local(
@@ -110,25 +159,25 @@
     outgoing = outgoing.reshape(expert_count, places * quarter // 128, 128)
     slabs = jnp.swapaxes(updated.reshape(expert_count, slab, 2, 128), 1, 2)
     slabs = slabs.reshape(expert_count, 2 * slab, 128)
+    outgoing, query_latent, query_rope, new_latent, new_rope = lax.optimization_barrier(
+        (outgoing, query_latent, query_rope, new_latent, new_rope)
+    )
     payload = jnp.concatenate([slabs, outgoing], 1)
-    payload, query_latent, query_rope, new_latent, new_rope = lax.optimization_barrier(
-        (payload, query_latent, query_rope, new_latent, new_rope)
-    )
     attention_out, summary = attend(
         query_latent, query_rope, cache_latent, cache_rope, new_latent, new_rope, lengths
     )
     arrived = lax.all_to_all(payload, "expert", split_axis=0, concat_axis=0, tiled=True)
     summary_all = lax.all_gather(summary, "tensor", axis=1, tiled=True)
-    arrived, summary_all = lax.optimization_barrier((arrived, summary_all))
     held = jnp.swapaxes(arrived[:, : 2 * slab].reshape(expert_count, 2, slab, 128), 1, 2)
     held = held.reshape(expert_count * slab, columns)
+    held, summary_all = lax.optimization_barrier((held, summary_all))
     rows_in = arrived[:, 2 * slab :].reshape(expert_count * places, quarter)
 
     copies = jnp.broadcast_to(held[None], (lax.axis_size("group"),) + held.shape)
     whole = lax.all_to_all(copies, "group", split_axis=0, concat_axis=0, tiled=True)
-    half = rows_in.shape[0] // 2
-    spread = [lax.all_gather(rows_in[i * half : (i + 1) * half], "tensor") for i in range(2)]
-    rows_whole = jnp.concatenate([jnp.swapaxes(x, 0, 1).reshape(half, width) for x in spread], 0)
+    rows_far = flip(rows_in, "tensor", 2)
+    rows_core = flip(rows_in, "tensor", 1)
+    rows_diag = flip(rows_far, "tensor", 1)
 
     logits = jnp.einsum("sbc,ce->sbe", summary_all, router, preferred_element_type=jnp.float32)
     gate_prob = jax.nn.sigmoid(logits)
@@ -137,9 +186,7 @@
     expert_weight = jnp.sum(picked * route_weight.astype(jnp.float32)[..., None], 2)
     combine = (slot_hit * expert_weight[..., None]).astype(jnp.bfloat16)
 
-    whole = whole.reshape(width, columns)
-    pre_act = jnp.dot(rows_whole, whole, preferred_element_type=jnp.float32)
-    active = jax.nn.silu(pre_act).astype(jnp.bfloat16)
+    active = expert_rows((rows_in, rows_core, rows_far, rows_diag), whole)
     active = active.reshape(expert_count, places, columns)
     returned = lax.all_to_all(active, "expert", split_axis=0, concat_axis=0, tiled=True)
     returned = returned.reshape(EXPERTS, step_count, slot_count, columns)

time: 138 us -> 135 us (0.978)
  the two profiles are of different devices: /device:TPU:8 before, /device:TPU:2 now
where the time goes in v5:
time: 135 us; the launch traced here: 134 us
  waiting for transfers between devices  69.2 us (51%)
  starting transfers between devices  41 us (30%)
  other arithmetic  5.77 us (4%)
  local copies, waits for them, and re-layouts  5.34 us (4%)
  blocking collectives  5.21 us (4%)
  matrix products  3.22 us (2%)
  Pallas kernels  3 us (2%)
  between operations  1.58 us (1%)
    all_to_all x1, waiting for transfers between devices, local(): lax.all_to_all(payload, 'expert', split_axis=0, concat_axis=0, tiled=True)  39.4 us
    all_to_all x1, waiting for transfers between devices, local(): lax.all_to_all(active, 'expert', split_axis=0, concat_axis=0, tiled=True)  16.8 us
    all_to_all x1, starting transfers between devices, local(): lax.all_to_all(payload, 'expert', split_axis=0, concat_axis=0, tiled=True)  12 us
    all_to_all x1, starting transfers between devices, local(): lax.all_to_all(jnp.swapaxes(hidden_in.reshape(step_count, 4, quarter), 0,...  9.28 us
    all_to_all x1, starting transfers between devices, local(): lax.all_to_all(active, 'expert', split_axis=0, concat_axis=0, tiled=True)  8.65 us
    ppermute x3, waiting for transfers between devices, flip(): return lax.ppermute(value, axis, [(i, i ^ distance) for i in range(size)])  7.77 us
    ppermute x3, starting transfers between devices, flip(): return lax.ppermute(value, axis, [(i, i ^ distance) for i in range(size)])  6.62 us
    all_to_all x1, waiting for transfers between devices, local(): lax.all_to_all(copies, 'group', split_axis=0, concat_axis=0, tiled=True)  5.34 us
  transfers between devices with their start and end apart: 7, of which 5 were waited for; matrix products, arithmetic and copies ran while one was open for 7% of the time, Pallas kernels for 0%

profile of v5, /device:TPU:2, one launch (start us, length us, event | category | flops | bytes accessed | tf_op | source)
XLA Modules:
  0.0 134.3 jit_solution(2183065252814811519)
XLA Ops:
  0.6 9.3 %all-to-all-start = ((bf16[4,4,896]{2,1,0:T(4,128)(2,1)}), bf16[4,4,896]{2,1,0:T(4,128)(2,1)S(1)}, u32[]{:S(2)}, u32[]{:S(2)}) async-start(bf16[4,4,896]{2,1,0:T(4,128)(2,1)} %bitcast.119), calls=%async_computation | async-start | bytes 57344 | tf_op jit(solution)/shard_map/all_to_all | solution.py:137
  9.9 3.8 %fusion.16 = (bf16[32,28,256]{2,0,1:T(8,128)(2,1)S(1)}, f32[32,28,256]{2,0,1:T(8,128)}, f32[32,28,256]{2,0,1:T(8,128)}) fusion(bf16[32,28,256]{2,0,1:T(8,128)(2,1)} %param.14, bf16[32,28,256]{2,0,1:T(8,128)(2,1)} %param.15, f32[32,28,256]{2,0,1:T(8,128)} %param.17, f32[32,28,256]{2,0,1:T(8,128)} %param.16), kind=kLoop, calls=%fused_computation.27 | loop fusion | flops 4128768 | bytes 5046272 | tf_op jit(solution)/shard_map/convert_element_type | solution.py:32
  14.1 0.2 copy.42
  14.3 0.3 fusion
  14.6 0.4 copy.40
  15.0 0.3 reshape.227
  15.3 1.0 pad_maximum_fusion
  16.3 12.0 %all-to-all-start.1 = ((bf16[32,112,128]{2,1,0:T(8,128)(2,1)}), bf16[32,112,128]{2,1,0:T(8,128)(2,1)S(1)}, u32[]{:S(2)}, u32[]{:S(2)}) async-start(bf16[32,112,128]{2,1,0:T(8,128)(2,1)} %pad_maximum_fusion), calls=%async_computation.1 | async-start | bytes 1835008 | tf_op jit(solution)/shard_map/all_to_all | solution.py:169
  29.1 0.2 fusion.20
  29.3 0.2 fusion.58
  29.6 0.3 fusion.57
  30.0 0.2 fusion.23
  30.2 0.2 convolution_bitcast_fusion
  30.4 0.9 fusion.56
  31.5 5.2 %all_gather.3 = bf16[4,4,512]{2,0,1:T(4,128)(2,1)S(1)} all-gather(bf16[4,1,512]{2,0,1:T(4,128)(2,1)S(1)} %fusion.35), channel_id=1, replica_groups=mesh['group'=4,'expert'=32,'tensor'=4] {'tensor'}, dimensions={1}, use_global_device_ids=true | all-gather | bytes 20480 | tf_op jit(solution)/shard_map/all_gather | solution.py:170
  36.7 39.4 %all-to-all-done.1 = bf16[32,112,128]{2,1,0:T(8,128)(2,1)S(1)} async-done(((bf16[32,112,128]{2,1,0:T(8,128)(2,1)}), bf16[32,112,128]{2,1,0:T(8,128)(2,1)S(1)}, u32[]{:S(2)}, u32[]{:S(2)}) %all-to-all-start.1) | async-done | bytes 917536 | tf_op jit(solution)/shard_map/all_to_all | solution.py:169
  76.2 0.5 copy.44
  76.8 1.4 %broadcast_in_dim.30 = bf16[4,896,256]{2,1,0:T(8,128)(2,1)} broadcast(bf16[896,256]{1,0:T(8,128)(2,1)S(1)} %bitcast.114), dimensions={1,2} | broadcast | bytes 2293760 | tf_op jit(solution)/shard_map/broadcast_in_dim | solution.py:176
  78.2 4.5 %all-to-all-start.2 = ((bf16[4,896,256]{2,1,0:T(8,128)(2,1)}), bf16[4,896,256]{2,1,0:T(8,128)(2,1)S(1)}, u32[]{:S(2)}, u32[]{:S(2)}) async-start(bf16[4,896,256]{2,1,0:T(8,128)(2,1)} %broadcast_in_dim.30), calls=%async_computation.2 | async-start | bytes 3670016 | tf_op jit(solution)/shard_map/all_to_all | solution.py:177
  82.6 0.5 reshape.241.own
  83.1 2.8 %collective-permute-start.1 = (bf16[256,896]{1,0:T(8,128)(2,1)S(1)}, bf16[256,896]{1,0:T(8,128)(2,1)S(1)}, u32[]{:S(2)}, u32[]{:S(2)}) collective-permute-start(bf16[256,896]{1,0:T(8,128)(2,1)S(1)} %reshape.241.own), channel_id=1, source_target_pairs={{0,2},{1,3},{2,0},{3,1},{4,6},{5,7},{6,4},{7,5},{8,10},{9,11},{10,... | collective-permute-start | bytes 1376264 | tf_op jit(solution)/shard_map/ppermute | solution.py:72
  85.9 1.9 %collective-permute-start = (bf16[256,896]{1,0:T(8,128)(2,1)S(1)}, bf16[256,896]{1,0:T(8,128)(2,1)S(1)}, u32[]{:S(2)}, u32[]{:S(2)}) collective-permute-start(bf16[256,896]{1,0:T(8,128)(2,1)S(1)} %reshape.241.own), channel_id=1, source_target_pairs={{0,1},{1,0},{2,3},{3,2},{4,5},{5,4},{6,7},{7,6},{8,9},{9,8},{10,11... | collective-permute-start | bytes 1376264 | tf_op jit(solution)/shard_map/ppermute | solution.py:72
  87.8 7.5 %collective-permute-done.1.far = bf16[256,896]{1,0:T(8,128)(2,1)S(1)} collective-permute-done((bf16[256,896]{1,0:T(8,128)(2,1)S(1)}, bf16[256,896]{1,0:T(8,128)(2,1)S(1)}, u32[]{:S(2)}, u32[]{:S(2)}) %collective-permute-start.1) | collective-permute-done | bytes 458784 | tf_op jit(solution)/shard_map/ppermute | solution.py:72
  95.3 1.9 %collective-permute-start.2 = (bf16[256,896]{1,0:T(8,128)(2,1)S(1)}, bf16[256,896]{1,0:T(8,128)(2,1)}, u32[]{:S(2)}, u32[]{:S(2)}) collective-permute-start(bf16[256,896]{1,0:T(8,128)(2,1)S(1)} %collective-permute-done.1.far), channel_id=1, source_target_pairs={{0,1},{1,0},{2,3},{3,2},{4,5},{5,4},{6,7},{7,6},{8,9},{9,8},{10,11... | collective-permute-start | bytes 1376264 | tf_op jit(solution)/shard_map/ppermute | solution.py:72
  97.3 1.6 %convert_element_type.81 = bf16[4,1,16384]{2,0,1:T(4,128)(2,1)} reshape(bf16[4,1,32,512]{3,2,0,1:T(8,128)(2,1)} %get-tuple-element.26) | data formatting | bytes 262144 | tf_op jit(solution)/shard_map/convert_element_type | solution.py:66
  98.9 0.3 collective-permute-done.2.diag
  99.2 5.3 %all-to-all-done.2.whole = bf16[4,896,256]{2,1,0:T(8,128)(2,1)S(1)} async-done(((bf16[4,896,256]{2,1,0:T(8,128)(2,1)}), bf16[4,896,256]{2,1,0:T(8,128)(2,1)S(1)}, u32[]{:S(2)}, u32[]{:S(2)}) %all-to-all-start.2) | async-done | bytes 1835040 | tf_op jit(solution)/shard_map/all_to_all | solution.py:177
  104.5 3.0 %shard_map.165 = bf16[256,256]{1,0:T(8,128)(2,1)} custom-call(s32[1]{0:T(128)} %bitcast.30.turn_ref, bf16[256,896]{1,0:T(8,128)(2,1)S(1)} %reshape.241.own, bf16[256,896]{1,0:T(8,128)(2,1)S(1)} %collective-permute-done.core, bf16[256,896]{1,0:T(8,128)(2,1)S(1)} %collective-permute-done.1.far, bf16[256,896]{1,0:T(8,128)(2,1)} %collective-permute-done.2.diag, ...), custom_call_target="tpu_custom_call" | custom-call | flops 469762048 | bytes 3670016 | tf_op jit(solution)/shard_map/pallas_call | solution.py:93
  107.5 8.6 %all-to-all-start.3 = ((bf16[32,8,256]{2,1,0:T(8,128)(2,1)}), bf16[32,8,256]{2,1,0:T(8,128)(2,1)S(1)}, u32[]{:S(2)}, u32[]{:S(2)}) async-start(bf16[32,8,256]{2,1,0:T(8,128)(2,1)} %bitcast.31), calls=%async_computation.3 | async-start | bytes 262144 | tf_op jit(solution)/shard_map/all_to_all | solution.py:191
  116.3 0.2 select_reduce_fusion
  116.7 16.8 %all-to-all-done.3 = bf16[32,8,256]{2,1,0:T(8,128)(2,1)S(1)} async-done(((bf16[32,8,256]{2,1,0:T(8,128)(2,1)}), bf16[32,8,256]{2,1,0:T(8,128)(2,1)S(1)}, u32[]{:S(2)}, u32[]{:S(2)}) %all-to-all-start.3) | async-done | bytes 131104 | tf_op jit(solution)/shard_map/all_to_all | solution.py:191
  133.5 0.8 fusion.6
  (40 shorter events, 1.4 us)
Async XLA Ops:
  0.6 29.0 %copy-start = (bf16[1,256,512]{2,1,0:T(8,128)(2,1)S(1)}, bf16[1,256,512]{2,1,0:T(8,128)(2,1)}, u32[]{:S(2)}) copy-start(bf16[1,256,512]{2,1,0:T(8,128)(2,1)} %param.21) | copy-start | bytes 786436
  0.6 13.6 %all-to-all-start = ((bf16[4,4,896]{2,1,0:T(4,128)(2,1)}), bf16[4,4,896]{2,1,0:T(4,128)(2,1)S(1)}, u32[]{:S(2)}, u32[]{:S(2)}) async-start(bf16[4,4,896]{2,1,0:T(4,128)(2,1)} %bitcast.119), calls=%async_computation | async-start | bytes 57344 | tf_op jit(solution)/shard_map/all_to_all | solution.py:137
  9.9 3.8 %copy-start.2 = (s32[4,4,8]{2,1,0:T(4,128)S(1)}, s32[4,4,8]{2,1,0:T(4,128)}, u32[]{:S(2)}) copy-start(s32[4,4,8]{2,1,0:T(4,128)} %param.26) | copy-start | bytes 1540
  15.3 13.7 %copy-start.5 = (bf16[4,1,2048]{2,0,1:T(4,128)(2,1)S(1)}, bf16[4,1,2048]{2,0,1:T(4,128)(2,1)}, u32[]{:S(2)}) copy-start(bf16[4,1,2048]{2,0,1:T(4,128)(2,1)} %param.20) | copy-start | bytes 49156
  15.3 13.8 %copy-start.1 = (bf16[4,1,16384]{2,0,1:T(4,128)(2,1)S(1)}, bf16[4,1,16384]{2,0,1:T(4,128)(2,1)}, u32[]{:S(2)}) copy-start(bf16[4,1,16384]{2,0,1:T(4,128)(2,1)} %param.19) | copy-start | bytes 393220
  15.3 13.8 %copy-start.4 = (bf16[4,1,512]{2,0,1:T(4,128)(2,1)S(1)}, bf16[4,1,512]{2,0,1:T(4,128)(2,1)}, u32[]{:S(2)}) copy-start(bf16[4,1,512]{2,0,1:T(4,128)(2,1)} %param.23) | copy-start | bytes 12292
  15.3 14.0 %copy-start.7 = (bf16[4,1,64]{2,0,1:T(4,128)(2,1)S(1)}, bf16[4,1,64]{2,0,1:T(4,128)(2,1)}, u32[]{:S(2)}) copy-start(bf16[4,1,64]{2,0,1:T(4,128)(2,1)} %param.24) | copy-start | bytes 1540
  15.3 14.2 %copy-start.3 = (bf16[1,64,256]{2,1,0:T(8,128)(2,1)S(1)}, bf16[1,64,256]{2,1,0:T(8,128)(2,1)}, u32[]{:S(2)}) copy-start(bf16[1,64,256]{2,1,0:T(8,128)(2,1)} %param.22) | copy-start | bytes 98308
  16.3 59.8 %all-to-all-start.1 = ((bf16[32,112,128]{2,1,0:T(8,128)(2,1)}), bf16[32,112,128]{2,1,0:T(8,128)(2,1)S(1)}, u32[]{:S(2)}, u32[]{:S(2)}) async-start(bf16[32,112,128]{2,1,0:T(8,128)(2,1)} %pad_maximum_fusion), calls=%async_computation.1 | async-start | bytes 1835008 | tf_op jit(solution)/shard_map/all_to_all | solution.py:169
  78.2 26.3 %all-to-all-start.2 = ((bf16[4,896,256]{2,1,0:T(8,128)(2,1)}), bf16[4,896,256]{2,1,0:T(8,128)(2,1)S(1)}, u32[]{:S(2)}, u32[]{:S(2)}) async-start(bf16[4,896,256]{2,1,0:T(8,128)(2,1)} %broadcast_in_dim.30), calls=%async_computation.2 | async-start | bytes 3670016 | tf_op jit(solution)/shard_map/all_to_all | solution.py:177
  83.1 12.2 %collective-permute-start.1 = (bf16[256,896]{1,0:T(8,128)(2,1)S(1)}, bf16[256,896]{1,0:T(8,128)(2,1)S(1)}, u32[]{:S(2)}, u32[]{:S(2)}) collective-permute-start(bf16[256,896]{1,0:T(8,128)(2,1)S(1)} %reshape.241.own), channel_id=1, source_target_pairs={{0,2},{1,3},{2,0},{3,1},{4,6},{5,7},{6,4},{7,5},{8,10},{9,11},{10,... | collective-permute-start | bytes 1376264 | tf_op jit(solution)/shard_map/ppermute | solution.py:72
  85.9 13.0 %collective-permute-start = (bf16[256,896]{1,0:T(8,128)(2,1)S(1)}, bf16[256,896]{1,0:T(8,128)(2,1)S(1)}, u32[]{:S(2)}, u32[]{:S(2)}) collective-permute-start(bf16[256,896]{1,0:T(8,128)(2,1)S(1)} %reshape.241.own), channel_id=1, source_target_pairs={{0,1},{1,0},{2,3},{3,2},{4,5},{5,4},{6,7},{7,6},{8,9},{9,8},{10,11... | collective-permute-start | bytes 1376264 | tf_op jit(solution)/shard_map/ppermute | solution.py:72
  95.3 3.8 %collective-permute-start.2 = (bf16[256,896]{1,0:T(8,128)(2,1)S(1)}, bf16[256,896]{1,0:T(8,128)(2,1)}, u32[]{:S(2)}, u32[]{:S(2)}) collective-permute-start(bf16[256,896]{1,0:T(8,128)(2,1)S(1)} %collective-permute-done.1.far), channel_id=1, source_target_pairs={{0,1},{1,0},{2,3},{3,2},{4,5},{5,4},{6,7},{7,6},{8,9},{9,8},{10,11... | collective-permute-start | bytes 1376264 | tf_op jit(solution)/shard_map/ppermute | solution.py:72
  104.5 11.7 %copy-start.6 = (bf16[512,32]{0,1:T(8,128)(2,1)S(1)}, bf16[512,32]{0,1:T(8,128)(2,1)}, u32[]{:S(2)}) copy-start(bf16[512,32]{0,1:T(8,128)(2,1)} %param.27) | copy-start | bytes 98308
  107.5 26.0 %all-to-all-start.3 = ((bf16[32,8,256]{2,1,0:T(8,128)(2,1)}), bf16[32,8,256]{2,1,0:T(8,128)(2,1)S(1)}, u32[]{:S(2)}, u32[]{:S(2)}) async-start(bf16[32,8,256]{2,1,0:T(8,128)(2,1)} %bitcast.31), calls=%async_computation.3 | async-start | bytes 262144 | tf_op jit(solution)/shard_map/all_to_all | solution.py:191

commit v6 on v5

--- a/solution.py
+++ b/solution.py
@@ -31,6 +31,36 @@
     ratio = first_new / BIAS_ONE / (jnp.sqrt(second_new / BIAS_TWO) + ADAM_EPS)
     updated = (old_weight - LEARN_RATE * (ratio + WEIGHT_DECAY * old_weight)).astype(jnp.bfloat16)
     return (first_new, second_new, updated)
+
+
+def adamw_kernel(weights, gradients, moment_one, moment_two, first_new, second_new, updated):
+    first_new[...], second_new[...], updated[...] = adamw(
+        weights[...], gradients[...], moment_one[...], moment_two[...]
+    )
+
+
+def adamw_rows(*operands):
+    operands = [jnp.swapaxes(x, 0, 1) for x in operands]
+    slab, expert_count, columns = operands[0].shape
+    depth = slab // 4
+    block = pl.BlockSpec((depth, expert_count, columns), lambda i: (i, 0, 0))
+    results = pl.pallas_call(
+        adamw_kernel,
+        out_shape=[
+            jax.ShapeDtypeStruct(operands[0].shape, kind)
+            for kind in (jnp.float32, jnp.float32, jnp.bfloat16)
+        ],
+        grid=(slab // depth,),
+        in_specs=[block] * 4,
+        out_specs=[block] * 3,
+        compiler_params=pltpu.CompilerParams(vmem_limit_bytes=16 * 2**20),
+        cost_estimate=pl.CostEstimate(
+            flops=20 * operands[0].size,
+            bytes_accessed=22 * operands[0].size,
+            transcendentals=2 * operands[0].size,
+        ),
+    )(*operands)
+    return [jnp.swapaxes(x, 0, 1) for x in results]
 
 
 def attend(query_latent, query_rope, cache_latent, cache_rope, new_latent, new_rope, lengths):
@@ -72,19 +102,15 @@
     return lax.ppermute(value, axis, [(i, i ^ distance) for i in range(size)])
 
 
-def expert_kernel(turn_ref, own, core, far, diag, whole, out, total):
-    step = pl.program_id(0)
-    for index, part in enumerate((own, core, far, diag)):
-
-        @pl.when(step == index)
-        def _(index=index, part=part):
-            product = jnp.dot(part[...], whole[0], preferred_element_type=jnp.float32)
-            total[...] = product if index == 0 else total[...] + product
-
-    @pl.when(step == 3)
-    def _():
-        value = total[...]
-        out[...] = (value / (1.0 + jnp.exp(-value))).astype(out.dtype)
+def expert_kernel(turn, own, core, far, diag, whole, out):
+    total = jnp.dot(own[...], whole[turn[0]], preferred_element_type=jnp.float32)
+    for index, part in ((1, core), (2, far), (3, diag)):
+        total = total + jnp.dot(
+            part[...],
+            whole[jnp.bitwise_xor(turn[0], index)],
+            preferred_element_type=jnp.float32,
+        )
+    out[...] = (total / (1.0 + jnp.exp(-total))).astype(out.dtype)
 
 
 def expert_rows(parts, whole):
@@ -93,19 +119,10 @@
     return pl.pallas_call(
         expert_kernel,
         out_shape=jax.ShapeDtypeStruct((rows, columns), jnp.bfloat16),
-        grid_spec=pltpu.PrefetchScalarGridSpec(
-            num_scalar_prefetch=1,
-            grid=(4,),
-            in_specs=[pl.BlockSpec((rows, quarter), lambda k, turn: (0, 0))] * 4
-            + [
-                pl.BlockSpec(
-                    (1, quarter, columns), lambda k, turn: (jnp.bitwise_xor(k, turn[0]), 0, 0)
-                )
-            ],
-            out_specs=pl.BlockSpec((rows, columns), lambda k, turn: (0, 0)),
-            scratch_shapes=[pltpu.VMEM((rows, columns), jnp.float32)],
-        ),
-        compiler_params=pltpu.CompilerParams(vmem_limit_bytes=32 * 2**20),
+        in_specs=[pl.BlockSpec(memory_space=pltpu.SMEM)]
+        + [pl.BlockSpec(memory_space=pltpu.VMEM)] * 5,
+        out_specs=pl.BlockSpec(memory_space=pltpu.VMEM),
+        compiler_params=pltpu.CompilerParams(vmem_limit_bytes=16 * 2**20),
         cost_estimate=pl.CostEstimate(
             flops=8 * rows * quarter * columns,
             bytes_accessed=8 * quarter * (rows + columns),
@@ -130,7 +147,7 @@
     expert_ids,
     router,
 ):
-    first_new, second_new, updated = adamw(weights, gradients, moment_one, moment_two)
+    first_new, second_new, updated = adamw_rows(weights, gradients, moment_one, moment_two)
     expert_count, slab, columns = updated.shape
     step_count, _, width = hidden_in.shape
     quarter = width // 4
@@ -150,13 +167,18 @@
     slot_hit = (earlier[..., None] == jnp.arange(slot_count, dtype=jnp.float32)).astype(
         jnp.float32
     ) * per_expert[..., None]
-    outgoing = jnp.einsum(
-        "sbec,bsd->escd",
-        slot_hit.astype(jnp.bfloat16),
-        my_part,
+    same_step = jnp.eye(step_count, dtype=jnp.float32)
+    placed = jnp.transpose(slot_hit, (1, 0, 2, 3))[:, :, :, None] * same_step[:, None, :, None]
+    placed = placed.reshape(4 * step_count, expert_count * places)
+    outgoing = lax.dot_general(
+        placed.astype(jnp.bfloat16),
+        my_part.reshape(4 * step_count, quarter),
+        (((0,), (0,)), ((), ())),
         preferred_element_type=jnp.float32,
     ).astype(jnp.bfloat16)
-    outgoing = outgoing.reshape(expert_count, places * quarter // 128, 128)
+    lanes = quarter // 128
+    outgoing = jnp.swapaxes(outgoing.reshape(expert_count, places, lanes, 128), 1, 2)
+    outgoing = outgoing.reshape(expert_count, places * lanes, 128)
     slabs = jnp.swapaxes(updated.reshape(expert_count, slab, 2, 128), 1, 2)
     slabs = slabs.reshape(expert_count, 2 * slab, 128)
     outgoing, query_latent, query_rope, new_latent, new_rope = lax.optimization_barrier(
@@ -171,7 +193,8 @@
     held = jnp.swapaxes(arrived[:, : 2 * slab].reshape(expert_count, 2, slab, 128), 1, 2)
     held = held.reshape(expert_count * slab, columns)
     held, summary_all = lax.optimization_barrier((held, summary_all))
-    rows_in = arrived[:, 2 * slab :].reshape(expert_count * places, quarter)
+    rows_in = arrived[:, 2 * slab :].reshape(expert_count, lanes, places, 128)
+    rows_in = jnp.swapaxes(rows_in, 1, 2).reshape(expert_count * places, quarter)
 
     copies = jnp.broadcast_to(held[None], (lax.axis_size("group"),) + held.shape)
     whole = lax.all_to_all(copies, "group", split_axis=0, concat_axis=0, tiled=True)
@@ -184,15 +207,19 @@
     chosen = jnp.sum(picked * gate_prob[:, :, None, :], -1)
     route_weight = (ROUTE_SCALE * chosen / jnp.sum(chosen, -1, keepdims=True)).astype(jnp.bfloat16)
     expert_weight = jnp.sum(picked * route_weight.astype(jnp.float32)[..., None], 2)
-    combine = (slot_hit * expert_weight[..., None]).astype(jnp.bfloat16)
+    share = jnp.transpose(expert_weight, (1, 0, 2))[..., None, None]
+    combine = placed.reshape(4, step_count, expert_count, step_count, slot_count) * share
+    combine = combine.reshape(4 * step_count, expert_count * places).astype(jnp.bfloat16)
 
     active = expert_rows((rows_in, rows_core, rows_far, rows_diag), whole)
     active = active.reshape(expert_count, places, columns)
     returned = lax.all_to_all(active, "expert", split_axis=0, concat_axis=0, tiled=True)
-    returned = returned.reshape(EXPERTS, step_count, slot_count, columns)
-    expert_out = jnp.einsum(
-        "sbec,escf->sbf", combine, returned, preferred_element_type=jnp.float32
+    expert_out = jnp.dot(
+        combine,
+        returned.reshape(expert_count * places, columns),
+        preferred_element_type=jnp.float32,
     ).astype(jnp.bfloat16)
+    expert_out = jnp.swapaxes(expert_out.reshape(4, step_count, columns), 0, 1)
     return (first_new, second_new, attention_out, expert_out)
 
 

time: 135 us -> 139 us (1.030)
  local copies, waits for them, and re-layouts: 5.34 us -> 11.6 us
  other arithmetic: 5.77 us -> 2.91 us
  Pallas kernels: 3 us -> 4.47 us
    unnamed x17 -> x28, local copies, waits for them, and re-layouts: 0.12 us -> 5.22 us
    convert_element_type x1 -> x3, other arithmetic: 3.79 us -> 1.13 us  [the longest x1 1.04 us: local(): combine.reshape(4 * step_count, expert_count * places).astype(jnp.bfloat16)]
    pallas_call x0 -> x1, Pallas kernels: none -> 2.08 us  [adamw_rows(): pl.pallas_call(adamw_kernel, out_shape=[jax.ShapeDtypeStruct(operands[0]....]
  transfers between devices with their start and end apart: 7 -> 7, of which waited for: 5 -> 4; matrix products, arithmetic and copies ran while one was open for 7% -> 5% of each run, Pallas kernels for 0% -> 2%
where the time goes in v6:
time: 139 us; the launch traced here: 138 us
  waiting for transfers between devices  68.3 us (49%)
  starting transfers between devices  41.1 us (30%)
  local copies, waits for them, and re-layouts  11.6 us (8%)
  blocking collectives  5.21 us (4%)
  Pallas kernels  4.47 us (3%)
  other arithmetic  2.91 us (2%)
  matrix products  2.48 us (2%)
  between operations  1.63 us (1%)
    all_to_all x1, waiting for transfers between devices, local(): lax.all_to_all(payload, 'expert', split_axis=0, concat_axis=0, tiled=True)  39.4 us
    all_to_all x1, waiting for transfers between devices, local(): lax.all_to_all(active, 'expert', split_axis=0, concat_axis=0, tiled=True)  15.8 us
    all_to_all x1, starting transfers between devices, local(): lax.all_to_all(payload, 'expert', split_axis=0, concat_axis=0, tiled=True)  12 us
    all_to_all x1, starting transfers between devices, local(): lax.all_to_all(jnp.swapaxes(hidden_in.reshape(step_count, 4, quarter), 0,...  9.28 us
    all_to_all x1, starting transfers between devices, local(): lax.all_to_all(active, 'expert', split_axis=0, concat_axis=0, tiled=True)  8.64 us
    ppermute x3, waiting for transfers between devices, flip(): return lax.ppermute(value, axis, [(i, i ^ distance) for i in range(size)])  7.47 us
    ppermute x3, starting transfers between devices, flip(): return lax.ppermute(value, axis, [(i, i ^ distance) for i in range(size)])  6.64 us
    all_to_all x1, waiting for transfers between devices, local(): lax.all_to_all(copies, 'group', split_axis=0, concat_axis=0, tiled=True)  5.72 us
  transfers between devices with their start and end apart: 7, of which 4 were waited for; matrix products, arithmetic and copies ran while one was open for 5% of the time, Pallas kernels for 2%

profile of v6, /device:TPU:2, one launch (start us, length us, event | category | flops | bytes accessed | tf_op | source)
XLA Modules:
  0.0 137.8 jit_solution(6904575416018929302)
XLA Ops:
  0.6 9.3 %all-to-all-start = ((bf16[4,4,896]{2,1,0:T(4,128)(2,1)}), bf16[4,4,896]{2,1,0:T(4,128)(2,1)S(1)}, u32[]{:S(2)}, u32[]{:S(2)}) async-start(bf16[4,4,896]{2,1,0:T(4,128)(2,1)} %bitcast.153), calls=%async_computation | async-start | bytes 57344 | tf_op jit(solution)/shard_map/all_to_all | solution.py:154
  9.9 0.8 convert_reduce_fusion
  11.0 1.2 copy-done.1
  12.2 1.2 copy-done.2
  13.4 1.0 copy-done.3
  14.4 1.0 copy-done.4
  15.4 2.1 %shard_map.165 = (f32[28,32,256]{2,1,0:T(8,128)}, f32[28,32,256]{2,1,0:T(8,128)}, bf16[28,32,256]{2,1,0:T(8,128)(2,1)S(1)}) custom-call(bf16[28,32,256]{2,1,0:T(8,128)(2,1)S(1)} %bitcast.142, bf16[28,32,256]{2,1,0:T(8,128)(2,1)S(1)} %bitcast.143, f32[28,32,256]{2,1,0:T(8,128)S(1)} %bitcast.140, f32[28,32,256]{2,1,0:T(8,128)S(1)} %bitcast.141), custom_call_target="tpu_custom_call" | custom-call | flops 4587520 | bytes 5046272 | tf_op jit(solution)/shard_map/pallas_call | solution.py:47
  17.6 0.6 copy-done.5
  18.6 0.2 fusion
  19.1 1.3 copy.45
  20.3 12.0 %all-to-all-start.1 = ((bf16[32,112,128]{2,1,0:T(8,128)(2,1)}), bf16[32,112,128]{2,1,0:T(8,128)(2,1)S(1)}, u32[]{:S(2)}, u32[]{:S(2)}) async-start(bf16[32,112,128]{2,1,0:T(8,128)(2,1)} %copy.45), calls=%async_computation.1 | async-start | bytes 1835008 | tf_op jit(solution)/shard_map/all_to_all | solution.py:191
  33.1 0.2 fusion.15
  33.7 0.3 fusion.40
  34.2 0.2 convolution_bitcast_fusion
  34.4 0.9 fusion.39
  35.5 5.2 %all_gather.3 = bf16[4,4,512]{2,0,1:T(4,128)(2,1)S(1)} all-gather(bf16[4,1,512]{2,0,1:T(4,128)(2,1)S(1)} %fusion.29), channel_id=1, replica_groups=mesh['group'=4,'expert'=32,'tensor'=4] {'tensor'}, dimensions={1}, use_global_device_ids=true | all-gather | bytes 20480 | tf_op jit(solution)/shard_map/all_gather | solution.py:192
  40.7 39.4 %all-to-all-done.1 = bf16[32,112,128]{2,1,0:T(8,128)(2,1)S(1)} async-done(((bf16[32,112,128]{2,1,0:T(8,128)(2,1)}), bf16[32,112,128]{2,1,0:T(8,128)(2,1)S(1)}, u32[]{:S(2)}, u32[]{:S(2)}) %all-to-all-start.1) | async-done | bytes 917536 | tf_op jit(solution)/shard_map/all_to_all | solution.py:191
  80.3 0.5 copy.47
  80.8 1.4 broadcast_in_dim.30
  82.2 4.6 %all-to-all-start.2 = ((bf16[4,896,256]{2,1,0:T(8,128)(2,1)}), bf16[4,896,256]{2,1,0:T(8,128)(2,1)S(1)}, u32[]{:S(2)}, u32[]{:S(2)}) async-start(bf16[4,896,256]{2,1,0:T(8,128)(2,1)} %broadcast_in_dim.30), calls=%async_computation.2 | async-start | bytes 3670016 | tf_op jit(solution)/shard_map/all_to_all | solution.py:200
  86.8 2.8 %collective-permute-start.1 = (bf16[256,896]{1,0:T(8,128)(2,1)S(1)}, bf16[256,896]{1,0:T(8,128)(2,1)S(1)}, u32[]{:S(2)}, u32[]{:S(2)}) collective-permute-start(bf16[256,896]{1,0:T(8,128)(2,1)S(1)} %get-tuple-element.26.own), channel_id=1, source_target_pairs={{0,2},{1,3},{2,0},{3,1},{4,6},{5,7},{6,4},{7,5},{8,10},{9,11},{10,... | collective-permute-start | bytes 1376264 | tf_op jit(solution)/shard_map/ppermute | solution.py:102
  89.6 1.9 %collective-permute-start = (bf16[256,896]{1,0:T(8,128)(2,1)S(1)}, bf16[256,896]{1,0:T(8,128)(2,1)S(1)}, u32[]{:S(2)}, u32[]{:S(2)}) collective-permute-start(bf16[256,896]{1,0:T(8,128)(2,1)S(1)} %get-tuple-element.26.own), channel_id=1, source_target_pairs={{0,1},{1,0},{2,3},{3,2},{4,5},{5,4},{6,7},{7,6},{8,9},{9,8},{10,11... | collective-permute-start | bytes 1376264 | tf_op jit(solution)/shard_map/ppermute | solution.py:102
  91.5 7.5 %collective-permute-done.1.far = bf16[256,896]{1,0:T(8,128)(2,1)S(1)} collective-permute-done((bf16[256,896]{1,0:T(8,128)(2,1)S(1)}, bf16[256,896]{1,0:T(8,128)(2,1)S(1)}, u32[]{:S(2)}, u32[]{:S(2)}) %collective-permute-start.1) | collective-permute-done | bytes 458784 | tf_op jit(solution)/shard_map/ppermute | solution.py:102
  99.0 1.9 %collective-permute-start.2 = (bf16[256,896]{1,0:T(8,128)(2,1)S(1)}, bf16[256,896]{1,0:T(8,128)(2,1)}, u32[]{:S(2)}, u32[]{:S(2)}) collective-permute-start(bf16[256,896]{1,0:T(8,128)(2,1)S(1)} %collective-permute-done.1.far), channel_id=1, source_target_pairs={{0,1},{1,0},{2,3},{3,2},{4,5},{5,4},{6,7},{7,6},{8,9},{9,8},{10,11... | collective-permute-start | bytes 1376264 | tf_op jit(solution)/shard_map/ppermute | solution.py:102
  100.9 1.6 %convert_element_type.94 = bf16[4,1,16384]{2,0,1:T(4,128)(2,1)} reshape(bf16[4,1,32,512]{3,2,0,1:T(8,128)(2,1)} %get-tuple-element.29) | data formatting | bytes 262144 | tf_op jit(solution)/shard_map/convert_element_type | solution.py:96
  102.7 0.2 select_reduce_fusion
  102.9 5.7 %all-to-all-done.2.whole = bf16[4,896,256]{2,1,0:T(8,128)(2,1)S(1)} async-done(((bf16[4,896,256]{2,1,0:T(8,128)(2,1)}), bf16[4,896,256]{2,1,0:T(8,128)(2,1)S(1)}, u32[]{:S(2)}, u32[]{:S(2)}) %all-to-all-start.2) | async-done | bytes 1835040 | tf_op jit(solution)/shard_map/all_to_all | solution.py:200
  108.7 2.4 %shard_map.166 = bf16[256,256]{1,0:T(8,128)(2,1)} custom-call(s32[1]{0:T(128)} %bitcast.41.turn, bf16[256,896]{1,0:T(8,128)(2,1)S(1)} %get-tuple-element.26.own, bf16[256,896]{1,0:T(8,128)(2,1)S(1)} %collective-permute-done.core, bf16[256,896]{1,0:T(8,128)(2,1)S(1)} %collective-permute-done.1.far, bf16[256,896]{1,0:T(8,128)(2,1)} %collective-permute-done.2.diag, ...), custom_call_target="tpu_custom_call" | custom-call | flops 469762048 | bytes 3670016 | tf_op jit(solution)/shard_map/pallas_call | solution.py:119
  111.1 8.6 %all-to-all-start.3 = ((bf16[32,8,256]{2,1,0:T(8,128)(2,1)}), bf16[32,8,256]{2,1,0:T(8,128)(2,1)S(1)}, u32[]{:S(2)}, u32[]{:S(2)}) async-start(bf16[32,8,256]{2,1,0:T(8,128)(2,1)} %bitcast.47), calls=%async_computation.3 | async-start | bytes 262144 | tf_op jit(solution)/shard_map/all_to_all | solution.py:216
  120.0 1.0 fusion.12
  121.2 15.8 %all-to-all-done.3 = bf16[32,8,256]{2,1,0:T(8,128)(2,1)S(1)} async-done(((bf16[32,8,256]{2,1,0:T(8,128)(2,1)}), bf16[32,8,256]{2,1,0:T(8,128)(2,1)S(1)}, u32[]{:S(2)}, u32[]{:S(2)}) %all-to-all-start.3) | async-done | bytes 131104 | tf_op jit(solution)/shard_map/all_to_all | solution.py:216
  137.2 0.6 copy.71
  (58 shorter events, 2.7 us)
Async XLA Ops:
  0.6 33.0 %copy-start = (bf16[1,256,512]{2,1,0:T(8,128)(2,1)S(1)}, bf16[1,256,512]{2,1,0:T(8,128)(2,1)}, u32[]{:S(2)}) copy-start(bf16[1,256,512]{2,1,0:T(8,128)(2,1)} %param.21) | copy-start | bytes 786436
  0.6 17.9 %all-to-all-start = ((bf16[4,4,896]{2,1,0:T(4,128)(2,1)}), bf16[4,4,896]{2,1,0:T(4,128)(2,1)S(1)}, u32[]{:S(2)}, u32[]{:S(2)}) async-start(bf16[4,4,896]{2,1,0:T(4,128)(2,1)} %bitcast.153), calls=%async_computation | async-start | bytes 57344 | tf_op jit(solution)/shard_map/all_to_all | solution.py:154
  11.0 1.2 copy-start.1
  12.2 1.2 copy-start.2
  13.4 1.0 copy-start.3
  14.4 1.0 copy-start.4
  17.6 0.7 copy-start.5
  19.0 14.0 %copy-start.10 = (bf16[4,1,2048]{2,0,1:T(4,128)(2,1)S(1)}, bf16[4,1,2048]{2,0,1:T(4,128)(2,1)}, u32[]{:S(2)}) copy-start(bf16[4,1,2048]{2,0,1:T(4,128)(2,1)} %param.20) | copy-start | bytes 49156
  19.0 14.1 %copy-start.6 = (bf16[4,1,16384]{2,0,1:T(4,128)(2,1)S(1)}, bf16[4,1,16384]{2,0,1:T(4,128)(2,1)}, u32[]{:S(2)}) copy-start(bf16[4,1,16384]{2,0,1:T(4,128)(2,1)} %param.19) | copy-start | bytes 393220
  19.0 14.1 %copy-start.9 = (bf16[4,1,512]{2,0,1:T(4,128)(2,1)S(1)}, bf16[4,1,512]{2,0,1:T(4,128)(2,1)}, u32[]{:S(2)}) copy-start(bf16[4,1,512]{2,0,1:T(4,128)(2,1)} %param.23) | copy-start | bytes 12292
  19.0 14.3 %copy-start.12 = (bf16[4,1,64]{2,0,1:T(4,128)(2,1)S(1)}, bf16[4,1,64]{2,0,1:T(4,128)(2,1)}, u32[]{:S(2)}) copy-start(bf16[4,1,64]{2,0,1:T(4,128)(2,1)} %param.24) | copy-start | bytes 1540
  19.0 14.5 %copy-start.8 = (bf16[1,64,256]{2,1,0:T(8,128)(2,1)S(1)}, bf16[1,64,256]{2,1,0:T(8,128)(2,1)}, u32[]{:S(2)}) copy-start(bf16[1,64,256]{2,1,0:T(8,128)(2,1)} %param.22) | copy-start | bytes 98308
  20.3 59.8 %all-to-all-start.1 = ((bf16[32,112,128]{2,1,0:T(8,128)(2,1)}), bf16[32,112,128]{2,1,0:T(8,128)(2,1)S(1)}, u32[]{:S(2)}, u32[]{:S(2)}) async-start(bf16[32,112,128]{2,1,0:T(8,128)(2,1)} %copy.45), calls=%async_computation.1 | async-start | bytes 1835008 | tf_op jit(solution)/shard_map/all_to_all | solution.py:191
  82.2 20.4 %copy-start.11 = (bf16[512,32]{0,1:T(8,128)(2,1)S(1)}, bf16[512,32]{0,1:T(8,128)(2,1)}, u32[]{:S(2)}) copy-start(bf16[512,32]{0,1:T(8,128)(2,1)} %param.27) | copy-start | bytes 98308
  82.2 20.5 %copy-start.7 = (s32[4,4,8]{2,1,0:T(4,128)S(1)}, s32[4,4,8]{2,1,0:T(4,128)}, u32[]{:S(2)}) copy-start(s32[4,4,8]{2,1,0:T(4,128)} %param.26) | copy-start | bytes 1540
  82.2 26.5 %all-to-all-start.2 = ((bf16[4,896,256]{2,1,0:T(8,128)(2,1)}), bf16[4,896,256]{2,1,0:T(8,128)(2,1)S(1)}, u32[]{:S(2)}, u32[]{:S(2)}) async-start(bf16[4,896,256]{2,1,0:T(8,128)(2,1)} %broadcast_in_dim.30), calls=%async_computation.2 | async-start | bytes 3670016 | tf_op jit(solution)/shard_map/all_to_all | solution.py:200
  86.8 12.2 %collective-permute-start.1 = (bf16[256,896]{1,0:T(8,128)(2,1)S(1)}, bf16[256,896]{1,0:T(8,128)(2,1)S(1)}, u32[]{:S(2)}, u32[]{:S(2)}) collective-permute-start(bf16[256,896]{1,0:T(8,128)(2,1)S(1)} %get-tuple-element.26.own), channel_id=1, source_target_pairs={{0,2},{1,3},{2,0},{3,1},{4,6},{5,7},{6,4},{7,5},{8,10},{9,11},{10,... | collective-permute-start | bytes 1376264 | tf_op jit(solution)/shard_map/ppermute | solution.py:102
  89.6 13.3 %collective-permute-start = (bf16[256,896]{1,0:T(8,128)(2,1)S(1)}, bf16[256,896]{1,0:T(8,128)(2,1)S(1)}, u32[]{:S(2)}, u32[]{:S(2)}) collective-permute-start(bf16[256,896]{1,0:T(8,128)(2,1)S(1)} %get-tuple-element.26.own), channel_id=1, source_target_pairs={{0,1},{1,0},{2,3},{3,2},{4,5},{5,4},{6,7},{7,6},{8,9},{9,8},{10,11... | collective-permute-start | bytes 1376264 | tf_op jit(solution)/shard_map/ppermute | solution.py:102
  99.0 3.9 %collective-permute-start.2 = (bf16[256,896]{1,0:T(8,128)(2,1)S(1)}, bf16[256,896]{1,0:T(8,128)(2,1)}, u32[]{:S(2)}, u32[]{:S(2)}) collective-permute-start(bf16[256,896]{1,0:T(8,128)(2,1)S(1)} %collective-permute-done.1.far), channel_id=1, source_target_pairs={{0,1},{1,0},{2,3},{3,2},{4,5},{5,4},{6,7},{7,6},{8,9},{9,8},{10,11... | collective-permute-start | bytes 1376264 | tf_op jit(solution)/shard_map/ppermute | solution.py:102
  111.1 26.0 %all-to-all-start.3 = ((bf16[32,8,256]{2,1,0:T(8,128)(2,1)}), bf16[32,8,256]{2,1,0:T(8,128)(2,1)S(1)}, u32[]{:S(2)}, u32[]{:S(2)}) async-start(bf16[32,8,256]{2,1,0:T(8,128)(2,1)} %bitcast.47), calls=%async_computation.3 | async-start | bytes 262144 | tf_op jit(solution)/shard_map/all_to_all | solution.py:216

commit v7 on v5

--- a/solution.py
+++ b/solution.py
@@ -72,19 +72,19 @@
     return lax.ppermute(value, axis, [(i, i ^ distance) for i in range(size)])
 
 
-def expert_kernel(turn_ref, own, core, far, diag, whole, out, total):
-    step = pl.program_id(0)
-    for index, part in enumerate((own, core, far, diag)):
-
-        @pl.when(step == index)
-        def _(index=index, part=part):
-            product = jnp.dot(part[...], whole[0], preferred_element_type=jnp.float32)
-            total[...] = product if index == 0 else total[...] + product
-
-    @pl.when(step == 3)
-    def _():
-        value = total[...]
-        out[...] = (value / (1.0 + jnp.exp(-value))).astype(out.dtype)
+def expert_kernel(turn, own, core, far, diag, whole, out, last, arrival):
+    fetch = pltpu.make_async_copy(diag, last, arrival)
+    fetch.start()
+    total = jnp.dot(own[...], whole[turn[0]], preferred_element_type=jnp.float32)
+    for index, part in ((1, core), (2, far), (3, last)):
+        if index == 3:
+            fetch.wait()
+        total = total + jnp.dot(
+            part[...],
+            whole[jnp.bitwise_xor(turn[0], index)],
+            preferred_element_type=jnp.float32,
+        )
+    out[...] = (total / (1.0 + jnp.exp(-total))).astype(out.dtype)
 
 
 def expert_rows(parts, whole):
@@ -93,19 +93,12 @@
     return pl.pallas_call(
         expert_kernel,
         out_shape=jax.ShapeDtypeStruct((rows, columns), jnp.bfloat16),
-        grid_spec=pltpu.PrefetchScalarGridSpec(
-            num_scalar_prefetch=1,
-            grid=(4,),
-            in_specs=[pl.BlockSpec((rows, quarter), lambda k, turn: (0, 0))] * 4
-            + [
-                pl.BlockSpec(
-                    (1, quarter, columns), lambda k, turn: (jnp.bitwise_xor(k, turn[0]), 0, 0)
-                )
-            ],
-            out_specs=pl.BlockSpec((rows, columns), lambda k, turn: (0, 0)),
-            scratch_shapes=[pltpu.VMEM((rows, columns), jnp.float32)],
-        ),
-        compiler_params=pltpu.CompilerParams(vmem_limit_bytes=32 * 2**20),
+        in_specs=[pl.BlockSpec(memory_space=pltpu.SMEM)]
+        + [pl.BlockSpec(memory_space=pltpu.VMEM)] * 3
+        + [pl.BlockSpec(memory_space=pl.ANY), pl.BlockSpec(memory_space=pltpu.VMEM)],
+        out_specs=pl.BlockSpec(memory_space=pltpu.VMEM),
+        scratch_shapes=[pltpu.VMEM((rows, quarter), jnp.bfloat16), pltpu.SemaphoreType.DMA],
+        compiler_params=pltpu.CompilerParams(vmem_limit_bytes=16 * 2**20),
         cost_estimate=pl.CostEstimate(
             flops=8 * rows * quarter * columns,
             bytes_accessed=8 * quarter * (rows + columns),

time: 135 us -> 134 us (level)
  no operation moved by 1% of the time
where the time goes in v7:
time: 134 us
  waiting for transfers between devices  69.2 us (52%)
  starting transfers between devices  41 us (31%)
  other arithmetic  5.77 us (4%)
  local copies, waits for them, and re-layouts  5.34 us (4%)
  blocking collectives  5.21 us (4%)
  matrix products  3.22 us (2%)
  Pallas kernels  2.18 us (2%)
  between operations  1.58 us (1%)
    all_to_all x1, waiting for transfers between devices, local(): lax.all_to_all(payload, 'expert', split_axis=0, concat_axis=0, tiled=True)  39.4 us
    all_to_all x1, waiting for transfers between devices, local(): lax.all_to_all(active, 'expert', split_axis=0, concat_axis=0, tiled=True)  16.8 us
    all_to_all x1, starting transfers between devices, local(): lax.all_to_all(payload, 'expert', split_axis=0, concat_axis=0, tiled=True)  12 us
    all_to_all x1, starting transfers between devices, local(): lax.all_to_all(jnp.swapaxes(hidden_in.reshape(step_count, 4, quarter), 0,...  9.28 us
    all_to_all x1, starting transfers between devices, local(): lax.all_to_all(active, 'expert', split_axis=0, concat_axis=0, tiled=True)  8.66 us
    ppermute x3, waiting for transfers between devices, flip(): return lax.ppermute(value, axis, [(i, i ^ distance) for i in range(size)])  7.77 us
    ppermute x3, starting transfers between devices, flip(): return lax.ppermute(value, axis, [(i, i ^ distance) for i in range(size)])  6.62 us
    all_to_all x1, waiting for transfers between devices, local(): lax.all_to_all(copies, 'group', split_axis=0, concat_axis=0, tiled=True)  5.34 us
  transfers between devices with their start and end apart: 7, of which 5 were waited for; matrix products, arithmetic and copies ran while one was open for 7% of the time, Pallas kernels for 0%

profile of v7, /device:TPU:2, one launch (start us, length us, event | category | flops | bytes accessed | tf_op | source)
XLA Modules:
  0.0 133.5 jit_solution(1371676621631677630)
XLA Ops:
  0.6 9.3 %all-to-all-start = ((bf16[4,4,896]{2,1,0:T(4,128)(2,1)}), bf16[4,4,896]{2,1,0:T(4,128)(2,1)S(1)}, u32[]{:S(2)}, u32[]{:S(2)}) async-start(bf16[4,4,896]{2,1,0:T(4,128)(2,1)} %bitcast.119), calls=%async_computation | async-start | bytes 57344 | tf_op jit(solution)/shard_map/all_to_all | solution.py:130
  9.9 3.8 %fusion.16 = (bf16[32,28,256]{2,0,1:T(8,128)(2,1)S(1)}, f32[32,28,256]{2,0,1:T(8,128)}, f32[32,28,256]{2,0,1:T(8,128)}) fusion(bf16[32,28,256]{2,0,1:T(8,128)(2,1)} %param.14, bf16[32,28,256]{2,0,1:T(8,128)(2,1)} %param.15, f32[32,28,256]{2,0,1:T(8,128)} %param.17, f32[32,28,256]{2,0,1:T(8,128)} %param.16), kind=kLoop, calls=%fused_computation.27 | loop fusion | flops 4128768 | bytes 5046272 | tf_op jit(solution)/shard_map/convert_element_type | solution.py:32
  14.1 0.2 copy.42
  14.3 0.3 fusion
  14.6 0.4 copy.40
  15.0 0.3 reshape.227
  15.3 1.0 pad_maximum_fusion
  16.3 12.0 %all-to-all-start.1 = ((bf16[32,112,128]{2,1,0:T(8,128)(2,1)}), bf16[32,112,128]{2,1,0:T(8,128)(2,1)S(1)}, u32[]{:S(2)}, u32[]{:S(2)}) async-start(bf16[32,112,128]{2,1,0:T(8,128)(2,1)} %pad_maximum_fusion), calls=%async_computation.1 | async-start | bytes 1835008 | tf_op jit(solution)/shard_map/all_to_all | solution.py:162
  29.1 0.2 fusion.20
  29.3 0.2 fusion.58
  29.6 0.3 fusion.57
  30.0 0.2 fusion.23
  30.2 0.2 convolution_bitcast_fusion
  30.4 0.9 fusion.56
  31.5 5.2 %all_gather.3 = bf16[4,4,512]{2,0,1:T(4,128)(2,1)S(1)} all-gather(bf16[4,1,512]{2,0,1:T(4,128)(2,1)S(1)} %fusion.35), channel_id=1, replica_groups=mesh['group'=4,'expert'=32,'tensor'=4] {'tensor'}, dimensions={1}, use_global_device_ids=true | all-gather | bytes 20480 | tf_op jit(solution)/shard_map/all_gather | solution.py:163
  36.7 39.4 %all-to-all-done.1 = bf16[32,112,128]{2,1,0:T(8,128)(2,1)S(1)} async-done(((bf16[32,112,128]{2,1,0:T(8,128)(2,1)}), bf16[32,112,128]{2,1,0:T(8,128)(2,1)S(1)}, u32[]{:S(2)}, u32[]{:S(2)}) %all-to-all-start.1) | async-done | bytes 917536 | tf_op jit(solution)/shard_map/all_to_all | solution.py:162
  76.2 0.5 copy.44
  76.8 1.4 %broadcast_in_dim.30 = bf16[4,896,256]{2,1,0:T(8,128)(2,1)} broadcast(bf16[896,256]{1,0:T(8,128)(2,1)S(1)} %bitcast.114), dimensions={1,2} | broadcast | bytes 2293760 | tf_op jit(solution)/shard_map/broadcast_in_dim | solution.py:169
  78.2 4.5 %all-to-all-start.2 = ((bf16[4,896,256]{2,1,0:T(8,128)(2,1)}), bf16[4,896,256]{2,1,0:T(8,128)(2,1)S(1)}, u32[]{:S(2)}, u32[]{:S(2)}) async-start(bf16[4,896,256]{2,1,0:T(8,128)(2,1)} %broadcast_in_dim.30), calls=%async_computation.2 | async-start | bytes 3670016 | tf_op jit(solution)/shard_map/all_to_all | solution.py:170
  82.6 0.5 reshape.241.own
  83.1 2.8 %collective-permute-start.1 = (bf16[256,896]{1,0:T(8,128)(2,1)S(1)}, bf16[256,896]{1,0:T(8,128)(2,1)S(1)}, u32[]{:S(2)}, u32[]{:S(2)}) collective-permute-start(bf16[256,896]{1,0:T(8,128)(2,1)S(1)} %reshape.241.own), channel_id=1, source_target_pairs={{0,2},{1,3},{2,0},{3,1},{4,6},{5,7},{6,4},{7,5},{8,10},{9,11},{10,... | collective-permute-start | bytes 1376264 | tf_op jit(solution)/shard_map/ppermute | solution.py:72
  85.9 1.9 %collective-permute-start = (bf16[256,896]{1,0:T(8,128)(2,1)S(1)}, bf16[256,896]{1,0:T(8,128)(2,1)S(1)}, u32[]{:S(2)}, u32[]{:S(2)}) collective-permute-start(bf16[256,896]{1,0:T(8,128)(2,1)S(1)} %reshape.241.own), channel_id=1, source_target_pairs={{0,1},{1,0},{2,3},{3,2},{4,5},{5,4},{6,7},{7,6},{8,9},{9,8},{10,11... | collective-permute-start | bytes 1376264 | tf_op jit(solution)/shard_map/ppermute | solution.py:72
  87.8 7.5 %collective-permute-done.1.far = bf16[256,896]{1,0:T(8,128)(2,1)S(1)} collective-permute-done((bf16[256,896]{1,0:T(8,128)(2,1)S(1)}, bf16[256,896]{1,0:T(8,128)(2,1)S(1)}, u32[]{:S(2)}, u32[]{:S(2)}) %collective-permute-start.1) | collective-permute-done | bytes 458784 | tf_op jit(solution)/shard_map/ppermute | solution.py:72
  95.3 1.9 %collective-permute-start.2 = (bf16[256,896]{1,0:T(8,128)(2,1)S(1)}, bf16[256,896]{1,0:T(8,128)(2,1)}, u32[]{:S(2)}, u32[]{:S(2)}) collective-permute-start(bf16[256,896]{1,0:T(8,128)(2,1)S(1)} %collective-permute-done.1.far), channel_id=1, source_target_pairs={{0,1},{1,0},{2,3},{3,2},{4,5},{5,4},{6,7},{7,6},{8,9},{9,8},{10,11... | collective-permute-start | bytes 1376264 | tf_op jit(solution)/shard_map/ppermute | solution.py:72
  97.3 1.6 %convert_element_type.81 = bf16[4,1,16384]{2,0,1:T(4,128)(2,1)} reshape(bf16[4,1,32,512]{3,2,0,1:T(8,128)(2,1)} %get-tuple-element.26) | data formatting | bytes 262144 | tf_op jit(solution)/shard_map/convert_element_type | solution.py:66
  98.9 0.3 collective-permute-done.2.diag
  99.2 5.3 %all-to-all-done.2.whole = bf16[4,896,256]{2,1,0:T(8,128)(2,1)S(1)} async-done(((bf16[4,896,256]{2,1,0:T(8,128)(2,1)}), bf16[4,896,256]{2,1,0:T(8,128)(2,1)S(1)}, u32[]{:S(2)}, u32[]{:S(2)}) %all-to-all-start.2) | async-done | bytes 1835040 | tf_op jit(solution)/shard_map/all_to_all | solution.py:170
  104.5 2.2 %shard_map.165 = bf16[256,256]{1,0:T(8,128)(2,1)} custom-call(s32[1]{0:T(128)} %bitcast.30.turn, bf16[256,896]{1,0:T(8,128)(2,1)S(1)} %reshape.241.own, bf16[256,896]{1,0:T(8,128)(2,1)S(1)} %collective-permute-done.core, bf16[256,896]{1,0:T(8,128)(2,1)S(1)} %collective-permute-done.1.far, bf16[256,896]{1,0:T(8,128)(2,1)} %collective-permute-done.2.diag, ...), custom_call_target="tpu_custom_call" | custom-call | flops 469762048 | bytes 3670016 | tf_op jit(solution)/shard_map/pallas_call | solution.py:93
  106.7 8.7 %all-to-all-start.3 = ((bf16[32,8,256]{2,1,0:T(8,128)(2,1)}), bf16[32,8,256]{2,1,0:T(8,128)(2,1)S(1)}, u32[]{:S(2)}, u32[]{:S(2)}) async-start(bf16[32,8,256]{2,1,0:T(8,128)(2,1)} %bitcast.31), calls=%async_computation.3 | async-start | bytes 262144 | tf_op jit(solution)/shard_map/all_to_all | solution.py:184
  115.5 0.2 select_reduce_fusion
  115.9 16.8 %all-to-all-done.3 = bf16[32,8,256]{2,1,0:T(8,128)(2,1)S(1)} async-done(((bf16[32,8,256]{2,1,0:T(8,128)(2,1)}), bf16[32,8,256]{2,1,0:T(8,128)(2,1)S(1)}, u32[]{:S(2)}, u32[]{:S(2)}) %all-to-all-start.3) | async-done | bytes 131104 | tf_op jit(solution)/shard_map/all_to_all | solution.py:184
  132.7 0.8 fusion.6
  (40 shorter events, 1.4 us)
Async XLA Ops:
  0.6 29.0 %copy-start = (bf16[1,256,512]{2,1,0:T(8,128)(2,1)S(1)}, bf16[1,256,512]{2,1,0:T(8,128)(2,1)}, u32[]{:S(2)}) copy-start(bf16[1,256,512]{2,1,0:T(8,128)(2,1)} %param.21) | copy-start | bytes 786436
  0.6 13.6 %all-to-all-start = ((bf16[4,4,896]{2,1,0:T(4,128)(2,1)}), bf16[4,4,896]{2,1,0:T(4,128)(2,1)S(1)}, u32[]{:S(2)}, u32[]{:S(2)}) async-start(bf16[4,4,896]{2,1,0:T(4,128)(2,1)} %bitcast.119), calls=%async_computation | async-start | bytes 57344 | tf_op jit(solution)/shard_map/all_to_all | solution.py:130
  9.9 3.8 %copy-start.2 = (s32[4,4,8]{2,1,0:T(4,128)S(1)}, s32[4,4,8]{2,1,0:T(4,128)}, u32[]{:S(2)}) copy-start(s32[4,4,8]{2,1,0:T(4,128)} %param.26) | copy-start | bytes 1540
  15.3 13.7 %copy-start.5 = (bf16[4,1,2048]{2,0,1:T(4,128)(2,1)S(1)}, bf16[4,1,2048]{2,0,1:T(4,128)(2,1)}, u32[]{:S(2)}) copy-start(bf16[4,1,2048]{2,0,1:T(4,128)(2,1)} %param.20) | copy-start | bytes 49156
  15.3 13.8 %copy-start.1 = (bf16[4,1,16384]{2,0,1:T(4,128)(2,1)S(1)}, bf16[4,1,16384]{2,0,1:T(4,128)(2,1)}, u32[]{:S(2)}) copy-start(bf16[4,1,16384]{2,0,1:T(4,128)(2,1)} %param.19) | copy-start | bytes 393220
  15.3 13.8 %copy-start.4 = (bf16[4,1,512]{2,0,1:T(4,128)(2,1)S(1)}, bf16[4,1,512]{2,0,1:T(4,128)(2,1)}, u32[]{:S(2)}) copy-start(bf16[4,1,512]{2,0,1:T(4,128)(2,1)} %param.23) | copy-start | bytes 12292
  15.3 14.0 %copy-start.7 = (bf16[4,1,64]{2,0,1:T(4,128)(2,1)S(1)}, bf16[4,1,64]{2,0,1:T(4,128)(2,1)}, u32[]{:S(2)}) copy-start(bf16[4,1,64]{2,0,1:T(4,128)(2,1)} %param.24) | copy-start | bytes 1540
  15.3 14.2 %copy-start.3 = (bf16[1,64,256]{2,1,0:T(8,128)(2,1)S(1)}, bf16[1,64,256]{2,1,0:T(8,128)(2,1)}, u32[]{:S(2)}) copy-start(bf16[1,64,256]{2,1,0:T(8,128)(2,1)} %param.22) | copy-start | bytes 98308
  16.3 59.8 %all-to-all-start.1 = ((bf16[32,112,128]{2,1,0:T(8,128)(2,1)}), bf16[32,112,128]{2,1,0:T(8,128)(2,1)S(1)}, u32[]{:S(2)}, u32[]{:S(2)}) async-start(bf16[32,112,128]{2,1,0:T(8,128)(2,1)} %pad_maximum_fusion), calls=%async_computation.1 | async-start | bytes 1835008 | tf_op jit(solution)/shard_map/all_to_all | solution.py:162
  78.2 26.3 %all-to-all-start.2 = ((bf16[4,896,256]{2,1,0:T(8,128)(2,1)}), bf16[4,896,256]{2,1,0:T(8,128)(2,1)S(1)}, u32[]{:S(2)}, u32[]{:S(2)}) async-start(bf16[4,896,256]{2,1,0:T(8,128)(2,1)} %broadcast_in_dim.30), calls=%async_computation.2 | async-start | bytes 3670016 | tf_op jit(solution)/shard_map/all_to_all | solution.py:170
  83.1 12.2 %collective-permute-start.1 = (bf16[256,896]{1,0:T(8,128)(2,1)S(1)}, bf16[256,896]{1,0:T(8,128)(2,1)S(1)}, u32[]{:S(2)}, u32[]{:S(2)}) collective-permute-start(bf16[256,896]{1,0:T(8,128)(2,1)S(1)} %reshape.241.own), channel_id=1, source_target_pairs={{0,2},{1,3},{2,0},{3,1},{4,6},{5,7},{6,4},{7,5},{8,10},{9,11},{10,... | collective-permute-start | bytes 1376264 | tf_op jit(solution)/shard_map/ppermute | solution.py:72
  85.9 13.0 %collective-permute-start = (bf16[256,896]{1,0:T(8,128)(2,1)S(1)}, bf16[256,896]{1,0:T(8,128)(2,1)S(1)}, u32[]{:S(2)}, u32[]{:S(2)}) collective-permute-start(bf16[256,896]{1,0:T(8,128)(2,1)S(1)} %reshape.241.own), channel_id=1, source_target_pairs={{0,1},{1,0},{2,3},{3,2},{4,5},{5,4},{6,7},{7,6},{8,9},{9,8},{10,11... | collective-permute-start | bytes 1376264 | tf_op jit(solution)/shard_map/ppermute | solution.py:72
  95.3 3.8 %collective-permute-start.2 = (bf16[256,896]{1,0:T(8,128)(2,1)S(1)}, bf16[256,896]{1,0:T(8,128)(2,1)}, u32[]{:S(2)}, u32[]{:S(2)}) collective-permute-start(bf16[256,896]{1,0:T(8,128)(2,1)S(1)} %collective-permute-done.1.far), channel_id=1, source_target_pairs={{0,1},{1,0},{2,3},{3,2},{4,5},{5,4},{6,7},{7,6},{8,9},{9,8},{10,11... | collective-permute-start | bytes 1376264 | tf_op jit(solution)/shard_map/ppermute | solution.py:72
  104.5 10.9 %copy-start.6 = (bf16[512,32]{0,1:T(8,128)(2,1)S(1)}, bf16[512,32]{0,1:T(8,128)(2,1)}, u32[]{:S(2)}) copy-start(bf16[512,32]{0,1:T(8,128)(2,1)} %param.27) | copy-start | bytes 98308
  106.7 26.0 %all-to-all-start.3 = ((bf16[32,8,256]{2,1,0:T(8,128)(2,1)}), bf16[32,8,256]{2,1,0:T(8,128)(2,1)S(1)}, u32[]{:S(2)}, u32[]{:S(2)}) async-start(bf16[32,8,256]{2,1,0:T(8,128)(2,1)} %bitcast.31), calls=%async_computation.3 | async-start | bytes 262144 | tf_op jit(solution)/shard_map/all_to_all | solution.py:184

commit v8 on v7

--- a/solution.py
+++ b/solution.py
@@ -123,8 +123,7 @@
     expert_ids,
     router,
 ):
-    first_new, second_new, updated = adamw(weights, gradients, moment_one, moment_two)
-    expert_count, slab, columns = updated.shape
+    expert_count, slab, columns = weights.shape
     step_count, _, width = hidden_in.shape
     quarter = width // 4
     my_part = lax.all_to_all(
@@ -143,19 +142,38 @@
     slot_hit = (earlier[..., None] == jnp.arange(slot_count, dtype=jnp.float32)).astype(
         jnp.float32
     ) * per_expert[..., None]
-    outgoing = jnp.einsum(
-        "sbec,bsd->escd",
-        slot_hit.astype(jnp.bfloat16),
-        my_part,
+    same_step = jnp.eye(step_count, dtype=jnp.float32)
+    placed = jnp.transpose(slot_hit, (1, 0, 2, 3))[:, :, :, None] * same_step[:, None, :, None]
+    placed = placed.reshape(4 * step_count, expert_count * places).astype(jnp.bfloat16)
+    placed, weights = lax.optimization_barrier((placed, weights))
+    updated = adamw(weights, gradients, moment_one, moment_two)[2]
+    outgoing = lax.dot_general(
+        placed,
+        my_part.reshape(4 * step_count, quarter),
+        (((0,), (0,)), ((), ())),
         preferred_element_type=jnp.float32,
     ).astype(jnp.bfloat16)
-    outgoing = outgoing.reshape(expert_count, places * quarter // 128, 128)
+    lanes = quarter // 128
+    outgoing = jnp.swapaxes(outgoing.reshape(expert_count, places, lanes, 128), 1, 2)
+    outgoing = outgoing.reshape(expert_count, places * lanes, 128)
     slabs = jnp.swapaxes(updated.reshape(expert_count, slab, 2, 128), 1, 2)
     slabs = slabs.reshape(expert_count, 2 * slab, 128)
-    outgoing, query_latent, query_rope, new_latent, new_rope = lax.optimization_barrier(
-        (outgoing, query_latent, query_rope, new_latent, new_rope)
+    outgoing, query_latent, query_rope, new_latent, new_rope, gradients, moment_one, moment_two = (
+        lax.optimization_barrier(
+            (
+                outgoing,
+                query_latent,
+                query_rope,
+                new_latent,
+                new_rope,
+                gradients,
+                moment_one,
+                moment_two,
+            )
+        )
     )
     payload = jnp.concatenate([slabs, outgoing], 1)
+    first_new, second_new, _ = adamw(weights, gradients, moment_one, moment_two)
     attention_out, summary = attend(
         query_latent, query_rope, cache_latent, cache_rope, new_latent, new_rope, lengths
     )
@@ -164,7 +182,8 @@
     held = jnp.swapaxes(arrived[:, : 2 * slab].reshape(expert_count, 2, slab, 128), 1, 2)
     held = held.reshape(expert_count * slab, columns)
     held, summary_all = lax.optimization_barrier((held, summary_all))
-    rows_in = arrived[:, 2 * slab :].reshape(expert_count * places, quarter)
+    rows_in = arrived[:, 2 * slab :].reshape(expert_count, lanes, places, 128)
+    rows_in = jnp.swapaxes(rows_in, 1, 2).reshape(expert_count * places, quarter)
 
     copies = jnp.broadcast_to(held[None], (lax.axis_size("group"),) + held.shape)
     whole = lax.all_to_all(copies, "group", split_axis=0, concat_axis=0, tiled=True)

time: 134 us -> 134 us (level)
  waiting for transfers between devices: 69.2 us -> 66.5 us
  other arithmetic: 5.77 us -> 7.67 us
    add x0 -> x1, other arithmetic: none -> 3.24 us  [adamw(): BETA_TWO * moment_two + (1.0 - BETA_TWO) * grad_wide * grad_wide]
    all_to_all x1, waiting for transfers between devices: 5.34 us -> 2.84 us  [local(): lax.all_to_all(copies, 'group', split_axis=0, concat_axis=0, tiled=True)]
  transfers between devices with their start and end apart: 7 -> 7, of which waited for: 5 -> 4; matrix products, arithmetic and copies ran while one was open for 7% -> 9% of each run, Pallas kernels for 0% -> 0%
where the time goes in v8:
time: 134 us; the launch traced here: 133 us
  waiting for transfers between devices  66.5 us (50%)
  starting transfers between devices  41 us (31%)
  other arithmetic  7.67 us (6%)
  local copies, waits for them, and re-layouts  5.74 us (4%)
  blocking collectives  5.19 us (4%)
  matrix products  3.14 us (2%)
  Pallas kernels  2.18 us (2%)
  between operations  1.64 us (1%)
    all_to_all x1, waiting for transfers between devices, local(): lax.all_to_all(payload, 'expert', split_axis=0, concat_axis=0, tiled=True)  39.4 us
    all_to_all x1, waiting for transfers between devices, local(): lax.all_to_all(active, 'expert', split_axis=0, concat_axis=0, tiled=True)  16.8 us
    all_to_all x1, starting transfers between devices, local(): lax.all_to_all(payload, 'expert', split_axis=0, concat_axis=0, tiled=True)  12 us
    all_to_all x1, starting transfers between devices, local(): lax.all_to_all(jnp.swapaxes(hidden_in.reshape(step_count, 4, quarter), 0,...  9.28 us
    all_to_all x1, starting transfers between devices, local(): lax.all_to_all(active, 'expert', split_axis=0, concat_axis=0, tiled=True)  8.64 us
    ppermute x3, waiting for transfers between devices, flip(): return lax.ppermute(value, axis, [(i, i ^ distance) for i in range(size)])  7.51 us
    ppermute x3, starting transfers between devices, flip(): return lax.ppermute(value, axis, [(i, i ^ distance) for i in range(size)])  6.61 us
    all_gather x1, blocking collectives, local(): summary_all = lax.all_gather(summary, 'tensor', axis=1, tiled=True)  5.19 us
  transfers between devices with their start and end apart: 7, of which 4 were waited for; matrix products, arithmetic and copies ran while one was open for 9% of the time, Pallas kernels for 0%

profile of v8, /device:TPU:2, one launch (start us, length us, event | category | flops | bytes accessed | tf_op | source)
XLA Modules:
  0.0 133.0 jit_solution(10020960127720570809)
XLA Ops:
  0.6 9.3 %all-to-all-start = ((bf16[4,4,896]{2,1,0:T(4,128)(2,1)}), bf16[4,4,896]{2,1,0:T(4,128)(2,1)S(1)}, u32[]{:S(2)}, u32[]{:S(2)}) async-start(bf16[4,4,896]{2,1,0:T(4,128)(2,1)} %bitcast.136), calls=%async_computation | async-start | bytes 57344 | tf_op jit(solution)/shard_map/all_to_all | solution.py:129
  9.9 0.8 convert_reduce_fusion
  10.8 0.1 copy.51
  11.1 0.2 convert_element_type.86
  11.2 2.6 %fusion.16 = bf16[32,28,256]{2,0,1:T(8,128)(2,1)S(1)} fusion(bf16[32,28,256]{2,0,1:T(8,128)(2,1)} %param.14, bf16[32,28,256]{2,0,1:T(8,128)(2,1)} %param.15, f32[32,28,256]{2,0,1:T(8,128)} %param.17, f32[32,28,256]{2,0,1:T(8,128)} %param.16), kind=kLoop, calls=%fused_computation.29 | loop fusion | flops 4128768 | bytes 3211264 | tf_op jit(solution)/shard_map/convert_element_type | solution.py:32
  14.0 0.2 fusion
  14.5 1.3 copy.55
  15.8 12.0 %all-to-all-start.1 = ((bf16[32,112,128]{2,1,0:T(8,128)(2,1)}), bf16[32,112,128]{2,1,0:T(8,128)(2,1)S(1)}, u32[]{:S(2)}, u32[]{:S(2)}) async-start(bf16[32,112,128]{2,1,0:T(8,128)(2,1)} %copy.55), calls=%async_computation.1 | async-start | bytes 1835008 | tf_op jit(solution)/shard_map/all_to_all | solution.py:180
  28.6 0.2 fusion.27
  28.8 0.2 fusion.58
  29.1 0.3 fusion.57
  29.5 0.2 fusion.30
  29.6 0.2 convolution_bitcast_fusion
  29.9 0.9 fusion.56
  31.0 5.2 %all_gather.3 = bf16[4,4,512]{2,0,1:T(4,128)(2,1)S(1)} all-gather(bf16[4,1,512]{2,0,1:T(4,128)(2,1)S(1)} %fusion.40), channel_id=1, replica_groups=mesh['group'=4,'expert'=32,'tensor'=4] {'tensor'}, dimensions={1}, use_global_device_ids=true | all-gather | bytes 20480 | tf_op jit(solution)/shard_map/all_gather | solution.py:181
  36.2 39.4 %all-to-all-done.1 = bf16[32,112,128]{2,1,0:T(8,128)(2,1)S(1)} async-done(((bf16[32,112,128]{2,1,0:T(8,128)(2,1)}), bf16[32,112,128]{2,1,0:T(8,128)(2,1)S(1)}, u32[]{:S(2)}, u32[]{:S(2)}) %all-to-all-start.1) | async-done | bytes 917536 | tf_op jit(solution)/shard_map/all_to_all | solution.py:180
  75.7 0.5 copy.57
  76.3 1.4 %broadcast_in_dim.30 = bf16[4,896,256]{2,1,0:T(8,128)(2,1)} broadcast(bf16[896,256]{1,0:T(8,128)(2,1)S(1)} %bitcast.131), dimensions={1,2} | broadcast | bytes 2293760 | tf_op jit(solution)/shard_map/broadcast_in_dim | solution.py:188
  77.6 4.5 %all-to-all-start.2 = ((bf16[4,896,256]{2,1,0:T(8,128)(2,1)}), bf16[4,896,256]{2,1,0:T(8,128)(2,1)S(1)}, u32[]{:S(2)}, u32[]{:S(2)}) async-start(bf16[4,896,256]{2,1,0:T(8,128)(2,1)} %broadcast_in_dim.30), calls=%async_computation.2 | async-start | bytes 3670016 | tf_op jit(solution)/shard_map/all_to_all | solution.py:189
  82.1 2.8 %collective-permute-start.1 = (bf16[256,896]{1,0:T(8,128)(2,1)S(1)}, bf16[256,896]{1,0:T(8,128)(2,1)S(1)}, u32[]{:S(2)}, u32[]{:S(2)}) collective-permute-start(bf16[256,896]{1,0:T(8,128)(2,1)S(1)} %get-tuple-element.31.own), channel_id=1, source_target_pairs={{0,2},{1,3},{2,0},{3,1},{4,6},{5,7},{6,4},{7,5},{8,10},{9,11},{10,... | collective-permute-start | bytes 1376264 | tf_op jit(solution)/shard_map/ppermute | solution.py:72
  84.9 1.9 %collective-permute-start = (bf16[256,896]{1,0:T(8,128)(2,1)S(1)}, bf16[256,896]{1,0:T(8,128)(2,1)S(1)}, u32[]{:S(2)}, u32[]{:S(2)}) collective-permute-start(bf16[256,896]{1,0:T(8,128)(2,1)S(1)} %get-tuple-element.31.own), channel_id=1, source_target_pairs={{0,1},{1,0},{2,3},{3,2},{4,5},{5,4},{6,7},{7,6},{8,9},{9,8},{10,11... | collective-permute-start | bytes 1376264 | tf_op jit(solution)/shard_map/ppermute | solution.py:72
  86.8 7.5 %collective-permute-done.1.far = bf16[256,896]{1,0:T(8,128)(2,1)S(1)} collective-permute-done((bf16[256,896]{1,0:T(8,128)(2,1)S(1)}, bf16[256,896]{1,0:T(8,128)(2,1)S(1)}, u32[]{:S(2)}, u32[]{:S(2)}) %collective-permute-start.1) | collective-permute-done | bytes 458784 | tf_op jit(solution)/shard_map/ppermute | solution.py:72
  94.3 1.9 %collective-permute-start.2 = (bf16[256,896]{1,0:T(8,128)(2,1)S(1)}, bf16[256,896]{1,0:T(8,128)(2,1)}, u32[]{:S(2)}, u32[]{:S(2)}) collective-permute-start(bf16[256,896]{1,0:T(8,128)(2,1)S(1)} %collective-permute-done.1.far), channel_id=1, source_target_pairs={{0,1},{1,0},{2,3},{3,2},{4,5},{5,4},{6,7},{7,6},{8,9},{9,8},{10,11... | collective-permute-start | bytes 1376264 | tf_op jit(solution)/shard_map/ppermute | solution.py:72
  96.3 1.6 %convert_element_type.92 = bf16[4,1,16384]{2,0,1:T(4,128)(2,1)} reshape(bf16[4,1,32,512]{3,2,0,1:T(8,128)(2,1)} %get-tuple-element.35) | data formatting | bytes 262144 | tf_op jit(solution)/shard_map/convert_element_type | solution.py:66
  97.9 3.2 %fusion.20 = (f32[32,28,256]{2,0,1:T(8,128)}, f32[32,28,256]{2,0,1:T(8,128)}) fusion(bf16[32,28,256]{2,0,1:T(8,128)(2,1)} %param.15, f32[32,28,256]{2,0,1:T(8,128)} %param.17, f32[32,28,256]{2,0,1:T(8,128)} %param.16), kind=kLoop, calls=%fused_computation.33 | loop fusion | flops 1835008 | bytes 4128768 | tf_op jit(solution)/shard_map/add | solution.py:29
  101.2 2.8 %all-to-all-done.2.whole = bf16[4,896,256]{2,1,0:T(8,128)(2,1)S(1)} async-done(((bf16[4,896,256]{2,1,0:T(8,128)(2,1)}), bf16[4,896,256]{2,1,0:T(8,128)(2,1)S(1)}, u32[]{:S(2)}, u32[]{:S(2)}) %all-to-all-start.2) | async-done | bytes 1835040 | tf_op jit(solution)/shard_map/all_to_all | solution.py:189
  104.0 2.2 %shard_map.165 = bf16[256,256]{1,0:T(8,128)(2,1)} custom-call(s32[1]{0:T(128)} %bitcast.33.turn, bf16[256,896]{1,0:T(8,128)(2,1)S(1)} %get-tuple-element.31.own, bf16[256,896]{1,0:T(8,128)(2,1)S(1)} %collective-permute-done.core, bf16[256,896]{1,0:T(8,128)(2,1)S(1)} %collective-permute-done.1.far, bf16[256,896]{1,0:T(8,128)(2,1)} %collective-permute-done.2.diag, ...), custom_call_target="tpu_custom_call" | custom-call | flops 469762048 | bytes 3670016 | tf_op jit(solution)/shard_map/pallas_call | solution.py:93
  106.2 8.6 %all-to-all-start.3 = ((bf16[32,8,256]{2,1,0:T(8,128)(2,1)}), bf16[32,8,256]{2,1,0:T(8,128)(2,1)S(1)}, u32[]{:S(2)}, u32[]{:S(2)}) async-start(bf16[32,8,256]{2,1,0:T(8,128)(2,1)} %bitcast.39), calls=%async_computation.3 | async-start | bytes 262144 | tf_op jit(solution)/shard_map/all_to_all | solution.py:203
  114.8 0.1 fusion.11
  115.0 0.2 select_reduce_fusion
  115.4 16.8 %all-to-all-done.3 = bf16[32,8,256]{2,1,0:T(8,128)(2,1)S(1)} async-done(((bf16[32,8,256]{2,1,0:T(8,128)(2,1)}), bf16[32,8,256]{2,1,0:T(8,128)(2,1)S(1)}, u32[]{:S(2)}, u32[]{:S(2)}) %all-to-all-start.3) | async-done | bytes 131104 | tf_op jit(solution)/shard_map/all_to_all | solution.py:203
  132.2 0.8 fusion.6
  (48 shorter events, 1.5 us)
Async XLA Ops:
  0.6 28.5 %copy-start = (bf16[1,256,512]{2,1,0:T(8,128)(2,1)S(1)}, bf16[1,256,512]{2,1,0:T(8,128)(2,1)}, u32[]{:S(2)}) copy-start(bf16[1,256,512]{2,1,0:T(8,128)(2,1)} %param.21) | copy-start | bytes 786436
  0.6 13.4 %all-to-all-start = ((bf16[4,4,896]{2,1,0:T(4,128)(2,1)}), bf16[4,4,896]{2,1,0:T(4,128)(2,1)S(1)}, u32[]{:S(2)}, u32[]{:S(2)}) async-start(bf16[4,4,896]{2,1,0:T(4,128)(2,1)} %bitcast.136), calls=%async_computation | async-start | bytes 57344 | tf_op jit(solution)/shard_map/all_to_all | solution.py:129
  14.5 14.0 %copy-start.5 = (bf16[4,1,2048]{2,0,1:T(4,128)(2,1)S(1)}, bf16[4,1,2048]{2,0,1:T(4,128)(2,1)}, u32[]{:S(2)}) copy-start(bf16[4,1,2048]{2,0,1:T(4,128)(2,1)} %param.20) | copy-start | bytes 49156
  14.5 14.1 %copy-start.1 = (bf16[4,1,16384]{2,0,1:T(4,128)(2,1)S(1)}, bf16[4,1,16384]{2,0,1:T(4,128)(2,1)}, u32[]{:S(2)}) copy-start(bf16[4,1,16384]{2,0,1:T(4,128)(2,1)} %param.19) | copy-start | bytes 393220
  14.5 14.1 %copy-start.4 = (bf16[4,1,512]{2,0,1:T(4,128)(2,1)S(1)}, bf16[4,1,512]{2,0,1:T(4,128)(2,1)}, u32[]{:S(2)}) copy-start(bf16[4,1,512]{2,0,1:T(4,128)(2,1)} %param.23) | copy-start | bytes 12292
  14.5 14.3 %copy-start.7 = (bf16[4,1,64]{2,0,1:T(4,128)(2,1)S(1)}, bf16[4,1,64]{2,0,1:T(4,128)(2,1)}, u32[]{:S(2)}) copy-start(bf16[4,1,64]{2,0,1:T(4,128)(2,1)} %param.24) | copy-start | bytes 1540
  14.5 14.4 %copy-start.3 = (bf16[1,64,256]{2,1,0:T(8,128)(2,1)S(1)}, bf16[1,64,256]{2,1,0:T(8,128)(2,1)}, u32[]{:S(2)}) copy-start(bf16[1,64,256]{2,1,0:T(8,128)(2,1)} %param.22) | copy-start | bytes 98308
  15.8 59.8 %all-to-all-start.1 = ((bf16[32,112,128]{2,1,0:T(8,128)(2,1)}), bf16[32,112,128]{2,1,0:T(8,128)(2,1)S(1)}, u32[]{:S(2)}, u32[]{:S(2)}) async-start(bf16[32,112,128]{2,1,0:T(8,128)(2,1)} %copy.55), calls=%async_computation.1 | async-start | bytes 1835008 | tf_op jit(solution)/shard_map/all_to_all | solution.py:180
  77.6 26.3 %all-to-all-start.2 = ((bf16[4,896,256]{2,1,0:T(8,128)(2,1)}), bf16[4,896,256]{2,1,0:T(8,128)(2,1)S(1)}, u32[]{:S(2)}, u32[]{:S(2)}) async-start(bf16[4,896,256]{2,1,0:T(8,128)(2,1)} %broadcast_in_dim.30), calls=%async_computation.2 | async-start | bytes 3670016 | tf_op jit(solution)/shard_map/all_to_all | solution.py:189
  82.1 12.2 %collective-permute-start.1 = (bf16[256,896]{1,0:T(8,128)(2,1)S(1)}, bf16[256,896]{1,0:T(8,128)(2,1)S(1)}, u32[]{:S(2)}, u32[]{:S(2)}) collective-permute-start(bf16[256,896]{1,0:T(8,128)(2,1)S(1)} %get-tuple-element.31.own), channel_id=1, source_target_pairs={{0,2},{1,3},{2,0},{3,1},{4,6},{5,7},{6,4},{7,5},{8,10},{9,11},{10,... | collective-permute-start | bytes 1376264 | tf_op jit(solution)/shard_map/ppermute | solution.py:72
  84.9 16.2 %collective-permute-start = (bf16[256,896]{1,0:T(8,128)(2,1)S(1)}, bf16[256,896]{1,0:T(8,128)(2,1)S(1)}, u32[]{:S(2)}, u32[]{:S(2)}) collective-permute-start(bf16[256,896]{1,0:T(8,128)(2,1)S(1)} %get-tuple-element.31.own), channel_id=1, source_target_pairs={{0,1},{1,0},{2,3},{3,2},{4,5},{5,4},{6,7},{7,6},{8,9},{9,8},{10,11... | collective-permute-start | bytes 1376264 | tf_op jit(solution)/shard_map/ppermute | solution.py:72
  94.3 6.8 %collective-permute-start.2 = (bf16[256,896]{1,0:T(8,128)(2,1)S(1)}, bf16[256,896]{1,0:T(8,128)(2,1)}, u32[]{:S(2)}, u32[]{:S(2)}) collective-permute-start(bf16[256,896]{1,0:T(8,128)(2,1)S(1)} %collective-permute-done.1.far), channel_id=1, source_target_pairs={{0,1},{1,0},{2,3},{3,2},{4,5},{5,4},{6,7},{7,6},{8,9},{9,8},{10,11... | collective-permute-start | bytes 1376264 | tf_op jit(solution)/shard_map/ppermute | solution.py:72
  104.0 10.8 %copy-start.6 = (bf16[512,32]{0,1:T(8,128)(2,1)S(1)}, bf16[512,32]{0,1:T(8,128)(2,1)}, u32[]{:S(2)}) copy-start(bf16[512,32]{0,1:T(8,128)(2,1)} %param.27) | copy-start | bytes 98308
  104.0 11.0 %copy-start.2 = (s32[4,4,8]{2,1,0:T(4,128)S(1)}, s32[4,4,8]{2,1,0:T(4,128)}, u32[]{:S(2)}) copy-start(s32[4,4,8]{2,1,0:T(4,128)} %param.26) | copy-start | bytes 1540
  106.2 26.0 %all-to-all-start.3 = ((bf16[32,8,256]{2,1,0:T(8,128)(2,1)}), bf16[32,8,256]{2,1,0:T(8,128)(2,1)S(1)}, u32[]{:S(2)}, u32[]{:S(2)}) async-start(bf16[32,8,256]{2,1,0:T(8,128)(2,1)} %bitcast.39), calls=%async_computation.3 | async-start | bytes 262144 | tf_op jit(solution)/shard_map/all_to_all | solution.py:203

commit v9 on v8

--- a/solution.py
+++ b/solution.py
@@ -179,24 +179,26 @@
     )
     arrived = lax.all_to_all(payload, "expert", split_axis=0, concat_axis=0, tiled=True)
     summary_all = lax.all_gather(summary, "tensor", axis=1, tiled=True)
-    held = jnp.swapaxes(arrived[:, : 2 * slab].reshape(expert_count, 2, slab, 128), 1, 2)
-    held = held.reshape(expert_count * slab, columns)
-    held, summary_all = lax.optimization_barrier((held, summary_all))
-    rows_in = arrived[:, 2 * slab :].reshape(expert_count, lanes, places, 128)
-    rows_in = jnp.swapaxes(rows_in, 1, 2).reshape(expert_count * places, quarter)
-
-    copies = jnp.broadcast_to(held[None], (lax.axis_size("group"),) + held.shape)
-    whole = lax.all_to_all(copies, "group", split_axis=0, concat_axis=0, tiled=True)
-    rows_far = flip(rows_in, "tensor", 2)
-    rows_core = flip(rows_in, "tensor", 1)
-    rows_diag = flip(rows_far, "tensor", 1)
-
     logits = jnp.einsum("sbc,ce->sbe", summary_all, router, preferred_element_type=jnp.float32)
     gate_prob = jax.nn.sigmoid(logits)
     chosen = jnp.sum(picked * gate_prob[:, :, None, :], -1)
     route_weight = (ROUTE_SCALE * chosen / jnp.sum(chosen, -1, keepdims=True)).astype(jnp.bfloat16)
     expert_weight = jnp.sum(picked * route_weight.astype(jnp.float32)[..., None], 2)
     combine = (slot_hit * expert_weight[..., None]).astype(jnp.bfloat16)
+
+    held = jnp.swapaxes(arrived[:, : 2 * slab].reshape(expert_count, 2, slab, 128), 1, 2)
+    held = held.reshape(expert_count * slab, columns)
+    held, combine, first_new, second_new, attention_out = lax.optimization_barrier(
+        (held, combine, first_new, second_new, attention_out)
+    )
+    rows_in = arrived[:, 2 * slab :].reshape(expert_count, lanes, places, 128)
+    rows_in = jnp.swapaxes(rows_in, 1, 2).reshape(expert_count * places, quarter)
+
+    copies = jnp.broadcast_to(held[None], (lax.axis_size("group"),) + held.shape)
+    whole = lax.all_to_all(copies, "group", split_axis=0, concat_axis=0, tiled=True)
+    rows_far = flip(rows_in, "tensor", 2)
+    rows_core = flip(rows_in, "tensor", 1)
+    rows_diag = flip(rows_far, "tensor", 1)
 
     active = expert_rows((rows_in, rows_core, rows_far, rows_diag), whole)
     active = active.reshape(expert_count, places, columns)

time: 134 us -> 134 us (level)
  blocking collectives: 5.19 us -> 31 us
  waiting for transfers between devices: 66.5 us -> 47.3 us
  starting transfers between devices: 41 us -> 32.3 us
  matrix products: 3.14 us -> 7.28 us
    all_to_all x0 -> x1, blocking collectives: none -> 25.8 us  [local(): lax.all_to_all(active, 'expert', split_axis=0, concat_axis=0, tiled=True)]
    all_to_all x1 -> x0, waiting for transfers between devices: 16.8 us -> none  [local(): lax.all_to_all(active, 'expert', split_axis=0, concat_axis=0, tiled=True)]
    all_to_all x1 -> x0, starting transfers between devices: 8.64 us -> none  [local(): lax.all_to_all(active, 'expert', split_axis=0, concat_axis=0, tiled=True)]
    all_to_all x1, waiting for transfers between devices: 39.4 us -> 32.1 us  [local(): lax.all_to_all(payload, 'expert', split_axis=0, concat_axis=0, tiled=True)]
    all_to_all x1, waiting for transfers between devices: 2.84 us -> 5.83 us  [local(): lax.all_to_all(copies, 'group', split_axis=0, concat_axis=0, tiled=True)]
    ppermute x3, waiting for transfers between devices: 7.51 us -> 9.41 us  [flip(): return lax.ppermute(value, axis, [(i, i ^ distance) for i in range(size)])]
    add x1, other arithmetic: 3.24 us -> 1.52 us  [adamw(): BETA_TWO * moment_two + (1.0 - BETA_TWO) * grad_wide * grad_wide]
  transfers between devices with their start and end apart: 7 -> 6, of which waited for: 4 -> 4; matrix products, arithmetic and copies ran while one was open for 9% -> 11% of each run, Pallas kernels for 0% -> 0%
where the time goes in v9:
time: 134 us; the launch traced here: 133 us
  waiting for transfers between devices  47.3 us (35%)
  starting transfers between devices  32.3 us (24%)
  blocking collectives  31 us (23%)
  matrix products  7.28 us (5%)
  other arithmetic  6.46 us (5%)
  local copies, waits for them, and re-layouts  5.74 us (4%)
  between operations  1.65 us (1%)
  Pallas kernels  1.43 us (1%)
    all_to_all x1, waiting for transfers between devices, local(): lax.all_to_all(payload, 'expert', split_axis=0, concat_axis=0, tiled=True)  32.1 us
    all_to_all x1, blocking collectives, local(): lax.all_to_all(active, 'expert', split_axis=0, concat_axis=0, tiled=True)  25.8 us
    all_to_all x1, starting transfers between devices, local(): lax.all_to_all(payload, 'expert', split_axis=0, concat_axis=0, tiled=True)  12 us
    ppermute x3, waiting for transfers between devices, flip(): return lax.ppermute(value, axis, [(i, i ^ distance) for i in range(size)])  9.41 us
    all_to_all x1, starting transfers between devices, local(): lax.all_to_all(jnp.swapaxes(hidden_in.reshape(step_count, 4, quarter), 0,...  9.28 us
    ppermute x3, starting transfers between devices, flip(): return lax.ppermute(value, axis, [(i, i ^ distance) for i in range(size)])  6.6 us
    all_to_all x1, waiting for transfers between devices, local(): lax.all_to_all(copies, 'group', split_axis=0, concat_axis=0, tiled=True)  5.83 us
    all_gather x1, blocking collectives, local(): summary_all = lax.all_gather(summary, 'tensor', axis=1, tiled=True)  5.19 us
  transfers between devices with their start and end apart: 6, of which 4 were waited for; matrix products, arithmetic and copies ran while one was open for 11% of the time, Pallas kernels for 0%

profile of v9, /device:TPU:2, one launch (start us, length us, event | category | flops | bytes accessed | tf_op | source)
XLA Modules:
  0.0 133.2 jit_solution(5136542623685124295)
XLA Ops:
  0.6 9.3 %all-to-all-start = ((bf16[4,4,896]{2,1,0:T(4,128)(2,1)}), bf16[4,4,896]{2,1,0:T(4,128)(2,1)S(1)}, u32[]{:S(2)}, u32[]{:S(2)}) async-start(bf16[4,4,896]{2,1,0:T(4,128)(2,1)} %bitcast.138), calls=%async_computation | async-start | bytes 57344 | tf_op jit(solution)/shard_map/all_to_all | solution.py:129
  9.9 0.8 convert_reduce_fusion
  11.1 0.2 convert_element_type.86
  11.2 2.6 %fusion.15 = bf16[32,28,256]{2,0,1:T(8,128)(2,1)S(1)} fusion(bf16[32,28,256]{2,0,1:T(8,128)(2,1)} %param.14, bf16[32,28,256]{2,0,1:T(8,128)(2,1)} %param.15, f32[32,28,256]{2,0,1:T(8,128)} %param.17, f32[32,28,256]{2,0,1:T(8,128)} %param.16), kind=kLoop, calls=%fused_computation.28 | loop fusion | flops 4128768 | bytes 3211264 | tf_op jit(solution)/shard_map/convert_element_type | solution.py:32
  13.8 0.5 iota_compare_fusion.3
  15.2 0.2 fusion
  15.7 1.3 copy.55
  16.9 12.0 %all-to-all-start.1 = ((bf16[32,112,128]{2,1,0:T(8,128)(2,1)}), bf16[32,112,128]{2,1,0:T(8,128)(2,1)S(1)}, u32[]{:S(2)}, u32[]{:S(2)}) async-start(bf16[32,112,128]{2,1,0:T(8,128)(2,1)} %copy.55), calls=%async_computation.1 | async-start | bytes 1835008 | tf_op jit(solution)/shard_map/all_to_all | solution.py:180
  29.1 1.2 fusion.27
  30.3 0.9 fusion.52
  31.2 0.9 fusion.36
  32.1 1.2 fusion.51
  33.5 0.2 convolution_bitcast_fusion
  33.8 0.9 fusion.50
  34.7 1.6 %convert_element_type.99 = bf16[4,1,16384]{2,0,1:T(4,128)(2,1)} reshape(bf16[4,1,32,512]{3,2,0,1:T(8,128)(2,1)} %get-tuple-element.40) | data formatting | bytes 262144 | tf_op jit(solution)/shard_map/convert_element_type | solution.py:66
  36.5 5.2 %all_gather.3 = bf16[4,4,512]{2,0,1:T(4,128)(2,1)S(1)} all-gather(bf16[4,1,512]{2,0,1:T(4,128)(2,1)S(1)} %fusion.40), channel_id=1, replica_groups=mesh['group'=4,'expert'=32,'tensor'=4] {'tensor'}, dimensions={1}, use_global_device_ids=true | all-gather | bytes 20480 | tf_op jit(solution)/shard_map/all_gather | solution.py:181
  41.7 0.9 fusion.11
  42.6 0.2 select_reduce_fusion
  43.1 1.5 %fusion.24 = (f32[32,28,256]{2,0,1:T(8,128)}, f32[32,28,256]{2,0,1:T(8,128)}) fusion(bf16[32,28,256]{2,0,1:T(8,128)(2,1)S(1)} %copy-done.3, f32[32,28,256]{2,0,1:T(8,128)S(1)} %copy-done.1, f32[32,28,256]{2,0,1:T(8,128)S(1)} %copy-done.2), kind=kLoop, calls=%fused_computation.37 | loop fusion | flops 1835008 | bytes 4128768 | tf_op jit(solution)/shard_map/add | solution.py:29
  44.6 32.1 %all-to-all-done.1 = bf16[32,112,128]{2,1,0:T(8,128)(2,1)S(1)} async-done(((bf16[32,112,128]{2,1,0:T(8,128)(2,1)}), bf16[32,112,128]{2,1,0:T(8,128)(2,1)S(1)}, u32[]{:S(2)}, u32[]{:S(2)}) %all-to-all-start.1) | async-done | bytes 917536 | tf_op jit(solution)/shard_map/all_to_all | solution.py:180
  76.9 0.5 copy.57
  77.4 1.4 %broadcast_in_dim.30 = bf16[4,896,256]{2,1,0:T(8,128)(2,1)} broadcast(bf16[896,256]{1,0:T(8,128)(2,1)S(1)} %bitcast.133), dimensions={1,2} | broadcast | bytes 2293760 | tf_op jit(solution)/shard_map/broadcast_in_dim | solution.py:197
  78.8 4.5 %all-to-all-start.2 = ((bf16[4,896,256]{2,1,0:T(8,128)(2,1)}), bf16[4,896,256]{2,1,0:T(8,128)(2,1)S(1)}, u32[]{:S(2)}, u32[]{:S(2)}) async-start(bf16[4,896,256]{2,1,0:T(8,128)(2,1)} %broadcast_in_dim.30), calls=%async_computation.2 | async-start | bytes 3670016 | tf_op jit(solution)/shard_map/all_to_all | solution.py:198
  83.3 2.8 %collective-permute-start.1 = (bf16[256,896]{1,0:T(8,128)(2,1)S(1)}, bf16[256,896]{1,0:T(8,128)(2,1)S(1)}, u32[]{:S(2)}, u32[]{:S(2)}) collective-permute-start(bf16[256,896]{1,0:T(8,128)(2,1)S(1)} %get-tuple-element.36.own), channel_id=1, source_target_pairs={{0,2},{1,3},{2,0},{3,1},{4,6},{5,7},{6,4},{7,5},{8,10},{9,11},{10,... | collective-permute-start | bytes 1376264 | tf_op jit(solution)/shard_map/ppermute | solution.py:72
  86.0 1.9 %collective-permute-start = (bf16[256,896]{1,0:T(8,128)(2,1)S(1)}, bf16[256,896]{1,0:T(8,128)(2,1)S(1)}, u32[]{:S(2)}, u32[]{:S(2)}) collective-permute-start(bf16[256,896]{1,0:T(8,128)(2,1)S(1)} %get-tuple-element.36.own), channel_id=1, source_target_pairs={{0,1},{1,0},{2,3},{3,2},{4,5},{5,4},{6,7},{7,6},{8,9},{9,8},{10,11... | collective-permute-start | bytes 1376264 | tf_op jit(solution)/shard_map/ppermute | solution.py:72
  88.0 7.5 %collective-permute-done.1.far = bf16[256,896]{1,0:T(8,128)(2,1)S(1)} collective-permute-done((bf16[256,896]{1,0:T(8,128)(2,1)S(1)}, bf16[256,896]{1,0:T(8,128)(2,1)S(1)}, u32[]{:S(2)}, u32[]{:S(2)}) %collective-permute-start.1) | collective-permute-done | bytes 458784 | tf_op jit(solution)/shard_map/ppermute | solution.py:72
  95.5 1.9 %collective-permute-start.2 = (bf16[256,896]{1,0:T(8,128)(2,1)S(1)}, bf16[256,896]{1,0:T(8,128)(2,1)}, u32[]{:S(2)}, u32[]{:S(2)}) collective-permute-start(bf16[256,896]{1,0:T(8,128)(2,1)S(1)} %collective-permute-done.1.far), channel_id=1, source_target_pairs={{0,1},{1,0},{2,3},{3,2},{4,5},{5,4},{6,7},{7,6},{8,9},{9,8},{10,11... | collective-permute-start | bytes 1376264 | tf_op jit(solution)/shard_map/ppermute | solution.py:72
  97.4 1.9 %collective-permute-done.2.diag = bf16[256,896]{1,0:T(8,128)(2,1)} collective-permute-done((bf16[256,896]{1,0:T(8,128)(2,1)S(1)}, bf16[256,896]{1,0:T(8,128)(2,1)}, u32[]{:S(2)}, u32[]{:S(2)}) %collective-permute-start.2) | collective-permute-done | bytes 458784 | tf_op jit(solution)/shard_map/ppermute | solution.py:72
  99.3 5.8 %all-to-all-done.2.whole = bf16[4,896,256]{2,1,0:T(8,128)(2,1)S(1)} async-done(((bf16[4,896,256]{2,1,0:T(8,128)(2,1)}), bf16[4,896,256]{2,1,0:T(8,128)(2,1)S(1)}, u32[]{:S(2)}, u32[]{:S(2)}) %all-to-all-start.2) | async-done | bytes 1835040 | tf_op jit(solution)/shard_map/all_to_all | solution.py:198
  105.1 1.4 %shard_map.165 = bf16[256,256]{1,0:T(8,128)(2,1)S(1)} custom-call(s32[1]{0:T(128)} %bitcast.33.turn, bf16[256,896]{1,0:T(8,128)(2,1)S(1)} %get-tuple-element.36.own, bf16[256,896]{1,0:T(8,128)(2,1)S(1)} %collective-permute-done.core, bf16[256,896]{1,0:T(8,128)(2,1)S(1)} %collective-permute-done.1.far, bf16[256,896]{1,0:T(8,128)(2,1)} %collective-permute-done.2.diag, ...), custom_call_target="tpu_custom_call" | custom-call | flops 469762048 | bytes 3670016 | tf_op jit(solution)/shard_map/pallas_call | solution.py:93
  106.6 25.8 %all_to_all.20 = bf16[32,8,256]{2,1,0:T(8,128)(2,1)S(1)} all-to-all(bf16[32,8,256]{2,1,0:T(8,128)(2,1)S(1)} %bitcast.127), channel_id=1, replica_groups=mesh['group'=4,'expert'=32,'tensor'=4] {'expert'}, dimensions={0} | all-to-all | bytes 262144 | tf_op jit(solution)/shard_map/all_to_all | solution.py:205
  132.4 0.8 fusion.6
  (46 shorter events, 1.7 us)
Async XLA Ops:
  0.6 31.5 %copy-start = (bf16[1,256,512]{2,1,0:T(8,128)(2,1)S(1)}, bf16[1,256,512]{2,1,0:T(8,128)(2,1)}, u32[]{:S(2)}) copy-start(bf16[1,256,512]{2,1,0:T(8,128)(2,1)} %param.21) | copy-start | bytes 786436
  0.6 14.5 %all-to-all-start = ((bf16[4,4,896]{2,1,0:T(4,128)(2,1)}), bf16[4,4,896]{2,1,0:T(4,128)(2,1)S(1)}, u32[]{:S(2)}, u32[]{:S(2)}) async-start(bf16[4,4,896]{2,1,0:T(4,128)(2,1)} %bitcast.138), calls=%async_computation | async-start | bytes 57344 | tf_op jit(solution)/shard_map/all_to_all | solution.py:129
  15.6 13.3 %copy-start.6 = (bf16[4,1,2048]{2,0,1:T(4,128)(2,1)S(1)}, bf16[4,1,2048]{2,0,1:T(4,128)(2,1)}, u32[]{:S(2)}) copy-start(bf16[4,1,2048]{2,0,1:T(4,128)(2,1)} %param.20) | copy-start | bytes 49156
  15.7 13.4 %copy-start.5 = (bf16[4,1,512]{2,0,1:T(4,128)(2,1)S(1)}, bf16[4,1,512]{2,0,1:T(4,128)(2,1)}, u32[]{:S(2)}) copy-start(bf16[4,1,512]{2,0,1:T(4,128)(2,1)} %param.23) | copy-start | bytes 12292
  16.9 59.8 %all-to-all-start.1 = ((bf16[32,112,128]{2,1,0:T(8,128)(2,1)}), bf16[32,112,128]{2,1,0:T(8,128)(2,1)S(1)}, u32[]{:S(2)}, u32[]{:S(2)}) async-start(bf16[32,112,128]{2,1,0:T(8,128)(2,1)} %copy.55), calls=%async_computation.1 | async-start | bytes 1835008 | tf_op jit(solution)/shard_map/all_to_all | solution.py:180
  28.9 13.7 %copy-start.4 = (s32[4,4,8]{2,1,0:T(4,128)S(1)}, s32[4,4,8]{2,1,0:T(4,128)}, u32[]{:S(2)}) copy-start(s32[4,4,8]{2,1,0:T(4,128)} %param.26) | copy-start | bytes 1540
  28.9 14.1 %copy-start.1 = (f32[32,28,256]{2,0,1:T(8,128)S(1)}, f32[32,28,256]{2,0,1:T(8,128)}, u32[]{:S(2)}) copy-start(f32[32,28,256]{2,0,1:T(8,128)} %param.17) | copy-start | bytes 2752516
  28.9 14.1 %copy-start.2 = (f32[32,28,256]{2,0,1:T(8,128)S(1)}, f32[32,28,256]{2,0,1:T(8,128)}, u32[]{:S(2)}) copy-start(f32[32,28,256]{2,0,1:T(8,128)} %param.16) | copy-start | bytes 2752516
  28.9 14.1 %copy-start.3 = (bf16[32,28,256]{2,0,1:T(8,128)(2,1)S(1)}, bf16[32,28,256]{2,0,1:T(8,128)(2,1)}, u32[]{:S(2)}) copy-start(bf16[32,28,256]{2,0,1:T(8,128)(2,1)} %param.15) | copy-start | bytes 1376260
  78.8 26.3 %all-to-all-start.2 = ((bf16[4,896,256]{2,1,0:T(8,128)(2,1)}), bf16[4,896,256]{2,1,0:T(8,128)(2,1)S(1)}, u32[]{:S(2)}, u32[]{:S(2)}) async-start(bf16[4,896,256]{2,1,0:T(8,128)(2,1)} %broadcast_in_dim.30), calls=%async_computation.2 | async-start | bytes 3670016 | tf_op jit(solution)/shard_map/all_to_all | solution.py:198
  83.3 12.2 %collective-permute-start.1 = (bf16[256,896]{1,0:T(8,128)(2,1)S(1)}, bf16[256,896]{1,0:T(8,128)(2,1)S(1)}, u32[]{:S(2)}, u32[]{:S(2)}) collective-permute-start(bf16[256,896]{1,0:T(8,128)(2,1)S(1)} %get-tuple-element.36.own), channel_id=1, source_target_pairs={{0,2},{1,3},{2,0},{3,1},{4,6},{5,7},{6,4},{7,5},{8,10},{9,11},{10,... | collective-permute-start | bytes 1376264 | tf_op jit(solution)/shard_map/ppermute | solution.py:72
  86.0 11.4 %collective-permute-start = (bf16[256,896]{1,0:T(8,128)(2,1)S(1)}, bf16[256,896]{1,0:T(8,128)(2,1)S(1)}, u32[]{:S(2)}, u32[]{:S(2)}) collective-permute-start(bf16[256,896]{1,0:T(8,128)(2,1)S(1)} %get-tuple-element.36.own), channel_id=1, source_target_pairs={{0,1},{1,0},{2,3},{3,2},{4,5},{5,4},{6,7},{7,6},{8,9},{9,8},{10,11... | collective-permute-start | bytes 1376264 | tf_op jit(solution)/shard_map/ppermute | solution.py:72
  95.5 3.8 %collective-permute-start.2 = (bf16[256,896]{1,0:T(8,128)(2,1)S(1)}, bf16[256,896]{1,0:T(8,128)(2,1)}, u32[]{:S(2)}, u32[]{:S(2)}) collective-permute-start(bf16[256,896]{1,0:T(8,128)(2,1)S(1)} %collective-permute-done.1.far), channel_id=1, source_target_pairs={{0,1},{1,0},{2,3},{3,2},{4,5},{5,4},{6,7},{7,6},{8,9},{9,8},{10,11... | collective-permute-start | bytes 1376264 | tf_op jit(solution)/shard_map/ppermute | solution.py:72

commit v10 on v9

--- a/solution.py
+++ b/solution.py
@@ -158,20 +158,11 @@
     outgoing = outgoing.reshape(expert_count, places * lanes, 128)
     slabs = jnp.swapaxes(updated.reshape(expert_count, slab, 2, 128), 1, 2)
     slabs = slabs.reshape(expert_count, 2 * slab, 128)
-    outgoing, query_latent, query_rope, new_latent, new_rope, gradients, moment_one, moment_two = (
-        lax.optimization_barrier(
-            (
-                outgoing,
-                query_latent,
-                query_rope,
-                new_latent,
-                new_rope,
-                gradients,
-                moment_one,
-                moment_two,
-            )
-        )
-    )
+    later = (query_latent, query_rope, cache_rope, new_latent, new_rope, lengths)
+    later = later + (gradients, moment_one, moment_two)
+    outgoing, later = lax.optimization_barrier((outgoing, later))
+    query_latent, query_rope, cache_rope, new_latent, new_rope, lengths = later[:6]
+    gradients, moment_one, moment_two = later[6:]
     payload = jnp.concatenate([slabs, outgoing], 1)
     first_new, second_new, _ = adamw(weights, gradients, moment_one, moment_two)
     attention_out, summary = attend(

time: 134 us -> 134 us (level)
  no operation moved by 1% of the time
where the time goes in v10:
time: 134 us; the launch traced here: 133 us
  waiting for transfers between devices  47.3 us (35%)
  starting transfers between devices  32.3 us (24%)
  blocking collectives  31 us (23%)
  matrix products  7.29 us (5%)
  other arithmetic  6.46 us (5%)
  local copies, waits for them, and re-layouts  5.74 us (4%)
  between operations  1.64 us (1%)
  Pallas kernels  1.43 us (1%)
    all_to_all x1, waiting for transfers between devices, local(): lax.all_to_all(payload, 'expert', split_axis=0, concat_axis=0, tiled=True)  32.1 us
    all_to_all x1, blocking collectives, local(): lax.all_to_all(active, 'expert', split_axis=0, concat_axis=0, tiled=True)  25.8 us
    all_to_all x1, starting transfers between devices, local(): lax.all_to_all(payload, 'expert', split_axis=0, concat_axis=0, tiled=True)  12 us
    ppermute x3, waiting for transfers between devices, flip(): return lax.ppermute(value, axis, [(i, i ^ distance) for i in range(size)])  9.41 us
    all_to_all x1, starting transfers between devices, local(): lax.all_to_all(jnp.swapaxes(hidden_in.reshape(step_count, 4, quarter), 0,...  9.28 us
    ppermute x3, starting transfers between devices, flip(): return lax.ppermute(value, axis, [(i, i ^ distance) for i in range(size)])  6.6 us
    all_to_all x1, waiting for transfers between devices, local(): lax.all_to_all(copies, 'group', split_axis=0, concat_axis=0, tiled=True)  5.83 us
    all_gather x1, blocking collectives, local(): summary_all = lax.all_gather(summary, 'tensor', axis=1, tiled=True)  5.19 us
  transfers between devices with their start and end apart: 6, of which 4 were waited for; matrix products, arithmetic and copies ran while one was open for 11% of the time, Pallas kernels for 0%

profile of v10, /device:TPU:2, one launch (start us, length us, event | category | flops | bytes accessed | tf_op | source)
XLA Modules:
  0.0 133.2 jit_solution(14117320741805673933)
XLA Ops:
  0.6 9.3 %all-to-all-start = ((bf16[4,4,896]{2,1,0:T(4,128)(2,1)}), bf16[4,4,896]{2,1,0:T(4,128)(2,1)S(1)}, u32[]{:S(2)}, u32[]{:S(2)}) async-start(bf16[4,4,896]{2,1,0:T(4,128)(2,1)} %bitcast.148), calls=%async_computation | async-start | bytes 57344 | tf_op jit(solution)/shard_map/all_to_all | solution.py:129
  9.9 0.8 convert_reduce_fusion
  11.1 0.2 convert_element_type.86
  11.2 2.6 %fusion.16 = bf16[32,28,256]{2,0,1:T(8,128)(2,1)S(1)} fusion(bf16[32,28,256]{2,0,1:T(8,128)(2,1)} %param.14, bf16[32,28,256]{2,0,1:T(8,128)(2,1)} %param.15, f32[32,28,256]{2,0,1:T(8,128)} %param.17, f32[32,28,256]{2,0,1:T(8,128)} %param.16), kind=kLoop, calls=%fused_computation.29 | loop fusion | flops 4128768 | bytes 3211264 | tf_op jit(solution)/shard_map/convert_element_type | solution.py:32
  13.8 0.5 iota_compare_fusion.3
  15.2 0.2 fusion
  15.7 1.3 copy.55
  16.9 12.0 %all-to-all-start.1 = ((bf16[32,112,128]{2,1,0:T(8,128)(2,1)}), bf16[32,112,128]{2,1,0:T(8,128)(2,1)S(1)}, u32[]{:S(2)}, u32[]{:S(2)}) async-start(bf16[32,112,128]{2,1,0:T(8,128)(2,1)} %copy.55), calls=%async_computation.1 | async-start | bytes 1835008 | tf_op jit(solution)/shard_map/all_to_all | solution.py:171
  29.1 1.2 fusion.28
  30.3 0.9 fusion.53
  31.2 0.9 fusion.37
  32.1 1.2 fusion.52
  33.5 0.2 convolution_bitcast_fusion
  33.8 0.9 fusion.51
  34.7 1.6 %convert_element_type.99 = bf16[4,1,16384]{2,0,1:T(4,128)(2,1)} reshape(bf16[4,1,32,512]{3,2,0,1:T(8,128)(2,1)} %get-tuple-element.44) | data formatting | bytes 262144 | tf_op jit(solution)/shard_map/convert_element_type | solution.py:66
  36.5 5.2 %all_gather.3 = bf16[4,4,512]{2,0,1:T(4,128)(2,1)S(1)} all-gather(bf16[4,1,512]{2,0,1:T(4,128)(2,1)S(1)} %fusion.41), channel_id=1, replica_groups=mesh['group'=4,'expert'=32,'tensor'=4] {'tensor'}, dimensions={1}, use_global_device_ids=true | all-gather | bytes 20480 | tf_op jit(solution)/shard_map/all_gather | solution.py:172
  41.7 0.9 fusion.12
  42.6 0.2 select_reduce_fusion
  43.1 1.5 %fusion.25 = (f32[32,28,256]{2,0,1:T(8,128)}, f32[32,28,256]{2,0,1:T(8,128)}) fusion(bf16[32,28,256]{2,0,1:T(8,128)(2,1)S(1)} %copy-done.3, f32[32,28,256]{2,0,1:T(8,128)S(1)} %copy-done.1, f32[32,28,256]{2,0,1:T(8,128)S(1)} %copy-done.2), kind=kLoop, calls=%fused_computation.38 | loop fusion | flops 1835008 | bytes 4128768 | tf_op jit(solution)/shard_map/add | solution.py:29
  44.6 32.1 %all-to-all-done.1 = bf16[32,112,128]{2,1,0:T(8,128)(2,1)S(1)} async-done(((bf16[32,112,128]{2,1,0:T(8,128)(2,1)}), bf16[32,112,128]{2,1,0:T(8,128)(2,1)S(1)}, u32[]{:S(2)}, u32[]{:S(2)}) %all-to-all-start.1) | async-done | bytes 917536 | tf_op jit(solution)/shard_map/all_to_all | solution.py:171
  76.9 0.5 copy.57
  77.4 1.4 %broadcast_in_dim.30 = bf16[4,896,256]{2,1,0:T(8,128)(2,1)} broadcast(bf16[896,256]{1,0:T(8,128)(2,1)S(1)} %bitcast.143), dimensions={1,2} | broadcast | bytes 2293760 | tf_op jit(solution)/shard_map/broadcast_in_dim | solution.py:188
  78.8 4.5 %all-to-all-start.2 = ((bf16[4,896,256]{2,1,0:T(8,128)(2,1)}), bf16[4,896,256]{2,1,0:T(8,128)(2,1)S(1)}, u32[]{:S(2)}, u32[]{:S(2)}) async-start(bf16[4,896,256]{2,1,0:T(8,128)(2,1)} %broadcast_in_dim.30), calls=%async_computation.2 | async-start | bytes 3670016 | tf_op jit(solution)/shard_map/all_to_all | solution.py:189
  83.3 2.8 %collective-permute-start.1 = (bf16[256,896]{1,0:T(8,128)(2,1)S(1)}, bf16[256,896]{1,0:T(8,128)(2,1)S(1)}, u32[]{:S(2)}, u32[]{:S(2)}) collective-permute-start(bf16[256,896]{1,0:T(8,128)(2,1)S(1)} %get-tuple-element.40.own), channel_id=1, source_target_pairs={{0,2},{1,3},{2,0},{3,1},{4,6},{5,7},{6,4},{7,5},{8,10},{9,11},{10,... | collective-permute-start | bytes 1376264 | tf_op jit(solution)/shard_map/ppermute | solution.py:72
  86.0 1.9 %collective-permute-start = (bf16[256,896]{1,0:T(8,128)(2,1)S(1)}, bf16[256,896]{1,0:T(8,128)(2,1)S(1)}, u32[]{:S(2)}, u32[]{:S(2)}) collective-permute-start(bf16[256,896]{1,0:T(8,128)(2,1)S(1)} %get-tuple-element.40.own), channel_id=1, source_target_pairs={{0,1},{1,0},{2,3},{3,2},{4,5},{5,4},{6,7},{7,6},{8,9},{9,8},{10,11... | collective-permute-start | bytes 1376264 | tf_op jit(solution)/shard_map/ppermute | solution.py:72
  88.0 7.5 %collective-permute-done.1.far = bf16[256,896]{1,0:T(8,128)(2,1)S(1)} collective-permute-done((bf16[256,896]{1,0:T(8,128)(2,1)S(1)}, bf16[256,896]{1,0:T(8,128)(2,1)S(1)}, u32[]{:S(2)}, u32[]{:S(2)}) %collective-permute-start.1) | collective-permute-done | bytes 458784 | tf_op jit(solution)/shard_map/ppermute | solution.py:72
  95.5 1.9 %collective-permute-start.2 = (bf16[256,896]{1,0:T(8,128)(2,1)S(1)}, bf16[256,896]{1,0:T(8,128)(2,1)}, u32[]{:S(2)}, u32[]{:S(2)}) collective-permute-start(bf16[256,896]{1,0:T(8,128)(2,1)S(1)} %collective-permute-done.1.far), channel_id=1, source_target_pairs={{0,1},{1,0},{2,3},{3,2},{4,5},{5,4},{6,7},{7,6},{8,9},{9,8},{10,11... | collective-permute-start | bytes 1376264 | tf_op jit(solution)/shard_map/ppermute | solution.py:72
  97.4 1.9 %collective-permute-done.2.diag = bf16[256,896]{1,0:T(8,128)(2,1)} collective-permute-done((bf16[256,896]{1,0:T(8,128)(2,1)S(1)}, bf16[256,896]{1,0:T(8,128)(2,1)}, u32[]{:S(2)}, u32[]{:S(2)}) %collective-permute-start.2) | collective-permute-done | bytes 458784 | tf_op jit(solution)/shard_map/ppermute | solution.py:72
  99.3 5.8 %all-to-all-done.2.whole = bf16[4,896,256]{2,1,0:T(8,128)(2,1)S(1)} async-done(((bf16[4,896,256]{2,1,0:T(8,128)(2,1)}), bf16[4,896,256]{2,1,0:T(8,128)(2,1)S(1)}, u32[]{:S(2)}, u32[]{:S(2)}) %all-to-all-start.2) | async-done | bytes 1835040 | tf_op jit(solution)/shard_map/all_to_all | solution.py:189
  105.1 1.4 %shard_map.165 = bf16[256,256]{1,0:T(8,128)(2,1)S(1)} custom-call(s32[1]{0:T(128)} %bitcast.33.turn, bf16[256,896]{1,0:T(8,128)(2,1)S(1)} %get-tuple-element.40.own, bf16[256,896]{1,0:T(8,128)(2,1)S(1)} %collective-permute-done.core, bf16[256,896]{1,0:T(8,128)(2,1)S(1)} %collective-permute-done.1.far, bf16[256,896]{1,0:T(8,128)(2,1)} %collective-permute-done.2.diag, ...), custom_call_target="tpu_custom_call" | custom-call | flops 469762048 | bytes 3670016 | tf_op jit(solution)/shard_map/pallas_call | solution.py:93
  106.6 25.8 %all_to_all.20 = bf16[32,8,256]{2,1,0:T(8,128)(2,1)S(1)} all-to-all(bf16[32,8,256]{2,1,0:T(8,128)(2,1)S(1)} %bitcast.137), channel_id=1, replica_groups=mesh['group'=4,'expert'=32,'tensor'=4] {'expert'}, dimensions={0} | all-to-all | bytes 262144 | tf_op jit(solution)/shard_map/all_to_all | solution.py:196
  132.4 0.8 fusion.7
  (46 shorter events, 1.7 us)
Async XLA Ops:
  0.6 31.5 %copy-start = (bf16[1,256,512]{2,1,0:T(8,128)(2,1)S(1)}, bf16[1,256,512]{2,1,0:T(8,128)(2,1)}, u32[]{:S(2)}) copy-start(bf16[1,256,512]{2,1,0:T(8,128)(2,1)} %param.21) | copy-start | bytes 786436
  0.6 14.5 %all-to-all-start = ((bf16[4,4,896]{2,1,0:T(4,128)(2,1)}), bf16[4,4,896]{2,1,0:T(4,128)(2,1)S(1)}, u32[]{:S(2)}, u32[]{:S(2)}) async-start(bf16[4,4,896]{2,1,0:T(4,128)(2,1)} %bitcast.148), calls=%async_computation | async-start | bytes 57344 | tf_op jit(solution)/shard_map/all_to_all | solution.py:129
  15.6 13.3 %copy-start.6 = (bf16[4,1,2048]{2,0,1:T(4,128)(2,1)S(1)}, bf16[4,1,2048]{2,0,1:T(4,128)(2,1)}, u32[]{:S(2)}) copy-start(bf16[4,1,2048]{2,0,1:T(4,128)(2,1)} %param.20) | copy-start | bytes 49156
  15.7 13.4 %copy-start.5 = (bf16[4,1,512]{2,0,1:T(4,128)(2,1)S(1)}, bf16[4,1,512]{2,0,1:T(4,128)(2,1)}, u32[]{:S(2)}) copy-start(bf16[4,1,512]{2,0,1:T(4,128)(2,1)} %param.23) | copy-start | bytes 12292
  16.9 59.8 %all-to-all-start.1 = ((bf16[32,112,128]{2,1,0:T(8,128)(2,1)}), bf16[32,112,128]{2,1,0:T(8,128)(2,1)S(1)}, u32[]{:S(2)}, u32[]{:S(2)}) async-start(bf16[32,112,128]{2,1,0:T(8,128)(2,1)} %copy.55), calls=%async_computation.1 | async-start | bytes 1835008 | tf_op jit(solution)/shard_map/all_to_all | solution.py:171
  28.9 13.7 %copy-start.4 = (s32[4,4,8]{2,1,0:T(4,128)S(1)}, s32[4,4,8]{2,1,0:T(4,128)}, u32[]{:S(2)}) copy-start(s32[4,4,8]{2,1,0:T(4,128)} %param.26) | copy-start | bytes 1540
  28.9 14.1 %copy-start.1 = (f32[32,28,256]{2,0,1:T(8,128)S(1)}, f32[32,28,256]{2,0,1:T(8,128)}, u32[]{:S(2)}) copy-start(f32[32,28,256]{2,0,1:T(8,128)} %param.17) | copy-start | bytes 2752516
  28.9 14.1 %copy-start.2 = (f32[32,28,256]{2,0,1:T(8,128)S(1)}, f32[32,28,256]{2,0,1:T(8,128)}, u32[]{:S(2)}) copy-start(f32[32,28,256]{2,0,1:T(8,128)} %param.16) | copy-start | bytes 2752516
  28.9 14.1 %copy-start.3 = (bf16[32,28,256]{2,0,1:T(8,128)(2,1)S(1)}, bf16[32,28,256]{2,0,1:T(8,128)(2,1)}, u32[]{:S(2)}) copy-start(bf16[32,28,256]{2,0,1:T(8,128)(2,1)} %param.15) | copy-start | bytes 1376260
  78.8 26.3 %all-to-all-start.2 = ((bf16[4,896,256]{2,1,0:T(8,128)(2,1)}), bf16[4,896,256]{2,1,0:T(8,128)(2,1)S(1)}, u32[]{:S(2)}, u32[]{:S(2)}) async-start(bf16[4,896,256]{2,1,0:T(8,128)(2,1)} %broadcast_in_dim.30), calls=%async_computation.2 | async-start | bytes 3670016 | tf_op jit(solution)/shard_map/all_to_all | solution.py:189
  83.3 12.2 %collective-permute-start.1 = (bf16[256,896]{1,0:T(8,128)(2,1)S(1)}, bf16[256,896]{1,0:T(8,128)(2,1)S(1)}, u32[]{:S(2)}, u32[]{:S(2)}) collective-permute-start(bf16[256,896]{1,0:T(8,128)(2,1)S(1)} %get-tuple-element.40.own), channel_id=1, source_target_pairs={{0,2},{1,3},{2,0},{3,1},{4,6},{5,7},{6,4},{7,5},{8,10},{9,11},{10,... | collective-permute-start | bytes 1376264 | tf_op jit(solution)/shard_map/ppermute | solution.py:72
  86.0 11.4 %collective-permute-start = (bf16[256,896]{1,0:T(8,128)(2,1)S(1)}, bf16[256,896]{1,0:T(8,128)(2,1)S(1)}, u32[]{:S(2)}, u32[]{:S(2)}) collective-permute-start(bf16[256,896]{1,0:T(8,128)(2,1)S(1)} %get-tuple-element.40.own), channel_id=1, source_target_pairs={{0,1},{1,0},{2,3},{3,2},{4,5},{5,4},{6,7},{7,6},{8,9},{9,8},{10,11... | collective-permute-start | bytes 1376264 | tf_op jit(solution)/shard_map/ppermute | solution.py:72
  95.5 3.8 %collective-permute-start.2 = (bf16[256,896]{1,0:T(8,128)(2,1)S(1)}, bf16[256,896]{1,0:T(8,128)(2,1)}, u32[]{:S(2)}, u32[]{:S(2)}) collective-permute-start(bf16[256,896]{1,0:T(8,128)(2,1)S(1)} %collective-permute-done.1.far), channel_id=1, source_target_pairs={{0,1},{1,0},{2,3},{3,2},{4,5},{5,4},{6,7},{7,6},{8,9},{9,8},{10,11... | collective-permute-start | bytes 1376264 | tf_op jit(solution)/shard_map/ppermute | solution.py:72

commit v11 on v10

--- a/solution.py
+++ b/solution.py
@@ -47,7 +47,8 @@
         + jnp.einsum("srhp,trp->srht", query_pos, new_rope, preferred_element_type=jnp.float32)
     ) * QK_SCALE
     valid_old = jnp.arange(slot_total, dtype=jnp.int32)[None, :] < lengths[:, None]
-    valid_new = jnp.arange(step_count)[None, :] <= jnp.arange(step_count)[:, None]
+    place = lengths[0] + jnp.arange(step_count, dtype=jnp.int32)
+    valid_new = place[None, :] <= place[:, None]
     old_scores = jnp.where(valid_old[None, :, None, :], old_scores, NEGATIVE)
     new_scores = jnp.where(valid_new[:, None, None, :], new_scores, NEGATIVE)
     peak_score = jnp.maximum(
@@ -160,7 +161,7 @@
     slabs = slabs.reshape(expert_count, 2 * slab, 128)
     later = (query_latent, query_rope, cache_rope, new_latent, new_rope, lengths)
     later = later + (gradients, moment_one, moment_two)
-    outgoing, later = lax.optimization_barrier((outgoing, later))
+    outgoing, slabs, later = lax.optimization_barrier((outgoing, slabs, later))
     query_latent, query_rope, cache_rope, new_latent, new_rope, lengths = later[:6]
     gradients, moment_one, moment_two = later[6:]
     payload = jnp.concatenate([slabs, outgoing], 1)

time: 134 us -> 134 us (level)
  no operation moved by 1% of the time
where the time goes in v11:
time: 134 us; the launch traced here: 133 us
  waiting for transfers between devices  47.4 us (35%)
  starting transfers between devices  32.3 us (24%)
  blocking collectives  30.9 us (23%)
  matrix products  7.29 us (5%)
  other arithmetic  6.53 us (5%)
  local copies, waits for them, and re-layouts  5.74 us (4%)
  between operations  1.64 us (1%)
  Pallas kernels  1.43 us (1%)
    all_to_all x1, waiting for transfers between devices, local(): lax.all_to_all(payload, 'expert', split_axis=0, concat_axis=0, tiled=True)  32.1 us
    all_to_all x1, blocking collectives, local(): lax.all_to_all(active, 'expert', split_axis=0, concat_axis=0, tiled=True)  25.8 us
    all_to_all x1, starting transfers between devices, local(): lax.all_to_all(payload, 'expert', split_axis=0, concat_axis=0, tiled=True)  12 us
    ppermute x3, waiting for transfers between devices, flip(): return lax.ppermute(value, axis, [(i, i ^ distance) for i in range(size)])  9.41 us
    all_to_all x1, starting transfers between devices, local(): lax.all_to_all(jnp.swapaxes(hidden_in.reshape(step_count, 4, quarter), 0,...  9.28 us
    ppermute x3, starting transfers between devices, flip(): return lax.ppermute(value, axis, [(i, i ^ distance) for i in range(size)])  6.61 us
    all_to_all x1, waiting for transfers between devices, local(): lax.all_to_all(copies, 'group', split_axis=0, concat_axis=0, tiled=True)  5.83 us
    all_gather x1, blocking collectives, local(): summary_all = lax.all_gather(summary, 'tensor', axis=1, tiled=True)  5.18 us
  transfers between devices with their start and end apart: 6, of which 4 were waited for; matrix products, arithmetic and copies ran while one was open for 11% of the time, Pallas kernels for 0%

profile of v11, /device:TPU:2, one launch (start us, length us, event | category | flops | bytes accessed | tf_op | source)
XLA Modules:
  0.0 133.2 jit_solution(4170682521624089198)
XLA Ops:
  0.6 9.3 %all-to-all-start = ((bf16[4,4,896]{2,1,0:T(4,128)(2,1)}), bf16[4,4,896]{2,1,0:T(4,128)(2,1)S(1)}, u32[]{:S(2)}, u32[]{:S(2)}) async-start(bf16[4,4,896]{2,1,0:T(4,128)(2,1)} %bitcast.149), calls=%async_computation | async-start | bytes 57344 | tf_op jit(solution)/shard_map/all_to_all | solution.py:130
  9.9 0.8 convert_reduce_fusion
  11.1 0.2 convert_element_type.86
  11.9 2.6 %fusion.16 = bf16[32,28,256]{2,0,1:T(8,128)(2,1)S(1)} fusion(bf16[32,28,256]{2,0,1:T(8,128)(2,1)} %param.14, bf16[32,28,256]{2,0,1:T(8,128)(2,1)} %param.15, f32[32,28,256]{2,0,1:T(8,128)} %param.17, f32[32,28,256]{2,0,1:T(8,128)} %param.16), kind=kLoop, calls=%fused_computation.29 | loop fusion | flops 4128768 | bytes 3211264 | tf_op jit(solution)/shard_map/convert_element_type | solution.py:32
  14.5 0.6 broadcast_compare_fusion
  15.3 0.2 fusion
  15.7 1.3 copy.55
  17.0 12.0 %all-to-all-start.1 = ((bf16[32,112,128]{2,1,0:T(8,128)(2,1)}), bf16[32,112,128]{2,1,0:T(8,128)(2,1)S(1)}, u32[]{:S(2)}, u32[]{:S(2)}) async-start(bf16[32,112,128]{2,1,0:T(8,128)(2,1)} %copy.55), calls=%async_computation.1 | async-start | bytes 1835008 | tf_op jit(solution)/shard_map/all_to_all | solution.py:172
  29.2 1.2 fusion.28
  30.4 0.9 fusion.53
  31.3 0.9 fusion.37
  32.2 1.2 fusion.52
  33.6 0.2 convolution_bitcast_fusion
  33.9 0.9 fusion.51
  34.8 1.6 %convert_element_type.99 = bf16[4,1,16384]{2,0,1:T(4,128)(2,1)} reshape(bf16[4,1,32,512]{3,2,0,1:T(8,128)(2,1)} %get-tuple-element.46) | data formatting | bytes 262144 | tf_op jit(solution)/shard_map/convert_element_type | solution.py:67
  36.6 5.2 %all_gather.3 = bf16[4,4,512]{2,0,1:T(4,128)(2,1)S(1)} all-gather(bf16[4,1,512]{2,0,1:T(4,128)(2,1)S(1)} %fusion.41), channel_id=1, replica_groups=mesh['group'=4,'expert'=32,'tensor'=4] {'tensor'}, dimensions={1}, use_global_device_ids=true | all-gather | bytes 20480 | tf_op jit(solution)/shard_map/all_gather | solution.py:173
  41.8 0.9 fusion.12
  42.7 0.2 select_reduce_fusion
  43.1 1.5 %fusion.25 = (f32[32,28,256]{2,0,1:T(8,128)}, f32[32,28,256]{2,0,1:T(8,128)}) fusion(bf16[32,28,256]{2,0,1:T(8,128)(2,1)S(1)} %copy-done.3, f32[32,28,256]{2,0,1:T(8,128)S(1)} %copy-done.1, f32[32,28,256]{2,0,1:T(8,128)S(1)} %copy-done.2), kind=kLoop, calls=%fused_computation.38 | loop fusion | flops 1835008 | bytes 4128768 | tf_op jit(solution)/shard_map/add | solution.py:29
  44.7 32.1 %all-to-all-done.1 = bf16[32,112,128]{2,1,0:T(8,128)(2,1)S(1)} async-done(((bf16[32,112,128]{2,1,0:T(8,128)(2,1)}), bf16[32,112,128]{2,1,0:T(8,128)(2,1)S(1)}, u32[]{:S(2)}, u32[]{:S(2)}) %all-to-all-start.1) | async-done | bytes 917536 | tf_op jit(solution)/shard_map/all_to_all | solution.py:172
  76.9 0.5 copy.57
  77.5 1.4 %broadcast_in_dim.30 = bf16[4,896,256]{2,1,0:T(8,128)(2,1)} broadcast(bf16[896,256]{1,0:T(8,128)(2,1)S(1)} %bitcast.144), dimensions={1,2} | broadcast | bytes 2293760 | tf_op jit(solution)/shard_map/broadcast_in_dim | solution.py:189
  78.9 4.5 %all-to-all-start.2 = ((bf16[4,896,256]{2,1,0:T(8,128)(2,1)}), bf16[4,896,256]{2,1,0:T(8,128)(2,1)S(1)}, u32[]{:S(2)}, u32[]{:S(2)}) async-start(bf16[4,896,256]{2,1,0:T(8,128)(2,1)} %broadcast_in_dim.30), calls=%async_computation.2 | async-start | bytes 3670016 | tf_op jit(solution)/shard_map/all_to_all | solution.py:190
  83.3 2.8 %collective-permute-start.1 = (bf16[256,896]{1,0:T(8,128)(2,1)S(1)}, bf16[256,896]{1,0:T(8,128)(2,1)S(1)}, u32[]{:S(2)}, u32[]{:S(2)}) collective-permute-start(bf16[256,896]{1,0:T(8,128)(2,1)S(1)} %get-tuple-element.42.own), channel_id=1, source_target_pairs={{0,2},{1,3},{2,0},{3,1},{4,6},{5,7},{6,4},{7,5},{8,10},{9,11},{10,... | collective-permute-start | bytes 1376264 | tf_op jit(solution)/shard_map/ppermute | solution.py:73
  86.1 1.9 %collective-permute-start = (bf16[256,896]{1,0:T(8,128)(2,1)S(1)}, bf16[256,896]{1,0:T(8,128)(2,1)S(1)}, u32[]{:S(2)}, u32[]{:S(2)}) collective-permute-start(bf16[256,896]{1,0:T(8,128)(2,1)S(1)} %get-tuple-element.42.own), channel_id=1, source_target_pairs={{0,1},{1,0},{2,3},{3,2},{4,5},{5,4},{6,7},{7,6},{8,9},{9,8},{10,11... | collective-permute-start | bytes 1376264 | tf_op jit(solution)/shard_map/ppermute | solution.py:73
  88.1 7.5 %collective-permute-done.1.far = bf16[256,896]{1,0:T(8,128)(2,1)S(1)} collective-permute-done((bf16[256,896]{1,0:T(8,128)(2,1)S(1)}, bf16[256,896]{1,0:T(8,128)(2,1)S(1)}, u32[]{:S(2)}, u32[]{:S(2)}) %collective-permute-start.1) | collective-permute-done | bytes 458784 | tf_op jit(solution)/shard_map/ppermute | solution.py:73
  95.6 1.9 %collective-permute-start.2 = (bf16[256,896]{1,0:T(8,128)(2,1)S(1)}, bf16[256,896]{1,0:T(8,128)(2,1)}, u32[]{:S(2)}, u32[]{:S(2)}) collective-permute-start(bf16[256,896]{1,0:T(8,128)(2,1)S(1)} %collective-permute-done.1.far), channel_id=1, source_target_pairs={{0,1},{1,0},{2,3},{3,2},{4,5},{5,4},{6,7},{7,6},{8,9},{9,8},{10,11... | collective-permute-start | bytes 1376264 | tf_op jit(solution)/shard_map/ppermute | solution.py:73
  97.5 1.9 %collective-permute-done.2.diag = bf16[256,896]{1,0:T(8,128)(2,1)} collective-permute-done((bf16[256,896]{1,0:T(8,128)(2,1)S(1)}, bf16[256,896]{1,0:T(8,128)(2,1)}, u32[]{:S(2)}, u32[]{:S(2)}) %collective-permute-start.2) | collective-permute-done | bytes 458784 | tf_op jit(solution)/shard_map/ppermute | solution.py:73
  99.4 5.8 %all-to-all-done.2.whole = bf16[4,896,256]{2,1,0:T(8,128)(2,1)S(1)} async-done(((bf16[4,896,256]{2,1,0:T(8,128)(2,1)}), bf16[4,896,256]{2,1,0:T(8,128)(2,1)S(1)}, u32[]{:S(2)}, u32[]{:S(2)}) %all-to-all-start.2) | async-done | bytes 1835040 | tf_op jit(solution)/shard_map/all_to_all | solution.py:190
  105.2 1.4 %shard_map.165 = bf16[256,256]{1,0:T(8,128)(2,1)S(1)} custom-call(s32[1]{0:T(128)} %bitcast.33.turn, bf16[256,896]{1,0:T(8,128)(2,1)S(1)} %get-tuple-element.42.own, bf16[256,896]{1,0:T(8,128)(2,1)S(1)} %collective-permute-done.core, bf16[256,896]{1,0:T(8,128)(2,1)S(1)} %collective-permute-done.1.far, bf16[256,896]{1,0:T(8,128)(2,1)} %collective-permute-done.2.diag, ...), custom_call_target="tpu_custom_call" | custom-call | flops 469762048 | bytes 3670016 | tf_op jit(solution)/shard_map/pallas_call | solution.py:94
  106.7 25.8 %all_to_all.20 = bf16[32,8,256]{2,1,0:T(8,128)(2,1)S(1)} all-to-all(bf16[32,8,256]{2,1,0:T(8,128)(2,1)S(1)} %bitcast.138), channel_id=1, replica_groups=mesh['group'=4,'expert'=32,'tensor'=4] {'expert'}, dimensions={0} | all-to-all | bytes 262144 | tf_op jit(solution)/shard_map/all_to_all | solution.py:197
  132.4 0.8 fusion.7
  (47 shorter events, 1.7 us)
Async XLA Ops:
  0.6 31.5 %copy-start = (bf16[1,256,512]{2,1,0:T(8,128)(2,1)S(1)}, bf16[1,256,512]{2,1,0:T(8,128)(2,1)}, u32[]{:S(2)}) copy-start(bf16[1,256,512]{2,1,0:T(8,128)(2,1)} %param.21) | copy-start | bytes 786436
  0.6 14.6 %all-to-all-start = ((bf16[4,4,896]{2,1,0:T(4,128)(2,1)}), bf16[4,4,896]{2,1,0:T(4,128)(2,1)S(1)}, u32[]{:S(2)}, u32[]{:S(2)}) async-start(bf16[4,4,896]{2,1,0:T(4,128)(2,1)} %bitcast.149), calls=%async_computation | async-start | bytes 57344 | tf_op jit(solution)/shard_map/all_to_all | solution.py:130
  15.7 13.3 %copy-start.6 = (bf16[4,1,2048]{2,0,1:T(4,128)(2,1)S(1)}, bf16[4,1,2048]{2,0,1:T(4,128)(2,1)}, u32[]{:S(2)}) copy-start(bf16[4,1,2048]{2,0,1:T(4,128)(2,1)} %param.20) | copy-start | bytes 49156
  15.7 13.4 %copy-start.5 = (bf16[4,1,512]{2,0,1:T(4,128)(2,1)S(1)}, bf16[4,1,512]{2,0,1:T(4,128)(2,1)}, u32[]{:S(2)}) copy-start(bf16[4,1,512]{2,0,1:T(4,128)(2,1)} %param.23) | copy-start | bytes 12292
  17.0 59.8 %all-to-all-start.1 = ((bf16[32,112,128]{2,1,0:T(8,128)(2,1)}), bf16[32,112,128]{2,1,0:T(8,128)(2,1)S(1)}, u32[]{:S(2)}, u32[]{:S(2)}) async-start(bf16[32,112,128]{2,1,0:T(8,128)(2,1)} %copy.55), calls=%async_computation.1 | async-start | bytes 1835008 | tf_op jit(solution)/shard_map/all_to_all | solution.py:172
  29.0 13.7 %copy-start.4 = (s32[4,4,8]{2,1,0:T(4,128)S(1)}, s32[4,4,8]{2,1,0:T(4,128)}, u32[]{:S(2)}) copy-start(s32[4,4,8]{2,1,0:T(4,128)} %param.26) | copy-start | bytes 1540
  29.0 14.1 %copy-start.1 = (f32[32,28,256]{2,0,1:T(8,128)S(1)}, f32[32,28,256]{2,0,1:T(8,128)}, u32[]{:S(2)}) copy-start(f32[32,28,256]{2,0,1:T(8,128)} %param.17) | copy-start | bytes 2752516
  29.0 14.1 %copy-start.2 = (f32[32,28,256]{2,0,1:T(8,128)S(1)}, f32[32,28,256]{2,0,1:T(8,128)}, u32[]{:S(2)}) copy-start(f32[32,28,256]{2,0,1:T(8,128)} %param.16) | copy-start | bytes 2752516
  29.0 14.1 %copy-start.3 = (bf16[32,28,256]{2,0,1:T(8,128)(2,1)S(1)}, bf16[32,28,256]{2,0,1:T(8,128)(2,1)}, u32[]{:S(2)}) copy-start(bf16[32,28,256]{2,0,1:T(8,128)(2,1)} %param.15) | copy-start | bytes 1376260
  78.9 26.4 %all-to-all-start.2 = ((bf16[4,896,256]{2,1,0:T(8,128)(2,1)}), bf16[4,896,256]{2,1,0:T(8,128)(2,1)S(1)}, u32[]{:S(2)}, u32[]{:S(2)}) async-start(bf16[4,896,256]{2,1,0:T(8,128)(2,1)} %broadcast_in_dim.30), calls=%async_computation.2 | async-start | bytes 3670016 | tf_op jit(solution)/shard_map/all_to_all | solution.py:190
  83.3 12.2 %collective-permute-start.1 = (bf16[256,896]{1,0:T(8,128)(2,1)S(1)}, bf16[256,896]{1,0:T(8,128)(2,1)S(1)}, u32[]{:S(2)}, u32[]{:S(2)}) collective-permute-start(bf16[256,896]{1,0:T(8,128)(2,1)S(1)} %get-tuple-element.42.own), channel_id=1, source_target_pairs={{0,2},{1,3},{2,0},{3,1},{4,6},{5,7},{6,4},{7,5},{8,10},{9,11},{10,... | collective-permute-start | bytes 1376264 | tf_op jit(solution)/shard_map/ppermute | solution.py:73
  86.1 11.4 %collective-permute-start = (bf16[256,896]{1,0:T(8,128)(2,1)S(1)}, bf16[256,896]{1,0:T(8,128)(2,1)S(1)}, u32[]{:S(2)}, u32[]{:S(2)}) collective-permute-start(bf16[256,896]{1,0:T(8,128)(2,1)S(1)} %get-tuple-element.42.own), channel_id=1, source_target_pairs={{0,1},{1,0},{2,3},{3,2},{4,5},{5,4},{6,7},{7,6},{8,9},{9,8},{10,11... | collective-permute-start | bytes 1376264 | tf_op jit(solution)/shard_map/ppermute | solution.py:73
  95.6 3.8 %collective-permute-start.2 = (bf16[256,896]{1,0:T(8,128)(2,1)S(1)}, bf16[256,896]{1,0:T(8,128)(2,1)}, u32[]{:S(2)}, u32[]{:S(2)}) collective-permute-start(bf16[256,896]{1,0:T(8,128)(2,1)S(1)} %collective-permute-done.1.far), channel_id=1, source_target_pairs={{0,1},{1,0},{2,3},{3,2},{4,5},{5,4},{6,7},{7,6},{8,9},{9,8},{10,11... | collective-permute-start | bytes 1376264 | tf_op jit(solution)/shard_map/ppermute | solution.py:73

commit v12 on v10

--- a/solution.py
+++ b/solution.py
@@ -1,5 +1,6 @@
 import jax
 import jax.numpy as jnp
+import numpy as np
 from jax import lax
 from jax.experimental import pallas as pl
 from jax.experimental.pallas import tpu as pltpu
@@ -47,9 +48,9 @@
         + jnp.einsum("srhp,trp->srht", query_pos, new_rope, preferred_element_type=jnp.float32)
     ) * QK_SCALE
     valid_old = jnp.arange(slot_total, dtype=jnp.int32)[None, :] < lengths[:, None]
-    valid_new = jnp.arange(step_count)[None, :] <= jnp.arange(step_count)[:, None]
+    valid_new = np.arange(step_count)[None, :] <= np.arange(step_count)[:, None]
     old_scores = jnp.where(valid_old[None, :, None, :], old_scores, NEGATIVE)
-    new_scores = jnp.where(valid_new[:, None, None, :], new_scores, NEGATIVE)
+    new_scores = jnp.where(jnp.asarray(valid_new[:, None, None, :]), new_scores, NEGATIVE)
     peak_score = jnp.maximum(
         jnp.max(old_scores, -1, keepdims=True), jnp.max(new_scores, -1, keepdims=True)
     )

time: 134 us -> 133 us (level)
  no operation moved by 1% of the time
where the time goes in v12:
time: 133 us
  waiting for transfers between devices  47.4 us (36%)
  starting transfers between devices  32.3 us (24%)
  blocking collectives  30.9 us (23%)
  matrix products  7.29 us (5%)
  other arithmetic  5.95 us (4%)
  local copies, waits for them, and re-layouts  5.74 us (4%)
  between operations  1.64 us (1%)
  Pallas kernels  1.43 us (1%)
    all_to_all x1, waiting for transfers between devices, local(): lax.all_to_all(payload, 'expert', split_axis=0, concat_axis=0, tiled=True)  32.1 us
    all_to_all x1, blocking collectives, local(): lax.all_to_all(active, 'expert', split_axis=0, concat_axis=0, tiled=True)  25.8 us
    all_to_all x1, starting transfers between devices, local(): lax.all_to_all(payload, 'expert', split_axis=0, concat_axis=0, tiled=True)  12 us
    ppermute x3, waiting for transfers between devices, flip(): return lax.ppermute(value, axis, [(i, i ^ distance) for i in range(size)])  9.41 us
    all_to_all x1, starting transfers between devices, local(): lax.all_to_all(jnp.swapaxes(hidden_in.reshape(step_count, 4, quarter), 0,...  9.28 us
    ppermute x3, starting transfers between devices, flip(): return lax.ppermute(value, axis, [(i, i ^ distance) for i in range(size)])  6.61 us
    all_to_all x1, waiting for transfers between devices, local(): lax.all_to_all(copies, 'group', split_axis=0, concat_axis=0, tiled=True)  5.83 us
    all_gather x1, blocking collectives, local(): summary_all = lax.all_gather(summary, 'tensor', axis=1, tiled=True)  5.18 us
  transfers between devices with their start and end apart: 6, of which 4 were waited for; matrix products, arithmetic and copies ran while one was open for 11% of the time, Pallas kernels for 0%

profile of v12, /device:TPU:2, one launch (start us, length us, event | category | flops | bytes accessed | tf_op | source)
XLA Modules:
  0.0 132.7 jit_solution(4727701353213182049)
XLA Ops:
  0.6 9.3 %all-to-all-start = ((bf16[4,4,896]{2,1,0:T(4,128)(2,1)}), bf16[4,4,896]{2,1,0:T(4,128)(2,1)S(1)}, u32[]{:S(2)}, u32[]{:S(2)}) async-start(bf16[4,4,896]{2,1,0:T(4,128)(2,1)} %bitcast.148), calls=%async_computation | async-start | bytes 57344 | tf_op jit(solution)/shard_map/all_to_all | solution.py:130
  9.9 0.8 convert_reduce_fusion
  11.1 0.2 convert_element_type.86
  11.2 2.6 %fusion.16 = bf16[32,28,256]{2,0,1:T(8,128)(2,1)S(1)} fusion(bf16[32,28,256]{2,0,1:T(8,128)(2,1)} %param.15, bf16[32,28,256]{2,0,1:T(8,128)(2,1)} %param.16, f32[32,28,256]{2,0,1:T(8,128)} %param.18, f32[32,28,256]{2,0,1:T(8,128)} %param.17), kind=kLoop, calls=%fused_computation.29 | loop fusion | flops 4128768 | bytes 3211264 | tf_op jit(solution)/shard_map/convert_element_type | solution.py:33
  14.7 0.2 fusion
  15.1 1.3 copy.56
  16.4 12.0 %all-to-all-start.1 = ((bf16[32,112,128]{2,1,0:T(8,128)(2,1)}), bf16[32,112,128]{2,1,0:T(8,128)(2,1)S(1)}, u32[]{:S(2)}, u32[]{:S(2)}) async-start(bf16[32,112,128]{2,1,0:T(8,128)(2,1)} %copy.56), calls=%async_computation.1 | async-start | bytes 1835008 | tf_op jit(solution)/shard_map/all_to_all | solution.py:172
  28.6 1.2 fusion.28
  29.8 0.9 fusion.53
  30.7 0.9 fusion.37
  31.6 1.2 fusion.52
  32.8 0.2 fusion.31
  33.0 0.2 convolution_bitcast_fusion
  33.3 0.9 fusion.51
  34.2 1.6 %convert_element_type.99 = bf16[4,1,16384]{2,0,1:T(4,128)(2,1)} reshape(bf16[4,1,32,512]{3,2,0,1:T(8,128)(2,1)} %get-tuple-element.44) | data formatting | bytes 262144 | tf_op jit(solution)/shard_map/convert_element_type | solution.py:67
  36.0 5.2 %all_gather.3 = bf16[4,4,512]{2,0,1:T(4,128)(2,1)S(1)} all-gather(bf16[4,1,512]{2,0,1:T(4,128)(2,1)S(1)} %fusion.41), channel_id=1, replica_groups=mesh['group'=4,'expert'=32,'tensor'=4] {'tensor'}, dimensions={1}, use_global_device_ids=true | all-gather | bytes 20480 | tf_op jit(solution)/shard_map/all_gather | solution.py:173
  41.2 0.9 fusion.12
  42.1 0.2 select_reduce_fusion
  42.6 1.5 %fusion.25 = (f32[32,28,256]{2,0,1:T(8,128)}, f32[32,28,256]{2,0,1:T(8,128)}) fusion(bf16[32,28,256]{2,0,1:T(8,128)(2,1)S(1)} %copy-done.3, f32[32,28,256]{2,0,1:T(8,128)S(1)} %copy-done.1, f32[32,28,256]{2,0,1:T(8,128)S(1)} %copy-done.2), kind=kLoop, calls=%fused_computation.38 | loop fusion | flops 1835008 | bytes 4128768 | tf_op jit(solution)/shard_map/add | solution.py:30
  44.1 32.1 %all-to-all-done.1 = bf16[32,112,128]{2,1,0:T(8,128)(2,1)S(1)} async-done(((bf16[32,112,128]{2,1,0:T(8,128)(2,1)}), bf16[32,112,128]{2,1,0:T(8,128)(2,1)S(1)}, u32[]{:S(2)}, u32[]{:S(2)}) %all-to-all-start.1) | async-done | bytes 917536 | tf_op jit(solution)/shard_map/all_to_all | solution.py:172
  76.3 0.5 copy.58
  76.9 1.4 %broadcast_in_dim.33 = bf16[4,896,256]{2,1,0:T(8,128)(2,1)} broadcast(bf16[896,256]{1,0:T(8,128)(2,1)S(1)} %bitcast.143), dimensions={1,2} | broadcast | bytes 2293760 | tf_op jit(solution)/shard_map/broadcast_in_dim | solution.py:189
  78.3 4.5 %all-to-all-start.2 = ((bf16[4,896,256]{2,1,0:T(8,128)(2,1)}), bf16[4,896,256]{2,1,0:T(8,128)(2,1)S(1)}, u32[]{:S(2)}, u32[]{:S(2)}) async-start(bf16[4,896,256]{2,1,0:T(8,128)(2,1)} %broadcast_in_dim.33), calls=%async_computation.2 | async-start | bytes 3670016 | tf_op jit(solution)/shard_map/all_to_all | solution.py:190
  82.8 2.8 %collective-permute-start.1 = (bf16[256,896]{1,0:T(8,128)(2,1)S(1)}, bf16[256,896]{1,0:T(8,128)(2,1)S(1)}, u32[]{:S(2)}, u32[]{:S(2)}) collective-permute-start(bf16[256,896]{1,0:T(8,128)(2,1)S(1)} %get-tuple-element.40.own), channel_id=1, source_target_pairs={{0,2},{1,3},{2,0},{3,1},{4,6},{5,7},{6,4},{7,5},{8,10},{9,11},{10,... | collective-permute-start | bytes 1376264 | tf_op jit(solution)/shard_map/ppermute | solution.py:73
  85.5 1.9 %collective-permute-start = (bf16[256,896]{1,0:T(8,128)(2,1)S(1)}, bf16[256,896]{1,0:T(8,128)(2,1)S(1)}, u32[]{:S(2)}, u32[]{:S(2)}) collective-permute-start(bf16[256,896]{1,0:T(8,128)(2,1)S(1)} %get-tuple-element.40.own), channel_id=1, source_target_pairs={{0,1},{1,0},{2,3},{3,2},{4,5},{5,4},{6,7},{7,6},{8,9},{9,8},{10,11... | collective-permute-start | bytes 1376264 | tf_op jit(solution)/shard_map/ppermute | solution.py:73
  87.5 7.5 %collective-permute-done.1.far = bf16[256,896]{1,0:T(8,128)(2,1)S(1)} collective-permute-done((bf16[256,896]{1,0:T(8,128)(2,1)S(1)}, bf16[256,896]{1,0:T(8,128)(2,1)S(1)}, u32[]{:S(2)}, u32[]{:S(2)}) %collective-permute-start.1) | collective-permute-done | bytes 458784 | tf_op jit(solution)/shard_map/ppermute | solution.py:73
  95.0 1.9 %collective-permute-start.2 = (bf16[256,896]{1,0:T(8,128)(2,1)S(1)}, bf16[256,896]{1,0:T(8,128)(2,1)}, u32[]{:S(2)}, u32[]{:S(2)}) collective-permute-start(bf16[256,896]{1,0:T(8,128)(2,1)S(1)} %collective-permute-done.1.far), channel_id=1, source_target_pairs={{0,1},{1,0},{2,3},{3,2},{4,5},{5,4},{6,7},{7,6},{8,9},{9,8},{10,11... | collective-permute-start | bytes 1376264 | tf_op jit(solution)/shard_map/ppermute | solution.py:73
  96.9 1.9 %collective-permute-done.2.diag = bf16[256,896]{1,0:T(8,128)(2,1)} collective-permute-done((bf16[256,896]{1,0:T(8,128)(2,1)S(1)}, bf16[256,896]{1,0:T(8,128)(2,1)}, u32[]{:S(2)}, u32[]{:S(2)}) %collective-permute-start.2) | collective-permute-done | bytes 458784 | tf_op jit(solution)/shard_map/ppermute | solution.py:73
  98.8 5.8 %all-to-all-done.2.whole = bf16[4,896,256]{2,1,0:T(8,128)(2,1)S(1)} async-done(((bf16[4,896,256]{2,1,0:T(8,128)(2,1)}), bf16[4,896,256]{2,1,0:T(8,128)(2,1)S(1)}, u32[]{:S(2)}, u32[]{:S(2)}) %all-to-all-start.2) | async-done | bytes 1835040 | tf_op jit(solution)/shard_map/all_to_all | solution.py:190
  104.6 1.4 %shard_map.174 = bf16[256,256]{1,0:T(8,128)(2,1)S(1)} custom-call(s32[1]{0:T(128)} %bitcast.33.turn, bf16[256,896]{1,0:T(8,128)(2,1)S(1)} %get-tuple-element.40.own, bf16[256,896]{1,0:T(8,128)(2,1)S(1)} %collective-permute-done.core, bf16[256,896]{1,0:T(8,128)(2,1)S(1)} %collective-permute-done.1.far, bf16[256,896]{1,0:T(8,128)(2,1)} %collective-permute-done.2.diag, ...), custom_call_target="tpu_custom_call" | custom-call | flops 469762048 | bytes 3670016 | tf_op jit(solution)/shard_map/pallas_call | solution.py:94
  106.1 25.8 %all_to_all.20 = bf16[32,8,256]{2,1,0:T(8,128)(2,1)S(1)} all-to-all(bf16[32,8,256]{2,1,0:T(8,128)(2,1)S(1)} %bitcast.137), channel_id=1, replica_groups=mesh['group'=4,'expert'=32,'tensor'=4] {'expert'}, dimensions={0} | all-to-all | bytes 262144 | tf_op jit(solution)/shard_map/all_to_all | solution.py:197
  131.9 0.8 fusion.7
  (45 shorter events, 1.5 us)
Async XLA Ops:
  0.6 30.9 %copy-start = (bf16[1,256,512]{2,1,0:T(8,128)(2,1)S(1)}, bf16[1,256,512]{2,1,0:T(8,128)(2,1)}, u32[]{:S(2)}) copy-start(bf16[1,256,512]{2,1,0:T(8,128)(2,1)} %param.22) | copy-start | bytes 786436
  0.6 14.0 %all-to-all-start = ((bf16[4,4,896]{2,1,0:T(4,128)(2,1)}), bf16[4,4,896]{2,1,0:T(4,128)(2,1)S(1)}, u32[]{:S(2)}, u32[]{:S(2)}) async-start(bf16[4,4,896]{2,1,0:T(4,128)(2,1)} %bitcast.148), calls=%async_computation | async-start | bytes 57344 | tf_op jit(solution)/shard_map/all_to_all | solution.py:130
  15.1 13.3 %copy-start.6 = (bf16[4,1,2048]{2,0,1:T(4,128)(2,1)S(1)}, bf16[4,1,2048]{2,0,1:T(4,128)(2,1)}, u32[]{:S(2)}) copy-start(bf16[4,1,2048]{2,0,1:T(4,128)(2,1)} %param.21) | copy-start | bytes 49156
  15.1 13.4 %copy-start.5 = (bf16[4,1,512]{2,0,1:T(4,128)(2,1)S(1)}, bf16[4,1,512]{2,0,1:T(4,128)(2,1)}, u32[]{:S(2)}) copy-start(bf16[4,1,512]{2,0,1:T(4,128)(2,1)} %param.24) | copy-start | bytes 12292
  16.4 59.8 %all-to-all-start.1 = ((bf16[32,112,128]{2,1,0:T(8,128)(2,1)}), bf16[32,112,128]{2,1,0:T(8,128)(2,1)S(1)}, u32[]{:S(2)}, u32[]{:S(2)}) async-start(bf16[32,112,128]{2,1,0:T(8,128)(2,1)} %copy.56), calls=%async_computation.1 | async-start | bytes 1835008 | tf_op jit(solution)/shard_map/all_to_all | solution.py:172
  28.4 13.7 %copy-start.4 = (s32[4,4,8]{2,1,0:T(4,128)S(1)}, s32[4,4,8]{2,1,0:T(4,128)}, u32[]{:S(2)}) copy-start(s32[4,4,8]{2,1,0:T(4,128)} %param.27) | copy-start | bytes 1540
  28.4 14.1 %copy-start.1 = (f32[32,28,256]{2,0,1:T(8,128)S(1)}, f32[32,28,256]{2,0,1:T(8,128)}, u32[]{:S(2)}) copy-start(f32[32,28,256]{2,0,1:T(8,128)} %param.18) | copy-start | bytes 2752516
  28.4 14.1 %copy-start.2 = (f32[32,28,256]{2,0,1:T(8,128)S(1)}, f32[32,28,256]{2,0,1:T(8,128)}, u32[]{:S(2)}) copy-start(f32[32,28,256]{2,0,1:T(8,128)} %param.17) | copy-start | bytes 2752516
  28.4 14.1 %copy-start.3 = (bf16[32,28,256]{2,0,1:T(8,128)(2,1)S(1)}, bf16[32,28,256]{2,0,1:T(8,128)(2,1)}, u32[]{:S(2)}) copy-start(bf16[32,28,256]{2,0,1:T(8,128)(2,1)} %param.16) | copy-start | bytes 1376260
  78.3 26.4 %all-to-all-start.2 = ((bf16[4,896,256]{2,1,0:T(8,128)(2,1)}), bf16[4,896,256]{2,1,0:T(8,128)(2,1)S(1)}, u32[]{:S(2)}, u32[]{:S(2)}) async-start(bf16[4,896,256]{2,1,0:T(8,128)(2,1)} %broadcast_in_dim.33), calls=%async_computation.2 | async-start | bytes 3670016 | tf_op jit(solution)/shard_map/all_to_all | solution.py:190
  82.8 12.2 %collective-permute-start.1 = (bf16[256,896]{1,0:T(8,128)(2,1)S(1)}, bf16[256,896]{1,0:T(8,128)(2,1)S(1)}, u32[]{:S(2)}, u32[]{:S(2)}) collective-permute-start(bf16[256,896]{1,0:T(8,128)(2,1)S(1)} %get-tuple-element.40.own), channel_id=1, source_target_pairs={{0,2},{1,3},{2,0},{3,1},{4,6},{5,7},{6,4},{7,5},{8,10},{9,11},{10,... | collective-permute-start | bytes 1376264 | tf_op jit(solution)/shard_map/ppermute | solution.py:73
  85.5 11.4 %collective-permute-start = (bf16[256,896]{1,0:T(8,128)(2,1)S(1)}, bf16[256,896]{1,0:T(8,128)(2,1)S(1)}, u32[]{:S(2)}, u32[]{:S(2)}) collective-permute-start(bf16[256,896]{1,0:T(8,128)(2,1)S(1)} %get-tuple-element.40.own), channel_id=1, source_target_pairs={{0,1},{1,0},{2,3},{3,2},{4,5},{5,4},{6,7},{7,6},{8,9},{9,8},{10,11... | collective-permute-start | bytes 1376264 | tf_op jit(solution)/shard_map/ppermute | solution.py:73
  95.0 3.8 %collective-permute-start.2 = (bf16[256,896]{1,0:T(8,128)(2,1)S(1)}, bf16[256,896]{1,0:T(8,128)(2,1)}, u32[]{:S(2)}, u32[]{:S(2)}) collective-permute-start(bf16[256,896]{1,0:T(8,128)(2,1)S(1)} %collective-permute-done.1.far), channel_id=1, source_target_pairs={{0,1},{1,0},{2,3},{3,2},{4,5},{5,4},{6,7},{7,6},{8,9},{9,8},{10,11... | collective-permute-start | bytes 1376264 | tf_op jit(solution)/shard_map/ppermute | solution.py:73

commit v13 on v12

--- a/solution.py
+++ b/solution.py
@@ -66,6 +66,16 @@
     summary = summary * lax.rsqrt(jnp.mean(summary * summary, -1, keepdims=True) + 1e-05)
     attention_out = mixture.reshape(step_count, row_count, HEADS * LAT).astype(jnp.bfloat16)
     return (attention_out, summary.astype(jnp.bfloat16))
+
+
+def place_rows(expert_ids, slot_count):
+    picked = (expert_ids[..., None] == jnp.arange(EXPERTS, dtype=jnp.int32)).astype(jnp.float32)
+    per_expert = jnp.sum(picked, 2)
+    earlier = jnp.cumsum(per_expert, 1) - per_expert
+    slot_hit = (earlier[..., None] == jnp.arange(slot_count, dtype=jnp.float32)).astype(
+        jnp.float32
+    ) * per_expert[..., None]
+    return picked, slot_hit
 
 
 def flip(value, axis, distance):
@@ -137,12 +147,7 @@
     slot_count = 2
     places = step_count * slot_count
 
-    picked = (expert_ids[..., None] == jnp.arange(EXPERTS, dtype=jnp.int32)).astype(jnp.float32)
-    per_expert = jnp.sum(picked, 2)
-    earlier = jnp.cumsum(per_expert, 1) - per_expert
-    slot_hit = (earlier[..., None] == jnp.arange(slot_count, dtype=jnp.float32)).astype(
-        jnp.float32
-    ) * per_expert[..., None]
+    _, slot_hit = place_rows(expert_ids, slot_count)
     same_step = jnp.eye(step_count, dtype=jnp.float32)
     placed = jnp.transpose(slot_hit, (1, 0, 2, 3))[:, :, :, None] * same_step[:, None, :, None]
     placed = placed.reshape(4 * step_count, expert_count * places).astype(jnp.bfloat16)
@@ -159,10 +164,10 @@
     outgoing = outgoing.reshape(expert_count, places * lanes, 128)
     slabs = jnp.swapaxes(updated.reshape(expert_count, slab, 2, 128), 1, 2)
     slabs = slabs.reshape(expert_count, 2 * slab, 128)
-    later = (query_latent, query_rope, cache_rope, new_latent, new_rope, lengths)
+    later = (query_latent, query_rope, cache_rope, new_latent, new_rope, expert_ids)
     later = later + (gradients, moment_one, moment_two)
     outgoing, later = lax.optimization_barrier((outgoing, later))
-    query_latent, query_rope, cache_rope, new_latent, new_rope, lengths = later[:6]
+    query_latent, query_rope, cache_rope, new_latent, new_rope, expert_ids = later[:6]
     gradients, moment_one, moment_two = later[6:]
     payload = jnp.concatenate([slabs, outgoing], 1)
     first_new, second_new, _ = adamw(weights, gradients, moment_one, moment_two)
@@ -173,6 +178,7 @@
     summary_all = lax.all_gather(summary, "tensor", axis=1, tiled=True)
     logits = jnp.einsum("sbc,ce->sbe", summary_all, router, preferred_element_type=jnp.float32)
     gate_prob = jax.nn.sigmoid(logits)
+    picked, slot_hit = place_rows(expert_ids, slot_count)
     chosen = jnp.sum(picked * gate_prob[:, :, None, :], -1)
     route_weight = (ROUTE_SCALE * chosen / jnp.sum(chosen, -1, keepdims=True)).astype(jnp.bfloat16)
     expert_weight = jnp.sum(picked * route_weight.astype(jnp.float32)[..., None], 2)

time: 133 us -> 133 us (level)
  matrix products: 7.29 us -> 5.64 us
  transfers between devices with their start and end apart: 6 -> 6, of which waited for: 4 -> 4; matrix products, arithmetic and copies ran while one was open for 11% -> 10% of each run, Pallas kernels for 0% -> 0%
where the time goes in v13:
time: 133 us
  waiting for transfers between devices  48.1 us (36%)
  starting transfers between devices  32.3 us (24%)
  blocking collectives  31 us (23%)
  local copies, waits for them, and re-layouts  6.61 us (5%)
  other arithmetic  5.99 us (5%)
  matrix products  5.64 us (4%)
  between operations  1.66 us (1%)
  Pallas kernels  1.43 us (1%)
    all_to_all x1, waiting for transfers between devices, local(): lax.all_to_all(payload, 'expert', split_axis=0, concat_axis=0, tiled=True)  32.8 us
    all_to_all x1, blocking collectives, local(): lax.all_to_all(active, 'expert', split_axis=0, concat_axis=0, tiled=True)  25.8 us
    all_to_all x1, starting transfers between devices, local(): lax.all_to_all(payload, 'expert', split_axis=0, concat_axis=0, tiled=True)  12 us
    ppermute x3, waiting for transfers between devices, flip(): return lax.ppermute(value, axis, [(i, i ^ distance) for i in range(size)])  9.4 us
    all_to_all x1, starting transfers between devices, local(): lax.all_to_all(jnp.swapaxes(hidden_in.reshape(step_count, 4, quarter), 0,...  9.28 us
    ppermute x3, starting transfers between devices, flip(): return lax.ppermute(value, axis, [(i, i ^ distance) for i in range(size)])  6.6 us
    all_to_all x1, waiting for transfers between devices, local(): lax.all_to_all(copies, 'group', split_axis=0, concat_axis=0, tiled=True)  5.83 us
    all_gather x1, blocking collectives, local(): summary_all = lax.all_gather(summary, 'tensor', axis=1, tiled=True)  5.19 us
  transfers between devices with their start and end apart: 6, of which 4 were waited for; matrix products, arithmetic and copies ran while one was open for 10% of the time, Pallas kernels for 0%

profile of v13, /device:TPU:2, one launch (start us, length us, event | category | flops | bytes accessed | tf_op | source)
XLA Modules:
  0.0 132.6 jit_solution(613037413607130143)
XLA Ops:
  0.6 9.3 %all-to-all-start = ((bf16[4,4,896]{2,1,0:T(4,128)(2,1)}), bf16[4,4,896]{2,1,0:T(4,128)(2,1)S(1)}, u32[]{:S(2)}, u32[]{:S(2)}) async-start(bf16[4,4,896]{2,1,0:T(4,128)(2,1)} %bitcast.148), calls=%async_computation | async-start | bytes 57344 | tf_op jit(solution)/shard_map/all_to_all | solution.py:140
  9.9 0.8 convert_reduce_fusion.1
  10.8 0.1 copy.44
  11.1 0.2 convert_element_type.90
  11.2 2.6 %fusion.16 = bf16[32,28,256]{2,0,1:T(8,128)(2,1)S(1)} fusion(bf16[32,28,256]{2,0,1:T(8,128)(2,1)} %param.15, bf16[32,28,256]{2,0,1:T(8,128)(2,1)} %param.16, f32[32,28,256]{2,0,1:T(8,128)} %param.18, f32[32,28,256]{2,0,1:T(8,128)} %param.17), kind=kLoop, calls=%fused_computation.29 | loop fusion | flops 4128768 | bytes 3211264 | tf_op jit(solution)/shard_map/convert_element_type | solution.py:33
  14.7 0.2 fusion
  15.1 1.3 copy.48
  16.4 12.0 %all-to-all-start.1 = ((bf16[32,112,128]{2,1,0:T(8,128)(2,1)}), bf16[32,112,128]{2,1,0:T(8,128)(2,1)S(1)}, u32[]{:S(2)}, u32[]{:S(2)}) async-start(bf16[32,112,128]{2,1,0:T(8,128)(2,1)} %copy.48), calls=%async_computation.1 | async-start | bytes 1835008 | tf_op jit(solution)/shard_map/all_to_all | solution.py:177
  28.4 1.0 reshape.269
  29.4 1.1 fusion.28
  30.5 0.9 fusion.53
  31.6 1.2 fusion.52
  32.8 0.2 fusion.31
  33.0 0.2 convolution_bitcast_fusion
  33.3 0.9 fusion.51
  34.2 1.6 %convert_element_type.104 = bf16[4,1,16384]{2,0,1:T(4,128)(2,1)} reshape(bf16[4,1,32,512]{3,2,0,1:T(8,128)(2,1)} %get-tuple-element.45) | data formatting | bytes 262144 | tf_op jit(solution)/shard_map/convert_element_type | solution.py:67
  36.0 5.2 %all_gather.3 = bf16[4,4,512]{2,0,1:T(4,128)(2,1)S(1)} all-gather(bf16[4,1,512]{2,0,1:T(4,128)(2,1)S(1)} %fusion.41), channel_id=1, replica_groups=mesh['group'=4,'expert'=32,'tensor'=4] {'tensor'}, dimensions={1}, use_global_device_ids=true | all-gather | bytes 20480 | tf_op jit(solution)/shard_map/all_gather | solution.py:178
  41.3 0.2 select_reduce_fusion
  41.8 1.5 %fusion.25 = (f32[32,28,256]{2,0,1:T(8,128)}, f32[32,28,256]{2,0,1:T(8,128)}) fusion(bf16[32,28,256]{2,0,1:T(8,128)(2,1)S(1)} %copy-done.3, f32[32,28,256]{2,0,1:T(8,128)S(1)} %copy-done.1, f32[32,28,256]{2,0,1:T(8,128)S(1)} %copy-done.2), kind=kLoop, calls=%fused_computation.38 | loop fusion | flops 1835008 | bytes 4128768 | tf_op jit(solution)/shard_map/add | solution.py:30
  43.4 32.8 %all-to-all-done.1 = bf16[32,112,128]{2,1,0:T(8,128)(2,1)S(1)} async-done(((bf16[32,112,128]{2,1,0:T(8,128)(2,1)}), bf16[32,112,128]{2,1,0:T(8,128)(2,1)S(1)}, u32[]{:S(2)}, u32[]{:S(2)}) %all-to-all-start.1) | async-done | bytes 917536 | tf_op jit(solution)/shard_map/all_to_all | solution.py:177
  76.3 0.5 copy.50
  76.9 1.4 %broadcast_in_dim.33 = bf16[4,896,256]{2,1,0:T(8,128)(2,1)} broadcast(bf16[896,256]{1,0:T(8,128)(2,1)S(1)} %bitcast.143), dimensions={1,2} | broadcast | bytes 2293760 | tf_op jit(solution)/shard_map/broadcast_in_dim | solution.py:195
  78.3 4.5 %all-to-all-start.2 = ((bf16[4,896,256]{2,1,0:T(8,128)(2,1)}), bf16[4,896,256]{2,1,0:T(8,128)(2,1)S(1)}, u32[]{:S(2)}, u32[]{:S(2)}) async-start(bf16[4,896,256]{2,1,0:T(8,128)(2,1)} %broadcast_in_dim.33), calls=%async_computation.2 | async-start | bytes 3670016 | tf_op jit(solution)/shard_map/all_to_all | solution.py:196
  82.7 2.8 %collective-permute-start.1 = (bf16[256,896]{1,0:T(8,128)(2,1)S(1)}, bf16[256,896]{1,0:T(8,128)(2,1)S(1)}, u32[]{:S(2)}, u32[]{:S(2)}) collective-permute-start(bf16[256,896]{1,0:T(8,128)(2,1)S(1)} %get-tuple-element.41.own), channel_id=1, source_target_pairs={{0,2},{1,3},{2,0},{3,1},{4,6},{5,7},{6,4},{7,5},{8,10},{9,11},{10,... | collective-permute-start | bytes 1376264 | tf_op jit(solution)/shard_map/ppermute | solution.py:83
  85.5 1.9 %collective-permute-start = (bf16[256,896]{1,0:T(8,128)(2,1)S(1)}, bf16[256,896]{1,0:T(8,128)(2,1)S(1)}, u32[]{:S(2)}, u32[]{:S(2)}) collective-permute-start(bf16[256,896]{1,0:T(8,128)(2,1)S(1)} %get-tuple-element.41.own), channel_id=1, source_target_pairs={{0,1},{1,0},{2,3},{3,2},{4,5},{5,4},{6,7},{7,6},{8,9},{9,8},{10,11... | collective-permute-start | bytes 1376264 | tf_op jit(solution)/shard_map/ppermute | solution.py:83
  87.4 7.5 %collective-permute-done.1.far = bf16[256,896]{1,0:T(8,128)(2,1)S(1)} collective-permute-done((bf16[256,896]{1,0:T(8,128)(2,1)S(1)}, bf16[256,896]{1,0:T(8,128)(2,1)S(1)}, u32[]{:S(2)}, u32[]{:S(2)}) %collective-permute-start.1) | collective-permute-done | bytes 458784 | tf_op jit(solution)/shard_map/ppermute | solution.py:83
  94.9 1.9 %collective-permute-start.2 = (bf16[256,896]{1,0:T(8,128)(2,1)S(1)}, bf16[256,896]{1,0:T(8,128)(2,1)}, u32[]{:S(2)}, u32[]{:S(2)}) collective-permute-start(bf16[256,896]{1,0:T(8,128)(2,1)S(1)} %collective-permute-done.1.far), channel_id=1, source_target_pairs={{0,1},{1,0},{2,3},{3,2},{4,5},{5,4},{6,7},{7,6},{8,9},{9,8},{10,11... | collective-permute-start | bytes 1376264 | tf_op jit(solution)/shard_map/ppermute | solution.py:83
  96.9 1.9 %collective-permute-done.2.diag = bf16[256,896]{1,0:T(8,128)(2,1)} collective-permute-done((bf16[256,896]{1,0:T(8,128)(2,1)S(1)}, bf16[256,896]{1,0:T(8,128)(2,1)}, u32[]{:S(2)}, u32[]{:S(2)}) %collective-permute-start.2) | collective-permute-done | bytes 458784 | tf_op jit(solution)/shard_map/ppermute | solution.py:83
  98.8 5.8 %all-to-all-done.2.whole = bf16[4,896,256]{2,1,0:T(8,128)(2,1)S(1)} async-done(((bf16[4,896,256]{2,1,0:T(8,128)(2,1)}), bf16[4,896,256]{2,1,0:T(8,128)(2,1)S(1)}, u32[]{:S(2)}, u32[]{:S(2)}) %all-to-all-start.2) | async-done | bytes 1835040 | tf_op jit(solution)/shard_map/all_to_all | solution.py:196
  104.6 1.4 %shard_map.174 = bf16[256,256]{1,0:T(8,128)(2,1)S(1)} custom-call(s32[1]{0:T(128)} %bitcast.33.turn, bf16[256,896]{1,0:T(8,128)(2,1)S(1)} %get-tuple-element.41.own, bf16[256,896]{1,0:T(8,128)(2,1)S(1)} %collective-permute-done.core, bf16[256,896]{1,0:T(8,128)(2,1)S(1)} %collective-permute-done.1.far, bf16[256,896]{1,0:T(8,128)(2,1)} %collective-permute-done.2.diag, ...), custom_call_target="tpu_custom_call" | custom-call | flops 469762048 | bytes 3670016 | tf_op jit(solution)/shard_map/pallas_call | solution.py:104
  106.0 25.8 %all_to_all.20 = bf16[32,8,256]{2,1,0:T(8,128)(2,1)S(1)} all-to-all(bf16[32,8,256]{2,1,0:T(8,128)(2,1)S(1)} %bitcast.137), channel_id=1, replica_groups=mesh['group'=4,'expert'=32,'tensor'=4] {'expert'}, dimensions={0} | all-to-all | bytes 262144 | tf_op jit(solution)/shard_map/all_to_all | solution.py:203
  131.8 0.8 fusion.7
  (48 shorter events, 1.6 us)
Async XLA Ops:
  0.6 30.9 %copy-start = (bf16[1,256,512]{2,1,0:T(8,128)(2,1)S(1)}, bf16[1,256,512]{2,1,0:T(8,128)(2,1)}, u32[]{:S(2)}) copy-start(bf16[1,256,512]{2,1,0:T(8,128)(2,1)} %param.22) | copy-start | bytes 786436
  0.6 14.0 %all-to-all-start = ((bf16[4,4,896]{2,1,0:T(4,128)(2,1)}), bf16[4,4,896]{2,1,0:T(4,128)(2,1)S(1)}, u32[]{:S(2)}, u32[]{:S(2)}) async-start(bf16[4,4,896]{2,1,0:T(4,128)(2,1)} %bitcast.148), calls=%async_computation | async-start | bytes 57344 | tf_op jit(solution)/shard_map/all_to_all | solution.py:140
  15.1 14.3 %copy-start.6 = (bf16[4,1,512]{2,0,1:T(4,128)(2,1)S(1)}, bf16[4,1,512]{2,0,1:T(4,128)(2,1)}, u32[]{:S(2)}) copy-start(bf16[4,1,512]{2,0,1:T(4,128)(2,1)} %param.24) | copy-start | bytes 12292
  15.1 16.3 %copy-start.5 = (bf16[1,64,256]{2,1,0:T(8,128)(2,1)S(1)}, bf16[1,64,256]{2,1,0:T(8,128)(2,1)}, u32[]{:S(2)}) copy-start(bf16[1,64,256]{2,1,0:T(8,128)(2,1)} %param.23) | copy-start | bytes 98308
  16.4 59.8 %all-to-all-start.1 = ((bf16[32,112,128]{2,1,0:T(8,128)(2,1)}), bf16[32,112,128]{2,1,0:T(8,128)(2,1)S(1)}, u32[]{:S(2)}, u32[]{:S(2)}) async-start(bf16[32,112,128]{2,1,0:T(8,128)(2,1)} %copy.48), calls=%async_computation.1 | async-start | bytes 1835008 | tf_op jit(solution)/shard_map/all_to_all | solution.py:177
  28.4 12.9 %copy-start.4 = (s32[4,4,8]{2,1,0:T(4,128)S(1)}, s32[4,4,8]{2,1,0:T(4,128)}, u32[]{:S(2)}) copy-start(s32[4,4,8]{2,1,0:T(4,128)} %param.27) | copy-start | bytes 1540
  28.4 13.4 %copy-start.1 = (f32[32,28,256]{2,0,1:T(8,128)S(1)}, f32[32,28,256]{2,0,1:T(8,128)}, u32[]{:S(2)}) copy-start(f32[32,28,256]{2,0,1:T(8,128)} %param.18) | copy-start | bytes 2752516
  28.4 13.4 %copy-start.2 = (f32[32,28,256]{2,0,1:T(8,128)S(1)}, f32[32,28,256]{2,0,1:T(8,128)}, u32[]{:S(2)}) copy-start(f32[32,28,256]{2,0,1:T(8,128)} %param.17) | copy-start | bytes 2752516
  28.4 13.4 %copy-start.3 = (bf16[32,28,256]{2,0,1:T(8,128)(2,1)S(1)}, bf16[32,28,256]{2,0,1:T(8,128)(2,1)}, u32[]{:S(2)}) copy-start(bf16[32,28,256]{2,0,1:T(8,128)(2,1)} %param.16) | copy-start | bytes 1376260
  31.6 9.6 %copy-start.7 = (bf16[512,32]{0,1:T(8,128)(2,1)S(1)}, bf16[512,32]{0,1:T(8,128)(2,1)}, u32[]{:S(2)}) copy-start(bf16[512,32]{0,1:T(8,128)(2,1)} %param.28) | copy-start | bytes 98308
  78.3 26.3 %all-to-all-start.2 = ((bf16[4,896,256]{2,1,0:T(8,128)(2,1)}), bf16[4,896,256]{2,1,0:T(8,128)(2,1)S(1)}, u32[]{:S(2)}, u32[]{:S(2)}) async-start(bf16[4,896,256]{2,1,0:T(8,128)(2,1)} %broadcast_in_dim.33), calls=%async_computation.2 | async-start | bytes 3670016 | tf_op jit(solution)/shard_map/all_to_all | solution.py:196
  82.7 12.2 %collective-permute-start.1 = (bf16[256,896]{1,0:T(8,128)(2,1)S(1)}, bf16[256,896]{1,0:T(8,128)(2,1)S(1)}, u32[]{:S(2)}, u32[]{:S(2)}) collective-permute-start(bf16[256,896]{1,0:T(8,128)(2,1)S(1)} %get-tuple-element.41.own), channel_id=1, source_target_pairs={{0,2},{1,3},{2,0},{3,1},{4,6},{5,7},{6,4},{7,5},{8,10},{9,11},{10,... | collective-permute-start | bytes 1376264 | tf_op jit(solution)/shard_map/ppermute | solution.py:83
  85.5 11.4 %collective-permute-start = (bf16[256,896]{1,0:T(8,128)(2,1)S(1)}, bf16[256,896]{1,0:T(8,128)(2,1)S(1)}, u32[]{:S(2)}, u32[]{:S(2)}) collective-permute-start(bf16[256,896]{1,0:T(8,128)(2,1)S(1)} %get-tuple-element.41.own), channel_id=1, source_target_pairs={{0,1},{1,0},{2,3},{3,2},{4,5},{5,4},{6,7},{7,6},{8,9},{9,8},{10,11... | collective-permute-start | bytes 1376264 | tf_op jit(solution)/shard_map/ppermute | solution.py:83
  94.9 3.8 %collective-permute-start.2 = (bf16[256,896]{1,0:T(8,128)(2,1)S(1)}, bf16[256,896]{1,0:T(8,128)(2,1)}, u32[]{:S(2)}, u32[]{:S(2)}) collective-permute-start(bf16[256,896]{1,0:T(8,128)(2,1)S(1)} %collective-permute-done.1.far), channel_id=1, source_target_pairs={{0,1},{1,0},{2,3},{3,2},{4,5},{5,4},{6,7},{7,6},{8,9},{9,8},{10,11... | collective-permute-start | bytes 1376264 | tf_op jit(solution)/shard_map/ppermute | solution.py:83
